TPU v7x, 512 devices: a whole 4x4x16 slice. The times are simulated.
512 devices in a mesh: freq: 16 (over y, z_hi, core), sx: 8 (over z_lo), sy: 4 (over x).
Axes of the slice: x: 4, y: 4, z: 16 (z_hi: 2, z_lo: 8; z = z_hi * 8 + z_lo), core: 2. Of those that a mesh axis runs over, the one named last changes fastest.
Arguments:
- source: float32 [2, 32, 512, 1024], P(None, 'freq', 'sx', 'sy'), may hold values from -6 to 6
- receiver: float32 [2, 32, 512, 1024], P(None, 'freq', 'sx', 'sy'), may hold values from -6 to 6
- table_index: int32 [2, 32, 512, 1024], P(None, 'freq', 'sx', 'sy'), may hold values from 0 to 31
- coef_table: float32 [2, 32, 13], replicated, may hold values from -1.2 to 1.2
Outputs:
- source_out: float32 [2, 32, 512, 1024], P(None, 'freq', 'sx', 'sy')
- receiver_out: float32 [2, 32, 512, 1024], P(None, 'freq', 'sx', 'sy')
- image: float32 [2, 512, 1024], P(None, 'sx', 'sy')
All inputs are finite; a program needn't handle non-finite values.
Results may differ from a plain program's by a relative error of at most 0.0003.
Values sent between devices are 32-bit elements; how exact they have to be, the bound alone decides.
No kernel may reach another device: no remote copies, remote signals or barrier semaphores. Data moves between devices by JAX's collectives and lax.ppermute only.
A program may use at most 64 MiB of HBM per device.

v0:
```python
import jax
import jax.numpy as jnp
from jax import lax
from jax.sharding import PartitionSpec as P


def with_halo(block, sides, width):
    for axis, dim in sides:
        count = lax.axis_size(axis)
        forward = [(i, i + 1) for i in range(count - 1)]
        backward = [(target, source) for source, target in forward]
        low = lax.ppermute(
            lax.slice_in_dim(block, block.shape[dim] - width, None, axis=dim), axis, forward
        )
        high = lax.ppermute(lax.slice_in_dim(block, 0, width, axis=dim), axis, backward)
        block = jnp.concatenate([low, block, high], axis=dim)
    return block


def stencil(padded):
    centre = padded[..., 1:-1, 1:-1]
    edges = (
        padded[..., 2:, 1:-1]
        + padded[..., :-2, 1:-1]
        + padded[..., 1:-1, 2:]
        + padded[..., 1:-1, :-2]
    )
    corners = (
        padded[..., 2:, 2:] + padded[..., 2:, :-2] + padded[..., :-2, 2:] + padded[..., :-2, :-2]
    )
    return -0.5 * centre + 0.25 * edges + 0.125 * corners


def coef_planes(coef_table, index_now):
    entries = coef_table.shape[1]
    hits = (index_now[None] == jnp.arange(entries, dtype=jnp.int32)[:, None, None, None]).astype(
        jnp.float32
    )
    return jnp.einsum("tfxy,ctk->ckfxy", hits, coef_table, precision=lax.Precision.HIGHEST)


def combine(coef_re, coef_im, term, signs):
    real_part = coef_re * term[:, 0] - signs * coef_im * term[:, 1]
    imag_part = signs * coef_im * term[:, 0] + coef_re * term[:, 1]
    return jnp.stack([real_part, imag_part], axis=1)


def local(source, receiver, table_index, coef_table):
    waves = jnp.stack([source, receiver])
    signs = jnp.array([1.0, -1.0], jnp.float32).reshape(2, 1, 1, 1)
    count = coef_table.shape[2]
    images = []
    for depth in range(table_index.shape[0]):
        planes = coef_planes(coef_table, table_index[depth])
        start = waves

        def apply(field):
            return stencil(with_halo(field, (("sx", 3), ("sy", 4)), 1))

        current = apply(start)
        total = combine(planes[0, 0], planes[1, 0], start, signs) + combine(
            planes[0, 1], planes[1, 1], current, signs
        )

        def advance(order, carry):
            previous, present, summed = carry
            following = 2.0 * apply(present) - previous
            return (
                present,
                following,
                summed + combine(planes[0, order], planes[1, order], following, signs),
            )

        unused_a, unused_b, total = lax.fori_loop(2, count, advance, (start, current, total))
        waves = total
        local_image = jnp.sum(waves[0] * waves[1], axis=(0, 1))
        images.append(lax.psum(local_image, "freq"))
    image = jnp.stack(images)
    return (waves[0], waves[1], image)


def solution(mesh):
    placed = (
        P(None, "freq", "sx", "sy"),
        P(None, "freq", "sx", "sy"),
        P(None, "freq", "sx", "sy"),
        P(),
    )
    return jax.shard_map(
        local,
        mesh=mesh,
        in_specs=placed,
        out_specs=(P(None, "freq", "sx", "sy"), P(None, "freq", "sx", "sy"), P(None, "sx", "sy")),
        check_vma=False,
    )
```

profile of v0, /device:TPU:1, one launch (start us, length us, event | category | flops | bytes accessed | tf_op | source)
XLA Modules:
  0.0 804.3 jit_solution(8165040116585864547)
XLA Ops:
  9.4 5.0 collective-permute-start.9
  15.4 2.0 fusion.31
  17.7 2.0 fusion.28
  19.7 2.0 copy-done.1
  24.2 4.0 collective-permute-start.11
  28.3 3.7 copy.9
  33.4 209.9 %while.40 = (s32[]{:T(128)}, f32[2,2,2,64,256]{4,3,2,1,0:T(8,128)S(1)}, f32[2,2,2,64,256]{4,3,2,1,0:T(8,128)S(1)}, f32[2,2,2,64,256]{4,3,2,1,0:T(8,128)S(1)}, f3...) while((s32[]{:T(128)}, ...), condition=%wide.region_1.0_spmd.clone, body=%wide.region_0.0_spmd.clone.sunk | while | flops 3771494 | bytes 13075775 | solution.py:74
  34.7 4.2 collective-permute-start.1
  41.2 4.6 collective-permute-start.3
  52.2 5.5 collective-permute-start.1
  59.9 4.5 collective-permute-start.3
  70.8 5.7 collective-permute-start.1
  78.8 4.5 collective-permute-start.3
  89.6 5.2 collective-permute-start.1
  97.1 4.5 collective-permute-start.3
  107.9 5.5 collective-permute-start.1
  115.7 4.5 collective-permute-start.3
  126.5 5.5 collective-permute-start.1
  134.3 4.5 collective-permute-start.3
  145.1 5.7 collective-permute-start.1
  153.1 4.5 collective-permute-start.3
  164.0 5.7 collective-permute-start.1
  172.0 4.5 collective-permute-start.3
  178.8 1.8 collective-permute-done.3
  183.3 5.7 collective-permute-start.1
  191.4 4.5 collective-permute-start.3
  196.8 3.8 collective-permute-done.2
  200.6 1.8 collective-permute-done.3
  205.1 5.9 collective-permute-start.1
  213.3 4.8 collective-permute-start.3
  219.1 3.0 collective-permute-done.2
  225.8 5.3 collective-permute-start.1
  233.4 4.8 collective-permute-start.3
  244.5 5.2 collective-permute-start.13
  250.7 5.9 copy.11
  258.1 4.8 collective-permute-start.15
  263.5 4.0 collective-permute-done.14
  267.5 1.8 collective-permute-done.15
  270.6 210.0 %while.41 = (s32[]{:T(128)}, f32[2,2,2,64,256]{4,3,2,1,0:T(8,128)S(1)}, f32[2,2,2,64,256]{4,3,2,1,0:T(8,128)S(1)}, f32[2,2,2,64,256]{4,3,2,1,0:T(8,128)S(1)}, f3...) while((s32[]{:T(128)}, ...), condition=%wide.region_3.0_spmd.clone, body=%wide.region_2.0_spmd.clone.sunk | while | flops 3771494 | bytes 13075775 | solution.py:74
  271.9 5.4 collective-permute-start.5
  279.6 4.5 collective-permute-start.7
  290.5 5.5 collective-permute-start.5
  298.4 4.5 collective-permute-start.7
  309.2 5.2 collective-permute-start.5
  316.8 4.5 collective-permute-start.7
  327.6 5.2 collective-permute-start.5
  335.1 4.5 collective-permute-start.7
  346.0 5.5 collective-permute-start.5
  353.7 4.5 collective-permute-start.7
  364.6 5.6 collective-permute-start.5
  372.4 4.5 collective-permute-start.7
  383.7 5.7 collective-permute-start.5
  391.7 4.5 collective-permute-start.7
  397.2 3.6 collective-permute-done.6
  405.3 6.1 collective-permute-start.5
  413.7 4.5 collective-permute-start.7
  419.3 3.1 collective-permute-done.6
  426.1 5.6 collective-permute-start.5
  434.0 4.8 collective-permute-start.7
  445.1 5.3 collective-permute-start.5
  452.7 4.8 collective-permute-start.7
  463.9 4.9 collective-permute-start.5
  471.1 4.5 collective-permute-start.7
  482.1 313.8 %all-reduce.3.cloned.1.call-done = (f32[1,64,256]{2,1,0:T(8,128)}, f32[1,64,256]{2,1,0:T(8,128)}) async-done(((f32[1,64,256]{2,1,0:T(8,128)}, f32[1,64,256]{2,1,0:T(8,128)}), (f32[1,64,256]{2,1,0:T(8,128)}, f32[1,64,256]{2,1,0:T(8,128)})) %all-reduce.3.cloned.1.call-update) | async-done | bytes 131088 | tf_op jit(solution)/shard_map/psum | solution.py:77
  (393 shorter events, 196.5 us)
Async XLA Ops:
  7.2 788.8 %all-reduce.3.cloned.1.call-start = ((), (), s32[]{:S(2)}) async-start(), calls=%async_computation | async-start | bytes 262144 | tf_op jit(solution)/shard_map/psum | solution.py:77
  8.1 14.6 %collective-permute-start.8 = (f32[2,2,2,1,256]{4,3,2,1,0:T(1,128)S(1)}, f32[2,2,2,1,256]{4,3,2,1,0:T(1,128)S(1)}, u32[]{:S(2)}, u32[]{:S(2)}) collective-permute-start(f32[2,2,2,1,256]{4,3,2,1,0:T(1,128)S(1)} %get-tuple-element.421), channel_id=1, source_target_pairs={{4,0},{8,4},{12,8},{16,12},{20,16},{24,20},{28,24},{5,1},{9,5},{13... | collective-permute-start | bytes 24584 | tf_op jit(solution)/shard_map/ppermute | solution.py:15
  9.4 13.3 %collective-permute-start.9 = (f32[2,2,2,1,256]{4,3,2,1,0:T(1,128)S(1)}, f32[2,2,2,1,256]{4,3,2,1,0:T(1,128)S(1)}, u32[]{:S(2)}, u32[]{:S(2)}) collective-permute-start(f32[2,2,2,1,256]{4,3,2,1,0:T(1,128)S(1)} %get-tuple-element.420), channel_id=1, source_target_pairs={{0,4},{4,8},{8,12},{12,16},{16,20},{20,24},{24,28},{1,5},{5,9},{9,... | collective-permute-start | bytes 24584 | tf_op jit(solution)/shard_map/ppermute | solution.py:12
  22.9 9.1 %collective-permute-start.10 = (f32[2,2,2,66,1]{4,3,2,1,0:T(8,128)S(1)}, f32[2,2,2,66,1]{4,3,2,1,0:T(8,128)S(1)}, u32[]{:S(2)}, u32[]{:S(2)}) collective-permute-start(f32[2,2,2,66,1]{4,3,2,1,0:T(8,128)S(1)} %get-tuple-element.410), channel_id=1, source_target_pairs={{1,0},{2,1},{3,2},{5,4},{6,5},{7,6},{9,8},{10,9},{11,10},{13,12},{... | collective-permute-start | bytes 6344 | tf_op jit(solution)/shard_map/ppermute | solution.py:15
  24.2 7.8 collective-permute-start.11
  39.9 8.1 %collective-permute-start.2 = (f32[2,2,2,66,1]{4,3,2,1,0:T(8,128)S(1)}, f32[2,2,2,66,1]{4,3,2,1,0:T(8,128)S(1)}, u32[]{:S(2)}, u32[]{:S(2)}) collective-permute-start(f32[2,2,2,66,1]{4,3,2,1,0:T(8,128)S(1)} %get-tuple-element.515), channel_id=1, source_target_pairs={{1,0},{2,1},{3,2},{5,4},{6,5},{7,6},{9,8},{10,9},{11,10},{13,12},{... | collective-permute-start | bytes 6344 | tf_op jit(solution)/shard_map/while/body/eval_jaxpr/ppermute | solution.py:15
  41.2 8.3 %collective-permute-start.3 = (f32[2,2,2,66,1]{4,3,2,1,0:T(8,128)S(1)}, f32[2,2,2,66,1]{4,3,2,1,0:T(8,128)S(1)}, u32[]{:S(2)}, u32[]{:S(2)}) collective-permute-start(f32[2,2,2,66,1]{4,3,2,1,0:T(8,128)S(1)} %get-tuple-element.516), channel_id=1, source_target_pairs={{0,1},{1,2},{2,3},{4,5},{5,6},{6,7},{8,9},{9,10},{10,11},{12,13},{... | collective-permute-start | bytes 6344 | tf_op jit(solution)/shard_map/while/body/eval_jaxpr/ppermute | solution.py:12
  58.6 7.9 collective-permute-start.2
  59.9 8.1 %collective-permute-start.3 = (f32[2,2,2,66,1]{4,3,2,1,0:T(8,128)S(1)}, f32[2,2,2,66,1]{4,3,2,1,0:T(8,128)S(1)}, u32[]{:S(2)}, u32[]{:S(2)}) collective-permute-start(f32[2,2,2,66,1]{4,3,2,1,0:T(8,128)S(1)} %get-tuple-element.516), channel_id=1, source_target_pairs={{0,1},{1,2},{2,3},{4,5},{5,6},{6,7},{8,9},{9,10},{10,11},{12,13},{... | collective-permute-start | bytes 6344 | tf_op jit(solution)/shard_map/while/body/eval_jaxpr/ppermute | solution.py:12
  69.5 7.0 collective-permute-start
  77.5 7.9 collective-permute-start.2
  78.8 8.1 %collective-permute-start.3 = (f32[2,2,2,66,1]{4,3,2,1,0:T(8,128)S(1)}, f32[2,2,2,66,1]{4,3,2,1,0:T(8,128)S(1)}, u32[]{:S(2)}, u32[]{:S(2)}) collective-permute-start(f32[2,2,2,66,1]{4,3,2,1,0:T(8,128)S(1)} %get-tuple-element.516), channel_id=1, source_target_pairs={{0,1},{1,2},{2,3},{4,5},{5,6},{6,7},{8,9},{9,10},{10,11},{12,13},{... | collective-permute-start | bytes 6344 | tf_op jit(solution)/shard_map/while/body/eval_jaxpr/ppermute | solution.py:12
  95.8 7.9 collective-permute-start.2
  97.1 8.1 %collective-permute-start.3 = (f32[2,2,2,66,1]{4,3,2,1,0:T(8,128)S(1)}, f32[2,2,2,66,1]{4,3,2,1,0:T(8,128)S(1)}, u32[]{:S(2)}, u32[]{:S(2)}) collective-permute-start(f32[2,2,2,66,1]{4,3,2,1,0:T(8,128)S(1)} %get-tuple-element.516), channel_id=1, source_target_pairs={{0,1},{1,2},{2,3},{4,5},{5,6},{6,7},{8,9},{9,10},{10,11},{12,13},{... | collective-permute-start | bytes 6344 | tf_op jit(solution)/shard_map/while/body/eval_jaxpr/ppermute | solution.py:12
  114.4 7.9 collective-permute-start.2
  115.7 8.1 %collective-permute-start.3 = (f32[2,2,2,66,1]{4,3,2,1,0:T(8,128)S(1)}, f32[2,2,2,66,1]{4,3,2,1,0:T(8,128)S(1)}, u32[]{:S(2)}, u32[]{:S(2)}) collective-permute-start(f32[2,2,2,66,1]{4,3,2,1,0:T(8,128)S(1)} %get-tuple-element.516), channel_id=1, source_target_pairs={{0,1},{1,2},{2,3},{4,5},{5,6},{6,7},{8,9},{9,10},{10,11},{12,13},{... | collective-permute-start | bytes 6344 | tf_op jit(solution)/shard_map/while/body/eval_jaxpr/ppermute | solution.py:12
  133.0 8.0 collective-permute-start.2
  134.3 8.1 %collective-permute-start.3 = (f32[2,2,2,66,1]{4,3,2,1,0:T(8,128)S(1)}, f32[2,2,2,66,1]{4,3,2,1,0:T(8,128)S(1)}, u32[]{:S(2)}, u32[]{:S(2)}) collective-permute-start(f32[2,2,2,66,1]{4,3,2,1,0:T(8,128)S(1)} %get-tuple-element.516), channel_id=1, source_target_pairs={{0,1},{1,2},{2,3},{4,5},{5,6},{6,7},{8,9},{9,10},{10,11},{12,13},{... | collective-permute-start | bytes 6344 | tf_op jit(solution)/shard_map/while/body/eval_jaxpr/ppermute | solution.py:12
  143.8 7.0 collective-permute-start
  151.9 7.9 collective-permute-start.2
  153.1 8.1 %collective-permute-start.3 = (f32[2,2,2,66,1]{4,3,2,1,0:T(8,128)S(1)}, f32[2,2,2,66,1]{4,3,2,1,0:T(8,128)S(1)}, u32[]{:S(2)}, u32[]{:S(2)}) collective-permute-start(f32[2,2,2,66,1]{4,3,2,1,0:T(8,128)S(1)} %get-tuple-element.516), channel_id=1, source_target_pairs={{0,1},{1,2},{2,3},{4,5},{5,6},{6,7},{8,9},{9,10},{10,11},{12,13},{... | collective-permute-start | bytes 6344 | tf_op jit(solution)/shard_map/while/body/eval_jaxpr/ppermute | solution.py:12
  162.7 7.1 collective-permute-start
  170.7 8.1 %collective-permute-start.2 = (f32[2,2,2,66,1]{4,3,2,1,0:T(8,128)S(1)}, f32[2,2,2,66,1]{4,3,2,1,0:T(8,128)S(1)}, u32[]{:S(2)}, u32[]{:S(2)}) collective-permute-start(f32[2,2,2,66,1]{4,3,2,1,0:T(8,128)S(1)} %get-tuple-element.515), channel_id=1, source_target_pairs={{1,0},{2,1},{3,2},{5,4},{6,5},{7,6},{9,8},{10,9},{11,10},{13,12},{... | collective-permute-start | bytes 6344 | tf_op jit(solution)/shard_map/while/body/eval_jaxpr/ppermute | solution.py:15
  172.0 8.5 %collective-permute-start.3 = (f32[2,2,2,66,1]{4,3,2,1,0:T(8,128)S(1)}, f32[2,2,2,66,1]{4,3,2,1,0:T(8,128)S(1)}, u32[]{:S(2)}, u32[]{:S(2)}) collective-permute-start(f32[2,2,2,66,1]{4,3,2,1,0:T(8,128)S(1)} %get-tuple-element.516), channel_id=1, source_target_pairs={{0,1},{1,2},{2,3},{4,5},{5,6},{6,7},{8,9},{9,10},{10,11},{12,13},{... | collective-permute-start | bytes 6344 | tf_op jit(solution)/shard_map/while/body/eval_jaxpr/ppermute | solution.py:12
  182.0 7.1 collective-permute-start
  190.1 10.6 %collective-permute-start.2 = (f32[2,2,2,66,1]{4,3,2,1,0:T(8,128)S(1)}, f32[2,2,2,66,1]{4,3,2,1,0:T(8,128)S(1)}, u32[]{:S(2)}, u32[]{:S(2)}) collective-permute-start(f32[2,2,2,66,1]{4,3,2,1,0:T(8,128)S(1)} %get-tuple-element.515), channel_id=1, source_target_pairs={{1,0},{2,1},{3,2},{5,4},{6,5},{7,6},{9,8},{10,9},{11,10},{13,12},{... | collective-permute-start | bytes 6344 | tf_op jit(solution)/shard_map/while/body/eval_jaxpr/ppermute | solution.py:15
  191.4 11.0 %collective-permute-start.3 = (f32[2,2,2,66,1]{4,3,2,1,0:T(8,128)S(1)}, f32[2,2,2,66,1]{4,3,2,1,0:T(8,128)S(1)}, u32[]{:S(2)}, u32[]{:S(2)}) collective-permute-start(f32[2,2,2,66,1]{4,3,2,1,0:T(8,128)S(1)} %get-tuple-element.516), channel_id=1, source_target_pairs={{0,1},{1,2},{2,3},{4,5},{5,6},{6,7},{8,9},{9,10},{10,11},{12,13},{... | collective-permute-start | bytes 6344 | tf_op jit(solution)/shard_map/while/body/eval_jaxpr/ppermute | solution.py:12
  203.8 7.2 collective-permute-start
  212.0 10.1 %collective-permute-start.2 = (f32[2,2,2,66,1]{4,3,2,1,0:T(8,128)S(1)}, f32[2,2,2,66,1]{4,3,2,1,0:T(8,128)S(1)}, u32[]{:S(2)}, u32[]{:S(2)}) collective-permute-start(f32[2,2,2,66,1]{4,3,2,1,0:T(8,128)S(1)} %get-tuple-element.515), channel_id=1, source_target_pairs={{1,0},{2,1},{3,2},{5,4},{6,5},{7,6},{9,8},{10,9},{11,10},{13,12},{... | collective-permute-start | bytes 6344 | tf_op jit(solution)/shard_map/while/body/eval_jaxpr/ppermute | solution.py:15
  213.3 9.7 %collective-permute-start.3 = (f32[2,2,2,66,1]{4,3,2,1,0:T(8,128)S(1)}, f32[2,2,2,66,1]{4,3,2,1,0:T(8,128)S(1)}, u32[]{:S(2)}, u32[]{:S(2)}) collective-permute-start(f32[2,2,2,66,1]{4,3,2,1,0:T(8,128)S(1)} %get-tuple-element.516), channel_id=1, source_target_pairs={{0,1},{1,2},{2,3},{4,5},{5,6},{6,7},{8,9},{9,10},{10,11},{12,13},{... | collective-permute-start | bytes 6344 | tf_op jit(solution)/shard_map/while/body/eval_jaxpr/ppermute | solution.py:12
  232.1 8.2 %collective-permute-start.2 = (f32[2,2,2,66,1]{4,3,2,1,0:T(8,128)S(1)}, f32[2,2,2,66,1]{4,3,2,1,0:T(8,128)S(1)}, u32[]{:S(2)}, u32[]{:S(2)}) collective-permute-start(f32[2,2,2,66,1]{4,3,2,1,0:T(8,128)S(1)} %get-tuple-element.515), channel_id=1, source_target_pairs={{1,0},{2,1},{3,2},{5,4},{6,5},{7,6},{9,8},{10,9},{11,10},{13,12},{... | collective-permute-start | bytes 6344 | tf_op jit(solution)/shard_map/while/body/eval_jaxpr/ppermute | solution.py:15
  233.4 8.4 %collective-permute-start.3 = (f32[2,2,2,66,1]{4,3,2,1,0:T(8,128)S(1)}, f32[2,2,2,66,1]{4,3,2,1,0:T(8,128)S(1)}, u32[]{:S(2)}, u32[]{:S(2)}) collective-permute-start(f32[2,2,2,66,1]{4,3,2,1,0:T(8,128)S(1)} %get-tuple-element.516), channel_id=1, source_target_pairs={{0,1},{1,2},{2,3},{4,5},{5,6},{6,7},{8,9},{9,10},{10,11},{12,13},{... | collective-permute-start | bytes 6344 | tf_op jit(solution)/shard_map/while/body/eval_jaxpr/ppermute | solution.py:12
  243.2 13.3 %collective-permute-start.12 = (f32[2,2,2,1,256]{4,3,2,1,0:T(1,128)S(1)}, f32[2,2,2,1,256]{4,3,2,1,0:T(1,128)S(1)}, u32[]{:S(2)}, u32[]{:S(2)}) collective-permute-start(f32[2,2,2,1,256]{4,3,2,1,0:T(1,128)S(1)} %get-tuple-element.417), channel_id=1, source_target_pairs={{4,0},{8,4},{12,8},{16,12},{20,16},{24,20},{28,24},{5,1},{9,5},{13... | collective-permute-start | bytes 24584 | tf_op jit(solution)/shard_map/ppermute | solution.py:15
  244.5 12.0 %collective-permute-start.13 = (f32[2,2,2,1,256]{4,3,2,1,0:T(1,128)S(1)}, f32[2,2,2,1,256]{4,3,2,1,0:T(1,128)S(1)}, u32[]{:S(2)}, u32[]{:S(2)}) collective-permute-start(f32[2,2,2,1,256]{4,3,2,1,0:T(1,128)S(1)} %get-tuple-element.416), channel_id=1, source_target_pairs={{0,4},{4,8},{8,12},{12,16},{16,20},{20,24},{24,28},{1,5},{5,9},{9,... | collective-permute-start | bytes 24584 | tf_op jit(solution)/shard_map/ppermute | solution.py:12
  256.8 10.7 %collective-permute-start.14 = (f32[2,2,2,66,1]{4,3,2,1,0:T(8,128)S(1)}, f32[2,2,2,66,1]{4,3,2,1,0:T(8,128)S(1)}, u32[]{:S(2)}, u32[]{:S(2)}) collective-permute-start(f32[2,2,2,66,1]{4,3,2,1,0:T(8,128)S(1)} %get-tuple-element.408), channel_id=1, source_target_pairs={{1,0},{2,1},{3,2},{5,4},{6,5},{7,6},{9,8},{10,9},{11,10},{13,12},{... | collective-permute-start | bytes 6344 | tf_op jit(solution)/shard_map/ppermute | solution.py:15
  258.1 11.2 %collective-permute-start.15 = (f32[2,2,2,66,1]{4,3,2,1,0:T(8,128)S(1)}, f32[2,2,2,66,1]{4,3,2,1,0:T(8,128)S(1)}, u32[]{:S(2)}, u32[]{:S(2)}) collective-permute-start(f32[2,2,2,66,1]{4,3,2,1,0:T(8,128)S(1)} %get-tuple-element.409), channel_id=1, source_target_pairs={{0,1},{1,2},{2,3},{4,5},{5,6},{6,7},{8,9},{9,10},{10,11},{12,13},{... | collective-permute-start | bytes 6344 | tf_op jit(solution)/shard_map/ppermute | solution.py:12
  278.3 8.0 collective-permute-start.6
  279.6 8.2 %collective-permute-start.7 = (f32[2,2,2,66,1]{4,3,2,1,0:T(8,128)S(1)}, f32[2,2,2,66,1]{4,3,2,1,0:T(8,128)S(1)}, u32[]{:S(2)}, u32[]{:S(2)}) collective-permute-start(f32[2,2,2,66,1]{4,3,2,1,0:T(8,128)S(1)} %get-tuple-element.531), channel_id=1, source_target_pairs={{0,1},{1,2},{2,3},{4,5},{5,6},{6,7},{8,9},{9,10},{10,11},{12,13},{... | collective-permute-start | bytes 6344 | tf_op jit(solution)/shard_map/while/body/eval_jaxpr/ppermute | solution.py:12
  289.2 6.9 collective-permute-start.4
  297.1 7.9 collective-permute-start.6
  298.4 8.1 %collective-permute-start.7 = (f32[2,2,2,66,1]{4,3,2,1,0:T(8,128)S(1)}, f32[2,2,2,66,1]{4,3,2,1,0:T(8,128)S(1)}, u32[]{:S(2)}, u32[]{:S(2)}) collective-permute-start(f32[2,2,2,66,1]{4,3,2,1,0:T(8,128)S(1)} %get-tuple-element.531), channel_id=1, source_target_pairs={{0,1},{1,2},{2,3},{4,5},{5,6},{6,7},{8,9},{9,10},{10,11},{12,13},{... | collective-permute-start | bytes 6344 | tf_op jit(solution)/shard_map/while/body/eval_jaxpr/ppermute | solution.py:12
  315.5 7.9 collective-permute-start.6
  316.8 8.1 %collective-permute-start.7 = (f32[2,2,2,66,1]{4,3,2,1,0:T(8,128)S(1)}, f32[2,2,2,66,1]{4,3,2,1,0:T(8,128)S(1)}, u32[]{:S(2)}, u32[]{:S(2)}) collective-permute-start(f32[2,2,2,66,1]{4,3,2,1,0:T(8,128)S(1)} %get-tuple-element.531), channel_id=1, source_target_pairs={{0,1},{1,2},{2,3},{4,5},{5,6},{6,7},{8,9},{9,10},{10,11},{12,13},{... | collective-permute-start | bytes 6344 | tf_op jit(solution)/shard_map/while/body/eval_jaxpr/ppermute | solution.py:12
  333.8 7.9 collective-permute-start.6
  335.1 8.1 %collective-permute-start.7 = (f32[2,2,2,66,1]{4,3,2,1,0:T(8,128)S(1)}, f32[2,2,2,66,1]{4,3,2,1,0:T(8,128)S(1)}, u32[]{:S(2)}, u32[]{:S(2)}) collective-permute-start(f32[2,2,2,66,1]{4,3,2,1,0:T(8,128)S(1)} %get-tuple-element.531), channel_id=1, source_target_pairs={{0,1},{1,2},{2,3},{4,5},{5,6},{6,7},{8,9},{9,10},{10,11},{12,13},{... | collective-permute-start | bytes 6344 | tf_op jit(solution)/shard_map/while/body/eval_jaxpr/ppermute | solution.py:12
  352.4 7.9 collective-permute-start.6
  353.7 8.1 %collective-permute-start.7 = (f32[2,2,2,66,1]{4,3,2,1,0:T(8,128)S(1)}, f32[2,2,2,66,1]{4,3,2,1,0:T(8,128)S(1)}, u32[]{:S(2)}, u32[]{:S(2)}) collective-permute-start(f32[2,2,2,66,1]{4,3,2,1,0:T(8,128)S(1)} %get-tuple-element.531), channel_id=1, source_target_pairs={{0,1},{1,2},{2,3},{4,5},{5,6},{6,7},{8,9},{9,10},{10,11},{12,13},{... | collective-permute-start | bytes 6344 | tf_op jit(solution)/shard_map/while/body/eval_jaxpr/ppermute | solution.py:12
  363.3 6.9 collective-permute-start.4
  371.1 8.0 collective-permute-start.6
  372.4 8.5 %collective-permute-start.7 = (f32[2,2,2,66,1]{4,3,2,1,0:T(8,128)S(1)}, f32[2,2,2,66,1]{4,3,2,1,0:T(8,128)S(1)}, u32[]{:S(2)}, u32[]{:S(2)}) collective-permute-start(f32[2,2,2,66,1]{4,3,2,1,0:T(8,128)S(1)} %get-tuple-element.531), channel_id=1, source_target_pairs={{0,1},{1,2},{2,3},{4,5},{5,6},{6,7},{8,9},{9,10},{10,11},{12,13},{... | collective-permute-start | bytes 6344 | tf_op jit(solution)/shard_map/while/body/eval_jaxpr/ppermute | solution.py:12
  382.4 7.1 collective-permute-start.4
  390.4 10.4 %collective-permute-start.6 = (f32[2,2,2,66,1]{4,3,2,1,0:T(8,128)S(1)}, f32[2,2,2,66,1]{4,3,2,1,0:T(8,128)S(1)}, u32[]{:S(2)}, u32[]{:S(2)}) collective-permute-start(f32[2,2,2,66,1]{4,3,2,1,0:T(8,128)S(1)} %get-tuple-element.530), channel_id=1, source_target_pairs={{1,0},{2,1},{3,2},{5,4},{6,5},{7,6},{9,8},{10,9},{11,10},{13,12},{... | collective-permute-start | bytes 6344 | tf_op jit(solution)/shard_map/while/body/eval_jaxpr/ppermute | solution.py:15
  391.7 10.8 %collective-permute-start.7 = (f32[2,2,2,66,1]{4,3,2,1,0:T(8,128)S(1)}, f32[2,2,2,66,1]{4,3,2,1,0:T(8,128)S(1)}, u32[]{:S(2)}, u32[]{:S(2)}) collective-permute-start(f32[2,2,2,66,1]{4,3,2,1,0:T(8,128)S(1)} %get-tuple-element.531), channel_id=1, source_target_pairs={{0,1},{1,2},{2,3},{4,5},{5,6},{6,7},{8,9},{9,10},{10,11},{12,13},{... | collective-permute-start | bytes 6344 | tf_op jit(solution)/shard_map/while/body/eval_jaxpr/ppermute | solution.py:12
  404.0 7.4 collective-permute-start.4
  405.3 6.9 collective-permute-start.5
  412.4 10.0 %collective-permute-start.6 = (f32[2,2,2,66,1]{4,3,2,1,0:T(8,128)S(1)}, f32[2,2,2,66,1]{4,3,2,1,0:T(8,128)S(1)}, u32[]{:S(2)}, u32[]{:S(2)}) collective-permute-start(f32[2,2,2,66,1]{4,3,2,1,0:T(8,128)S(1)} %get-tuple-element.530), channel_id=1, source_target_pairs={{1,0},{2,1},{3,2},{5,4},{6,5},{7,6},{9,8},{10,9},{11,10},{13,12},{... | collective-permute-start | bytes 6344 | tf_op jit(solution)/shard_map/while/body/eval_jaxpr/ppermute | solution.py:15
  413.7 9.6 %collective-permute-start.7 = (f32[2,2,2,66,1]{4,3,2,1,0:T(8,128)S(1)}, f32[2,2,2,66,1]{4,3,2,1,0:T(8,128)S(1)}, u32[]{:S(2)}, u32[]{:S(2)}) collective-permute-start(f32[2,2,2,66,1]{4,3,2,1,0:T(8,128)S(1)} %get-tuple-element.531), channel_id=1, source_target_pairs={{0,1},{1,2},{2,3},{4,5},{5,6},{6,7},{8,9},{9,10},{10,11},{12,13},{... | collective-permute-start | bytes 6344 | tf_op jit(solution)/shard_map/while/body/eval_jaxpr/ppermute | solution.py:12
  424.8 6.9 collective-permute-start.4
  432.7 8.2 %collective-permute-start.6 = (f32[2,2,2,66,1]{4,3,2,1,0:T(8,128)S(1)}, f32[2,2,2,66,1]{4,3,2,1,0:T(8,128)S(1)}, u32[]{:S(2)}, u32[]{:S(2)}) collective-permute-start(f32[2,2,2,66,1]{4,3,2,1,0:T(8,128)S(1)} %get-tuple-element.530), channel_id=1, source_target_pairs={{1,0},{2,1},{3,2},{5,4},{6,5},{7,6},{9,8},{10,9},{11,10},{13,12},{... | collective-permute-start | bytes 6344 | tf_op jit(solution)/shard_map/while/body/eval_jaxpr/ppermute | solution.py:15
  434.0 8.4 %collective-permute-start.7 = (f32[2,2,2,66,1]{4,3,2,1,0:T(8,128)S(1)}, f32[2,2,2,66,1]{4,3,2,1,0:T(8,128)S(1)}, u32[]{:S(2)}, u32[]{:S(2)}) collective-permute-start(f32[2,2,2,66,1]{4,3,2,1,0:T(8,128)S(1)} %get-tuple-element.531), channel_id=1, source_target_pairs={{0,1},{1,2},{2,3},{4,5},{5,6},{6,7},{8,9},{9,10},{10,11},{12,13},{... | collective-permute-start | bytes 6344 | tf_op jit(solution)/shard_map/while/body/eval_jaxpr/ppermute | solution.py:12
  451.4 8.2 %collective-permute-start.6 = (f32[2,2,2,66,1]{4,3,2,1,0:T(8,128)S(1)}, f32[2,2,2,66,1]{4,3,2,1,0:T(8,128)S(1)}, u32[]{:S(2)}, u32[]{:S(2)}) collective-permute-start(f32[2,2,2,66,1]{4,3,2,1,0:T(8,128)S(1)} %get-tuple-element.530), channel_id=1, source_target_pairs={{1,0},{2,1},{3,2},{5,4},{6,5},{7,6},{9,8},{10,9},{11,10},{13,12},{... | collective-permute-start | bytes 6344 | tf_op jit(solution)/shard_map/while/body/eval_jaxpr/ppermute | solution.py:15
  452.7 8.4 %collective-permute-start.7 = (f32[2,2,2,66,1]{4,3,2,1,0:T(8,128)S(1)}, f32[2,2,2,66,1]{4,3,2,1,0:T(8,128)S(1)}, u32[]{:S(2)}, u32[]{:S(2)}) collective-permute-start(f32[2,2,2,66,1]{4,3,2,1,0:T(8,128)S(1)} %get-tuple-element.531), channel_id=1, source_target_pairs={{0,1},{1,2},{2,3},{4,5},{5,6},{6,7},{8,9},{9,10},{10,11},{12,13},{... | collective-permute-start | bytes 6344 | tf_op jit(solution)/shard_map/while/body/eval_jaxpr/ppermute | solution.py:12
  469.8 7.9 collective-permute-start.6
  471.1 8.1 %collective-permute-start.7 = (f32[2,2,2,66,1]{4,3,2,1,0:T(8,128)S(1)}, f32[2,2,2,66,1]{4,3,2,1,0:T(8,128)S(1)}, u32[]{:S(2)}, u32[]{:S(2)}) collective-permute-start(f32[2,2,2,66,1]{4,3,2,1,0:T(8,128)S(1)} %get-tuple-element.531), channel_id=1, source_target_pairs={{0,1},{1,2},{2,3},{4,5},{5,6},{6,7},{8,9},{9,10},{10,11},{12,13},{... | collective-permute-start | bytes 6344 | tf_op jit(solution)/shard_map/while/body/eval_jaxpr/ppermute | solution.py:12
  (39 other events, 231.6 us)
Sparse Core Ops, SparseCore 0:
  482.2 313.6 all-reduce.2
where the time goes:
time: 808 us; the launch traced here: 804 us
  waiting for transfers between devices  403 us (50%)
  starting transfers between devices  301 us (37%)
  local copies, waits for them, and re-layouts  42.1 us (5%)
  other arithmetic  37.2 us (5%)
  between operations  14.3 us (2%)
    psum x1, waiting for transfers between devices, local(): images.append(lax.psum(local_image, 'freq'))  314 us
    ppermute x48, starting transfers between devices, with_halo(): lax.ppermute(lax.slice_in_dim(block, block.shape[dim] - width, None, axis...  239 us
    ppermute x48, starting transfers between devices, with_halo(): lax.ppermute(lax.slice_in_dim(block, 0, width, axis=dim), axis, backward)  62 us
    ppermute x48, waiting for transfers between devices, with_halo(): lax.ppermute(lax.slice_in_dim(block, block.shape[dim] - width, None, axis...  50.8 us
    ppermute x48, waiting for transfers between devices, with_halo(): lax.ppermute(lax.slice_in_dim(block, 0, width, axis=dim), axis, backward)  38.8 us
    mul x22, local copies, waits for them, and re-layouts, combine(): real_part = coef_re * term[:, 0] - signs * coef_im * term[:, 1]  21.8 us
  transfers between devices with their start and end apart: 97, of which 69 were waited for; matrix products, arithmetic and copies ran while one was open for 5% of the time, Pallas kernels for 0%

commit v1 on v0

v1 whole, which is shorter than its diff:
```python
import jax
import jax.numpy as jnp
from jax import lax
from jax.experimental import pallas as pl
from jax.experimental.pallas import tpu as pltpu
from jax.sharding import PartitionSpec as P

ROWS, COLS = 64, 256
HALO = 24
SIDE = 32
STEPS = 5
FIRST = ROWS + 2 * HALO
SECOND = ROWS + HALO
INDEX_HALO = 16
SEND = 4 * STEPS * HALO + STEPS * INDEX_HALO
WIDE = STEPS * 128
VMEM = 48 * 1024 * 1024


def spread_matrix():
    k = lax.broadcasted_iota(jnp.int32, (WIDE, WIDE), 0)
    n = lax.broadcasted_iota(jnp.int32, (WIDE, WIDE), 1)
    step, lane = n // 128, n % 128
    wave, column = lane // 64, (lane % 64) * STEPS + step
    own = k < 2 * COLS
    edge = k - 2 * COLS
    from_wave = jnp.where(own, k // COLS, (edge // SIDE) % 2)
    from_column = jnp.where(own, SIDE + k % COLS, jnp.where(edge < 2 * SIDE, 0, SIDE + COLS) + edge % SIDE)
    return ((wave == from_wave) & (column == from_column)).astype(jnp.bfloat16)


def dot(left, right, contract):
    return lax.dot_general(left, right, (contract, ((), ())), preferred_element_type=jnp.float32)


def exact_dot(left, right, contract):
    high = left.astype(jnp.bfloat16)
    rest = left - high.astype(jnp.float32)
    middle = rest.astype(jnp.bfloat16)
    low = (rest - middle.astype(jnp.float32)).astype(jnp.bfloat16)
    return dot(high, right, contract) + dot(middle, right, contract) + dot(low, right, contract)


def edges_kernel(source, receiver, index, left, right):
    lane = lax.broadcasted_iota(jnp.int32, (ROWS, 128), 1)

    def join(parts, start):
        total = jnp.zeros((ROWS, 128), jnp.float32)
        for place, part in enumerate(parts):
            shift = (place * SIDE - start) % 128
            moved = part if shift == 0 else pltpu.roll(part, shift, 1)
            total = jnp.where((lane >= place * SIDE) & (lane < (place + 1) * SIDE), moved, total)
        return total

    for out, tile, start in ((left, 0, 0), (right, 1, 128 - SIDE)):
        cut = slice(tile * 128, (tile + 1) * 128)
        for place, waves in enumerate((source, receiver)):
            out[place] = join([waves[part, wave, :, cut] for part in range(2) for wave in range(2)], start)
        out[2] = join([index[wave, :, cut].astype(jnp.float32) for wave in range(2)], start)


def spread_kernel(source, receiver, index0, index1, low, high, spread, fields, indices0, indices1, top, bottom, joined, joined_index):
    lane = lax.broadcasted_iota(jnp.int32, (ROWS, 128), 1)

    def halos(place, part):
        from_low, from_high = low[place], high[place]
        if part == 0:
            return jnp.where(lane < 64, from_low, pltpu.roll(from_high, 64, 1))
        return jnp.where(lane < 64, pltpu.roll(from_low, 64, 1), from_high)

    for plane in range(4):
        waves, part = (source, receiver)[plane // 2], plane % 2
        rows = slice(plane * ROWS, (plane + 1) * ROWS)
        for wave in range(2):
            joined[rows, wave * COLS : (wave + 1) * COLS] = waves[part, wave]
        joined[rows, 2 * COLS :] = halos(plane // 2, part)
    for depth, index in enumerate((index0, index1)):
        rows = slice(depth * ROWS, (depth + 1) * ROWS)
        for wave in range(2):
            joined_index[rows, wave * COLS : (wave + 1) * COLS] = index[wave].astype(jnp.float32)
        joined_index[rows, 2 * COLS :] = halos(2, 0) if depth == 0 else jnp.zeros((ROWS, 128), jnp.float32)

    matrix = spread[...]
    for plane in range(4):
        values = exact_dot(joined[plane * ROWS : (plane + 1) * ROWS, :], matrix, ((1,), (0,)))
        for step in range(STEPS):
            piece = values[:, step * 128 : (step + 1) * 128]
            fields[plane, step] = piece
            at = (plane * STEPS + step) * HALO
            top[at : at + HALO, :] = piece[:HALO]
            bottom[at : at + HALO, :] = piece[ROWS - HALO :]
    values = dot(joined_index[...].astype(jnp.bfloat16), matrix, ((1,), (0,)))
    for step in range(STEPS):
        piece = values[:ROWS, step * 128 : (step + 1) * 128]
        indices0[step] = piece
        at = 4 * STEPS * HALO + step * INDEX_HALO
        top[at : at + INDEX_HALO, :] = piece[:INDEX_HALO]
        bottom[at : at + INDEX_HALO, :] = piece[ROWS - INDEX_HALO :]
        indices1[step] = values[ROWS:, step * 128 : (step + 1) * 128]


def march_kernel(
    flags, fields, indices0, indices1, above, below, table, spread, source_out, receiver_out, image,
    terms, masks, places, picture, result,
):
    orders = terms.shape[0]
    for plane in range(4):
        for step in range(STEPS):
            at = (plane * STEPS + step) * HALO
            terms[0, plane, step, :HALO, :] = above[at : at + HALO, :]
            terms[0, plane, step, HALO : HALO + ROWS, :] = fields[plane, step]
            terms[0, plane, step, HALO + ROWS :, :] = below[at : at + HALO, :]
    for step in range(STEPS):
        at = 4 * STEPS * HALO + step * INDEX_HALO
        places[0, step, HALO - INDEX_HALO : HALO, :] = above[at : at + INDEX_HALO, :].astype(jnp.int32)
        places[0, step, HALO : HALO + ROWS, :] = indices0[step].astype(jnp.int32)
        places[0, step, HALO + ROWS : HALO + ROWS + INDEX_HALO, :] = below[at : at + INDEX_HALO, :].astype(jnp.int32)
        places[1, step] = jnp.zeros((FIRST, 128), jnp.int32)
        places[1, step, HALO : HALO + ROWS, :] = indices1[step].astype(jnp.int32)

    lane = lax.broadcasted_iota(jnp.int32, (FIRST, 128), 1)
    row = lax.broadcasted_iota(jnp.int32, (FIRST, 128), 0)
    inside_row = jnp.where(row < HALO, flags[0], jnp.where(row >= HALO + ROWS, flags[1], 1.0))
    for step in range(STEPS):
        column = (lane % 64) * STEPS + step
        inside_column = jnp.where(column < SIDE, flags[2], jnp.where(column >= SIDE + COLS, flags[3], 1.0))
        masks[step] = 0.25 * inside_row * inside_column

    def depth_step(depth, base, count):
        def rows(r):
            return pl.ds(base + r, 8, stride=count)

        def advance(plane, now, first):
            def load(r):
                return [terms[now, plane, step, rows(r), :] for step in range(STEPS)]

            start = load(0)
            last = load(count - 1)
            wrapped = [pltpu.roll(v, 7, 0) for v in start]
            pair = [pltpu.roll(a + b, 1, 0) for a, b in zip(last, wrapped)]
            value = start
            for r in range(count):
                after = load(r + 1) if r + 1 < count else wrapped
                new_pair = [a + b for a, b in zip(value, after)]
                column = [a + b for a, b in zip(pair, new_pair)]
                right = [column[s] + column[s + 1] for s in range(STEPS - 1)]
                right.append(column[STEPS - 1] + pltpu.roll(column[0], 127, 1))
                both = [pltpu.roll(right[STEPS - 1], 1, 1) + right[0]]
                both += [right[s - 1] + right[s] for s in range(1, STEPS)]
                for step in range(STEPS):
                    moved = masks[step, rows(r), :] * both[step]
                    if first:
                        new = 0.5 * moved - value[step]
                    else:
                        new = (moved - (value[step] + value[step])) - terms[now - 1, plane, step, rows(r), :]
                    terms[now + 1, plane, step, rows(r), :] = new
                pair, value = new_pair, after

        def first_order(plane, carry):
            advance(plane, 0, True)
            return carry

        lax.fori_loop(0, 4, first_order, 0)

        def other_orders(count_down, carry):
            advance(lax.rem(count_down, 4), 1 + lax.div(count_down, 4), False)
            return carry

        lax.fori_loop(0, 4 * (orders - 2), other_orders, 0)

        def combine(r, carry):
            out_rows = pl.ds(HALO // 2 + r, 8, stride=SECOND // 8)
            for step in range(STEPS):
                place = places[depth, step, out_rows, :]
                total = [None] * 4
                for order in range(orders):
                    re = jnp.take_along_axis(jnp.broadcast_to(table[order, :][None], (8, 128)), place, axis=1)
                    im = jnp.take_along_axis(jnp.broadcast_to(table[orders + order, :][None], (8, 128)), place, axis=1)
                    for waves, sign in ((0, 1), (2, -1)):
                        real = terms[order, waves, step, out_rows, :]
                        imag = terms[order, waves + 1, step, out_rows, :]
                        if sign > 0:
                            new = (re * real - im * imag, re * imag + im * real)
                        else:
                            new = (re * real + im * imag, re * imag - im * real)
                        for part in range(2):
                            old = total[waves + part]
                            total[waves + part] = new[part] if old is None else old + new[part]
                for plane in range(4):
                    terms[0, plane, step, out_rows, :] = total[plane]
                picture[depth, step, out_rows, :] = total[0] * total[2] + total[1] * total[3]
            return carry

        lax.fori_loop(0, SECOND // 8, combine, 0)

    depth_step(0, 0, FIRST // 8)
    depth_step(1, HALO // 2, SECOND // 8)

    own = slice(HALO, HALO + ROWS)
    matrix = spread[: 2 * COLS, :]
    for plane in range(6):
        for step in range(STEPS):
            piece = terms[0, plane, step, own, :] if plane < 4 else picture[plane - 4, step, own, :]
            result[plane * ROWS : (plane + 1) * ROWS, step * 128 : (step + 1) * 128] = piece
    for plane in range(6):
        values = exact_dot(result[plane * ROWS : (plane + 1) * ROWS, :], matrix, ((1,), (1,)))
        if plane < 4:
            out = (source_out, receiver_out)[plane // 2]
            for wave in range(2):
                out[plane % 2, wave] = values[:, wave * COLS : (wave + 1) * COLS]
        else:
            total = values[:, :COLS] + values[:, COLS:]
            for part in range(8):
                image[part, plane - 4] = total[part * 8 : (part + 1) * 8]


def full(count):
    return [pl.BlockSpec(memory_space=pltpu.VMEM)] * count


def shape(*dims, dtype=jnp.float32):
    return jax.ShapeDtypeStruct(dims, dtype)


def params():
    return pltpu.CompilerParams(vmem_limit_bytes=VMEM)


def shift(block, axis, forward):
    count = lax.axis_size(axis)
    pairs = [(i, i + 1) for i in range(count - 1)]
    return lax.ppermute(block, axis, pairs if forward else [(b, a) for a, b in pairs])


def extrapolate(source, receiver, table_index, coef_table):
    orders = coef_table.shape[2]
    spread = spread_matrix()
    left, right = pl.pallas_call(
        edges_kernel,
        out_shape=(shape(3, ROWS, 128), shape(3, ROWS, 128)),
        in_specs=full(3),
        out_specs=tuple(full(2)),
        compiler_params=params(),
        name="edges",
    )(source, receiver, table_index[0])
    low = shift(right, "sy", True)
    high = shift(left, "sy", False)
    fields, indices0, indices1, top, bottom = pl.pallas_call(
        spread_kernel,
        out_shape=(
            shape(4, STEPS, ROWS, 128),
            shape(STEPS, ROWS, 128),
            shape(STEPS, ROWS, 128),
            shape(SEND, 128),
            shape(SEND, 128),
        ),
        in_specs=full(7),
        out_specs=tuple(full(5)),
        scratch_shapes=[pltpu.VMEM((4 * ROWS, WIDE), jnp.float32), pltpu.VMEM((2 * ROWS, WIDE), jnp.float32)],
        compiler_params=params(),
        name="spread",
    )(source, receiver, table_index[0], table_index[1], low, high, spread)
    above = shift(bottom, "sx", True)
    below = shift(top, "sx", False)
    at_x, at_y = lax.axis_index("sx"), lax.axis_index("sy")
    flags = jnp.stack(
        [at_x > 0, at_x < lax.axis_size("sx") - 1, at_y > 0, at_y < lax.axis_size("sy") - 1]
    ).astype(jnp.float32)
    table = jnp.pad(jnp.swapaxes(coef_table, 1, 2).reshape(2 * orders, -1), ((0, 0), (0, 128 - coef_table.shape[1])))
    return pl.pallas_call(
        march_kernel,
        out_shape=(shape(2, 2, ROWS, COLS), shape(2, 2, ROWS, COLS), shape(8, 2, 8, COLS)),
        in_specs=[pl.BlockSpec(memory_space=pltpu.SMEM)] + full(7),
        out_specs=tuple(full(3)),
        scratch_shapes=[
            pltpu.VMEM((orders, 4, STEPS, FIRST, 128), jnp.float32),
            pltpu.VMEM((STEPS, FIRST, 128), jnp.float32),
            pltpu.VMEM((2, STEPS, FIRST, 128), jnp.int32),
            pltpu.VMEM((2, STEPS, FIRST, 128), jnp.float32),
            pltpu.VMEM((6 * ROWS, WIDE), jnp.float32),
        ],
        compiler_params=params(),
        name="march",
    )(flags, fields, indices0, indices1, above, below, table, spread)


def add_over_freq(pieces):
    groups = [[y * 4 + z * 2 + core for y in range(4) for core in range(2)] for z in range(2)]
    mine = jnp.sum(lax.all_to_all(pieces, "freq", 0, 0, axis_index_groups=groups), axis=0)
    mine = mine + lax.ppermute(mine, "freq", [(i, i ^ 2) for i in range(16)])
    blocks = lax.all_to_all(jnp.broadcast_to(mine[None], pieces.shape), "freq", 0, 0, axis_index_groups=groups)
    return jnp.swapaxes(blocks, 0, 1).reshape(2, ROWS, COLS)


def local(source, receiver, table_index, coef_table):
    source_out, receiver_out, pieces = extrapolate(source, receiver, table_index, coef_table)
    return source_out, receiver_out, add_over_freq(pieces)


def solution(mesh):
    placed = P(None, "freq", "sx", "sy")
    return jax.shard_map(
        local,
        mesh=mesh,
        in_specs=(placed, placed, placed, P()),
        out_specs=(placed, placed, P(None, "sx", "sy")),
        check_vma=False,
    )
```

time: 808 us -> 90.4 us (0.11)
  waiting for transfers between devices: 403 us -> 9.5 us
  starting transfers between devices: 301 us -> 24.5 us
  local copies, waits for them, and re-layouts: 42.1 us -> 3.58 us
  other arithmetic: 37.2 us -> 1.8 us
  Pallas kernels: 0 us -> 27.2 us
  blocking collectives: 0 us -> 22.7 us
  between operations: 14.3 us -> 0.83 us
    psum x1 -> x0, waiting for transfers between devices: 314 us -> none  [local(): images.append(lax.psum(local_image, 'freq'))]
    ppermute x96 -> x5, starting transfers between devices: 300 us -> 24.5 us  [the longest x1 14.4 us: add_over_freq(): mine = mine + lax.ppermute(mine, 'freq', [(i, i ^ 2) for i in range(16)])]
    ppermute x96 -> x5, waiting for transfers between devices: 89.6 us -> 9.5 us  [the longest x4 8.38 us: shift(): lax.ppermute(block, axis, pairs if forward else [(b, a) for a, b in pairs])]
    pallas_call x0 -> x3, Pallas kernels: none -> 27.2 us  [the longest x1 25.1 us: extrapolate(): pl.pallas_call(march_kernel, out_shape=(shape(2, 2, ROWS, COLS), shape(2,...]
    all_to_all x0 -> x2, blocking collectives: none -> 22.7 us  [the longest x1 13.3 us: add_over_freq(): lax.all_to_all(pieces, 'freq', 0, 0, axis_index_groups=groups)]
    mul x22 -> x0, local copies, waits for them, and re-layouts: 21.8 us -> none  [combine(): real_part = coef_re * term[:, 0] - signs * coef_im * term[:, 1]]
    sub x46 -> x2, other arithmetic: 17.9 us -> 0.01 us  [the longest x1 0.01 us: spread_matrix(): step, lane = (n // 128, n % 128)]
    unnamed x18 -> x6, local copies, waits for them, and re-layouts: 12.6 us -> 1.9 us
  transfers between devices with their start and end apart: 97 -> 5, of which waited for: 69 -> 4; matrix products, arithmetic and copies ran while one was open for 5% -> 2% of each run, Pallas kernels for 0% -> 0%
where the time goes in v1:
time: 90.4 us; the launch traced here: 90 us
  Pallas kernels  27.2 us (30%)
  starting transfers between devices  24.5 us (27%)
  blocking collectives  22.7 us (25%)
  waiting for transfers between devices  9.5 us (11%)
  local copies, waits for them, and re-layouts  3.58 us (4%)
  other arithmetic  1.8 us (2%)
    pallas_call x1, Pallas kernels, extrapolate(): pl.pallas_call(march_kernel, out_shape=(shape(2, 2, ROWS, COLS), shape(2,...  25.1 us
    ppermute x1, starting transfers between devices, add_over_freq(): mine = mine + lax.ppermute(mine, 'freq', [(i, i ^ 2) for i in range(16)])  14.4 us
    all_to_all x1, blocking collectives, add_over_freq(): lax.all_to_all(pieces, 'freq', 0, 0, axis_index_groups=groups)  13.3 us
    ppermute x4, starting transfers between devices, shift(): lax.ppermute(block, axis, pairs if forward else [(b, a) for a, b in pairs])  10.1 us
    all_to_all x1, blocking collectives, add_over_freq(): lax.all_to_all(jnp.broadcast_to(mine[None], pieces.shape), 'freq', 0, 0,...  9.39 us
    ppermute x4, waiting for transfers between devices, shift(): lax.ppermute(block, axis, pairs if forward else [(b, a) for a, b in pairs])  8.38 us
    unnamed x6, local copies, waits for them, and re-layouts  1.9 us
    pallas_call x1, Pallas kernels, extrapolate(): pl.pallas_call(spread_kernel, out_shape=(shape(4, STEPS, ROWS, 128), shap...  1.84 us
  transfers between devices with their start and end apart: 5, of which 4 were waited for; matrix products, arithmetic and copies ran while one was open for 2% of the time, Pallas kernels for 0%

profile of v1, /device:TPU:1, one launch (start us, length us, event | category | flops | bytes accessed | tf_op | source)
XLA Modules:
  0.0 90.0 jit_solution(5235849807309513866)
XLA Ops:
  0.6 1.0 %slice_bitcast_fusion = (s32[2,64,256]{2,1,0:T(8,128)S(1)}, s32[2,64,256]{2,1,0:T(8,128)S(1)}) fusion(s32[2,2,64,256]{3,2,1,0:T(8,128)} %param.6), kind=kLoop, calls=%fused_computation.25 | loop fusion | bytes 524288 | tf_op jit(solution)/shard_map/squeeze | solution.py:262
  1.6 0.0 copy-start
  1.6 0.9 %copy-done = f32[2,2,64,256]{3,2,1,0:T(8,128)S(1)} copy-done((f32[2,2,64,256]{3,2,1,0:T(8,128)S(1)}, f32[2,2,64,256]{3,2,1,0:T(8,128)}, u32[]{:S(2)}) %copy-start) | copy-done | bytes 262168
  2.6 0.0 copy-start.1
  2.6 0.9 %copy-done.1 = f32[2,2,64,256]{3,2,1,0:T(8,128)S(1)} copy-done((f32[2,2,64,256]{3,2,1,0:T(8,128)S(1)}, f32[2,2,64,256]{3,2,1,0:T(8,128)}, u32[]{:S(2)}) %copy-start.1) | copy-done | bytes 262168
  3.5 0.2 edges.1
  3.7 4.0 %collective-permute-start = (f32[3,64,128]{2,1,0:T(8,128)S(1)}, f32[3,64,128]{2,1,0:T(8,128)S(1)}, u32[]{:S(2)}, u32[]{:S(2)}) collective-permute-start(f32[3,64,128]{2,1,0:T(8,128)S(1)} %get-tuple-element.13), channel_id=1, source_target_pairs={{0,1},{1,2},{2,3},{4,5},{5,6},{6,7},{8,9},{9,10},{10,11},{12,13},{... | collective-permute-start | bytes 294920 | tf_op jit(solution)/shard_map/ppermute | solution.py:232
  7.7 1.3 %collective-permute-start.1 = (f32[3,64,128]{2,1,0:T(8,128)S(1)}, f32[3,64,128]{2,1,0:T(8,128)S(1)}, u32[]{:S(2)}, u32[]{:S(2)}) collective-permute-start(f32[3,64,128]{2,1,0:T(8,128)S(1)} %get-tuple-element.14), channel_id=1, source_target_pairs={{1,0},{2,1},{3,2},{5,4},{6,5},{7,6},{9,8},{10,9},{11,10},{13,12},{... | collective-permute-start | bytes 294920 | tf_op jit(solution)/shard_map/ppermute | solution.py:232
  9.1 1.6 %and_convert_fusion.spread = bf16[640,640]{1,0:T(8,128)(2,1)S(1)} fusion(s32[640]{0:T(1024)S(1)} %get-tuple-element.30, s32[640]{0:T(1024)S(1)} %get-tuple-element.40, s32[640]{0:T(1024)S(1)} %get-tuple-element.39, s32[640]{0:T(1024)S(1)} %get-tuple-element.26, s32[640]{0:T(1024)S(1)} %get-tuple-element.34, s32[640]{0:T(1024)S(1)} %get-tuple-element.31, ...), kind=kLoop, calls=%fused_computation.23 | loop fusion | flops 18841600 | bytes 856960 | tf_op jit(solution)/shard_map/convert_element_type | solution.py:29
  10.8 0.0 collective-permute-done.low
  10.8 2.3 %collective-permute-done.1.high = f32[3,64,128]{2,1,0:T(8,128)S(1)} collective-permute-done((f32[3,64,128]{2,1,0:T(8,128)S(1)}, f32[3,64,128]{2,1,0:T(8,128)S(1)}, u32[]{:S(2)}, u32[]{:S(2)}) %collective-permute-start.1) | collective-permute-done | bytes 98336 | tf_op jit(solution)/shard_map/ppermute | solution.py:232
  13.0 0.0 copy-start.2
  13.0 1.8 %spread.1 = (f32[4,5,64,128]{3,2,1,0:T(8,128)S(1)}, f32[5,64,128]{2,1,0:T(8,128)S(1)}, f32[5,64,128]{2,1,0:T(8,128)S(1)}, f32[560,128]{1,0:T(8,128)S(1)}, f32[560,128]{1,0:T(8,128)S(1)}) custom-call(f32[2,2,64,256]{3,2,1,0:T(8,128)S(1)} %copy-done, f32[2,2,64,256]{3,2,1,0:T(8,128)S(1)} %copy-done.1, s32[2,64,256]{2,1,0:T(8,128)S(1)} %get-tuple-element.24.index.index0, ...), custom_call_target="tpu_custom_call" | custom-call | tf_op jit(solution)/shard_map/spread/pallas_call | solution.py:248
  14.9 3.6 %collective-permute-start.2 = (f32[560,128]{1,0:T(8,128)S(1)}, f32[560,128]{1,0:T(8,128)S(1)}, u32[]{:S(2)}, u32[]{:S(2)}) collective-permute-start(f32[560,128]{1,0:T(8,128)S(1)} %get-tuple-element.18), channel_id=1, source_target_pairs={{0,4},{4,8},{8,12},{12,16},{16,20},{20,24},{24,28},{1,5},{5,9},{9,... | collective-permute-start | bytes 860168 | tf_op jit(solution)/shard_map/ppermute | solution.py:232
  18.5 1.3 %collective-permute-start.3 = (f32[560,128]{1,0:T(8,128)S(1)}, f32[560,128]{1,0:T(8,128)S(1)}, u32[]{:S(2)}, u32[]{:S(2)}) collective-permute-start(f32[560,128]{1,0:T(8,128)S(1)} %get-tuple-element.19), channel_id=1, source_target_pairs={{4,0},{8,4},{12,8},{16,12},{20,16},{24,20},{28,24},{5,1},{9,5},{13... | collective-permute-start | bytes 860168 | tf_op jit(solution)/shard_map/ppermute | solution.py:232
  19.8 0.0 copy-done.2
  19.8 0.1 add_convert_fusion.flags
  19.9 2.1 %collective-permute-done.2.above = f32[560,128]{1,0:T(8,128)S(1)} collective-permute-done((f32[560,128]{1,0:T(8,128)S(1)}, f32[560,128]{1,0:T(8,128)S(1)}, u32[]{:S(2)}, u32[]{:S(2)}) %collective-permute-start.2) | collective-permute-done | bytes 286752 | tf_op jit(solution)/shard_map/ppermute | solution.py:232
  22.0 4.0 %collective-permute-done.3.below = f32[560,128]{1,0:T(8,128)S(1)} collective-permute-done((f32[560,128]{1,0:T(8,128)S(1)}, f32[560,128]{1,0:T(8,128)S(1)}, u32[]{:S(2)}, u32[]{:S(2)}) %collective-permute-start.3) | collective-permute-done | bytes 286752 | tf_op jit(solution)/shard_map/ppermute | solution.py:232
  26.0 25.1 %march.1 = (f32[2,2,64,256]{3,2,1,0:T(8,128)}, f32[2,2,64,256]{3,2,1,0:T(8,128)}, f32[8,2,8,256]{3,2,1,0:T(8,128)S(1)}) custom-call(f32[4]{0:T(128)S(1)} %add_convert_fusion.flags, f32[4,5,64,128]{3,2,1,0:T(8,128)S(1)} %get-tuple-element.15.fields, f32[5,64,128]{2,1,0:T(8,128)S(1)} %get-tuple-element.16.indices0, ...), custom_call_target="tpu_custom_call" | custom-call | tf_op jit(solution)/shard_map/march/pallas_call | solution.py:270
  51.1 13.3 %all_to_all.10 = f32[8,2,8,256]{3,2,1,0:T(8,128)S(1)} all-to-all(f32[8,2,8,256]{3,2,1,0:T(8,128)S(1)} %get-tuple-element.22), channel_id=1, replica_groups={{0,32,128,160,256,288,384,416},{64,96,192,224,320,352,448,480},{1,33,12..., dimensions={0} | all-to-all | bytes 262144 | tf_op jit(solution)/shard_map/all_to_all | solution.py:289
  64.4 14.4 %collective-permute-start.4 = (f32[2,8,256]{2,1,0:T(8,128)S(1)}, f32[2,8,256]{2,1,0:T(8,128)S(1)}, u32[]{:S(2)}, u32[]{:S(2)}) collective-permute-start(f32[2,8,256]{2,1,0:T(8,128)S(1)} %reduce_sum.9), channel_id=1, source_target_pairs={{0,64},{32,96},{64,0},{96,32},{128,192},{160,224},{192,128},{224,1... | collective-permute-start | bytes 49160 | tf_op jit(solution)/shard_map/ppermute | solution.py:290
  78.8 1.1 %collective-permute-done.4 = f32[2,8,256]{2,1,0:T(8,128)S(1)} collective-permute-done((f32[2,8,256]{2,1,0:T(8,128)S(1)}, f32[2,8,256]{2,1,0:T(8,128)S(1)}, u32[]{:S(2)}, u32[]{:S(2)}) %collective-permute-start.4) | collective-permute-done | bytes 16416 | tf_op jit(solution)/shard_map/ppermute | solution.py:290
  80.0 9.4 %all_to_all.11 = f32[8,2,8,256]{3,2,1,0:T(8,128)S(1)} all-to-all(f32[8,2,8,256]{3,2,1,0:T(8,128)S(1)} %broadcast_in_dim.13), channel_id=1, replica_groups={{0,32,128,160,256,288,384,416},{64,96,192,224,320,352,448,480},{1,33,12..., dimensions={0} | all-to-all | bytes 262144 | tf_op jit(solution)/shard_map/all_to_all | solution.py:291
  89.4 0.7 copy.13
  (17 shorter events, 0.1 us)
Async XLA Ops:
  1.6 1.0 %copy-start = (f32[2,2,64,256]{3,2,1,0:T(8,128)S(1)}, f32[2,2,64,256]{3,2,1,0:T(8,128)}, u32[]{:S(2)}) copy-start(f32[2,2,64,256]{3,2,1,0:T(8,128)} %source.3) | copy-start | bytes 786436
  2.6 0.9 %copy-start.1 = (f32[2,2,64,256]{3,2,1,0:T(8,128)S(1)}, f32[2,2,64,256]{3,2,1,0:T(8,128)}, u32[]{:S(2)}) copy-start(f32[2,2,64,256]{3,2,1,0:T(8,128)} %receiver.3) | copy-start | bytes 786436
  3.7 7.0 %collective-permute-start = (f32[3,64,128]{2,1,0:T(8,128)S(1)}, f32[3,64,128]{2,1,0:T(8,128)S(1)}, u32[]{:S(2)}, u32[]{:S(2)}) collective-permute-start(f32[3,64,128]{2,1,0:T(8,128)S(1)} %get-tuple-element.13), channel_id=1, source_target_pairs={{0,1},{1,2},{2,3},{4,5},{5,6},{6,7},{8,9},{9,10},{10,11},{12,13},{... | collective-permute-start | bytes 294920 | tf_op jit(solution)/shard_map/ppermute | solution.py:232
  7.7 5.4 %collective-permute-start.1 = (f32[3,64,128]{2,1,0:T(8,128)S(1)}, f32[3,64,128]{2,1,0:T(8,128)S(1)}, u32[]{:S(2)}, u32[]{:S(2)}) collective-permute-start(f32[3,64,128]{2,1,0:T(8,128)S(1)} %get-tuple-element.14), channel_id=1, source_target_pairs={{1,0},{2,1},{3,2},{5,4},{6,5},{7,6},{9,8},{10,9},{11,10},{13,12},{... | collective-permute-start | bytes 294920 | tf_op jit(solution)/shard_map/ppermute | solution.py:232
  13.0 6.7 %copy-start.2 = (f32[2,32,13]{1,0,2:T(2,128)S(1)}, f32[2,32,13]{1,0,2:T(2,128)}, u32[]{:S(2)}) copy-start(f32[2,32,13]{1,0,2:T(2,128)} %param.7) | copy-start | bytes 9988
  14.9 7.1 %collective-permute-start.2 = (f32[560,128]{1,0:T(8,128)S(1)}, f32[560,128]{1,0:T(8,128)S(1)}, u32[]{:S(2)}, u32[]{:S(2)}) collective-permute-start(f32[560,128]{1,0:T(8,128)S(1)} %get-tuple-element.18), channel_id=1, source_target_pairs={{0,4},{4,8},{8,12},{12,16},{16,20},{20,24},{24,28},{1,5},{5,9},{9,... | collective-permute-start | bytes 860168 | tf_op jit(solution)/shard_map/ppermute | solution.py:232
  18.5 7.5 %collective-permute-start.3 = (f32[560,128]{1,0:T(8,128)S(1)}, f32[560,128]{1,0:T(8,128)S(1)}, u32[]{:S(2)}, u32[]{:S(2)}) collective-permute-start(f32[560,128]{1,0:T(8,128)S(1)} %get-tuple-element.19), channel_id=1, source_target_pairs={{4,0},{8,4},{12,8},{16,12},{20,16},{24,20},{28,24},{5,1},{9,5},{13... | collective-permute-start | bytes 860168 | tf_op jit(solution)/shard_map/ppermute | solution.py:232
  64.4 15.5 %collective-permute-start.4 = (f32[2,8,256]{2,1,0:T(8,128)S(1)}, f32[2,8,256]{2,1,0:T(8,128)S(1)}, u32[]{:S(2)}, u32[]{:S(2)}) collective-permute-start(f32[2,8,256]{2,1,0:T(8,128)S(1)} %reduce_sum.9), channel_id=1, source_target_pairs={{0,64},{32,96},{64,0},{96,32},{128,192},{160,224},{192,128},{224,1... | collective-permute-start | bytes 49160 | tf_op jit(solution)/shard_map/ppermute | solution.py:290

commit v2 on v0

v2 whole, which is shorter than its diff:
```python
import jax
import jax.numpy as jnp
from jax import lax
from jax.experimental import pallas as pl
from jax.experimental.pallas import tpu as pltpu
from jax.sharding import PartitionSpec as P

ROWS, COLS = 64, 256
HALO = 24
HALF = HALO // 2
SIDE = 32
STEPS = 5
INDEX_HALO = 16
FIELD_ROWS = 4 * STEPS * HALO
SEND = FIELD_ROWS + STEPS * INDEX_HALO
WIDE = STEPS * 128
STRIP = 16
OFFSET = 32
TALL = 128
INNER = slice(HALO, ROWS - HALO)


def spread_matrix():
    k = lax.broadcasted_iota(jnp.int32, (WIDE, WIDE), 0)
    n = lax.broadcasted_iota(jnp.int32, (WIDE, WIDE), 1)
    step, lane = n // 128, n % 128
    wave, column = lane // 64, (lane % 64) * STEPS + step
    own = k < 2 * COLS
    edge = k - 2 * COLS
    from_wave = jnp.where(own, k // COLS, (edge // SIDE) % 2)
    from_column = jnp.where(own, SIDE + k % COLS, jnp.where(edge < 2 * SIDE, 0, SIDE + COLS) + edge % SIDE)
    return ((wave == from_wave) & (column == from_column)).astype(jnp.bfloat16)


def dot(left, right, contract):
    return lax.dot_general(left, right, (contract, ((), ())), preferred_element_type=jnp.float32)


def exact_dot(left, right, contract):
    high = left.astype(jnp.bfloat16)
    rest = left - high.astype(jnp.float32)
    middle = rest.astype(jnp.bfloat16)
    low = (rest - middle.astype(jnp.float32)).astype(jnp.bfloat16)
    return dot(high, right, contract) + dot(middle, right, contract) + dot(low, right, contract)


def edges_kernel(source, receiver, index, left, right, waves, places, sems):
    copies = [
        pltpu.make_async_copy(source, waves.at[0], sems.at[0]),
        pltpu.make_async_copy(receiver, waves.at[1], sems.at[1]),
        pltpu.make_async_copy(index.at[0], places, sems.at[2]),
    ]
    for copy in copies:
        copy.start()
    lane = lax.broadcasted_iota(jnp.int32, (ROWS, 128), 1)

    def join(parts, start):
        total = jnp.zeros((ROWS, 128), jnp.float32)
        for place, part in enumerate(parts):
            shift = (place * SIDE - start) % 128
            moved = part if shift == 0 else pltpu.roll(part, shift, 1)
            total = jnp.where((lane >= place * SIDE) & (lane < (place + 1) * SIDE), moved, total)
        return total

    ends = ((right, 1, 128 - SIDE), (left, 0, 0))
    for kind in range(3):
        copies[kind].wait()
        for out, tile, start in ends:
            cut = slice(tile * 128, (tile + 1) * 128)
            if kind < 2:
                out[kind] = join([waves[kind, part, wave, :, cut] for part in range(2) for wave in range(2)], start)
            else:
                out[2] = join([places[wave, :, cut].astype(jnp.float32) for wave in range(2)], start)


def own_kernel(source, receiver, index, spread, fields, indices, joined):
    matrix = spread[: 2 * COLS, :]
    for plane in range(6):
        for wave in range(2):
            cut = slice(wave * COLS, (wave + 1) * COLS)
            if plane < 4:
                joined[:, cut] = (source, receiver)[plane // 2][plane % 2, wave]
            else:
                joined[:, cut] = index[plane - 4, wave].astype(jnp.float32)
        if plane < 4:
            values = exact_dot(joined[...], matrix, ((1,), (0,)))
        else:
            values = dot(joined[...].astype(jnp.bfloat16), matrix, ((1,), (0,)))
        for step in range(STEPS):
            piece = values[:, step * 128 : (step + 1) * 128]
            if plane < 4:
                fields[plane, step] = piece
            else:
                indices[plane - 4, step] = piece


def merge_kernel(own, indices, low, high, spread, fields, indices0, top, bottom, joined):
    lane = lax.broadcasted_iota(jnp.int32, (ROWS, 128), 1)
    matrix = spread[2 * COLS :, :]
    for plane in range(5):
        from_low, from_high = low[plane // 2], high[plane // 2]
        if plane % 2 == 0:
            from_high = pltpu.roll(from_high, 64, 1)
        else:
            from_low = pltpu.roll(from_low, 64, 1)
        joined[plane * ROWS : (plane + 1) * ROWS, :] = jnp.where(lane < 64, from_low, from_high)
    values = exact_dot(joined[...], matrix, ((1,), (0,)))
    for plane in range(5):
        for step in range(STEPS):
            piece = values[plane * ROWS : (plane + 1) * ROWS, step * 128 : (step + 1) * 128]
            if plane < 4:
                piece = piece + own[plane, step]
                fields[plane, step] = piece
                rows, at = HALO, (plane * STEPS + step) * HALO
            else:
                piece = piece + indices[0, step]
                indices0[step] = piece
                rows, at = INDEX_HALO, FIELD_ROWS + step * INDEX_HALO
            top[at : at + rows, :] = piece[:rows]
            bottom[at : at + rows, :] = piece[ROWS - rows :]


def advance(terms, past, plane, origin, ahead, count, mask, first):
    now = 0 if first else past + 1

    def rows(first_row):
        return pl.ds(first_row, 8, stride=count)

    def load(r):
        return [terms[now, plane, step, rows(origin + ahead + r), :] for step in range(STEPS)]

    values = [load(r) for r in range(-1, count + 1)]
    pairs = [[a + b for a, b in zip(values[r], values[r + 1])] for r in range(count + 1)]
    for r in range(count):
        column = [a + b for a, b in zip(pairs[r], pairs[r + 1])]
        from_left = pltpu.roll(column[STEPS - 1], 1, 1)
        from_right = pltpu.roll(column[0], 127, 1)
        across = [column[s] + column[s + 1] for s in range(STEPS - 1)]
        both = [(from_left + column[0]) + across[0]]
        both += [across[s - 1] + across[s] for s in range(1, STEPS - 1)]
        both.append(across[STEPS - 2] + (column[STEPS - 1] + from_right))
        for step in range(STEPS):
            moved = mask(step, r) * both[step]
            value = values[r + 1][step]
            if first:
                new = 0.5 * moved - value
            else:
                new = (moved - (value + value)) - terms[past, plane, step, rows(origin + 2 * ahead + r), :]
            terms[now + 1, plane, step, rows(origin + r), :] = new


def combine(terms, table, place, rows, step, orders):
    total = [None] * 4
    for order in range(orders):
        re = jnp.take_along_axis(jnp.broadcast_to(table[order, :][None], (8, 128)), place, axis=1)
        im = jnp.take_along_axis(jnp.broadcast_to(table[orders + order, :][None], (8, 128)), place, axis=1)
        for waves in (0, 2):
            real = terms[order, waves, step, rows(order), :]
            imag = terms[order, waves + 1, step, rows(order), :]
            if waves == 0:
                new = (re * real - im * imag, re * imag + im * real)
            else:
                new = (re * real + im * imag, re * imag - im * real)
            for part in range(2):
                old = total[waves + part]
                total[waves + part] = new[part] if old is None else old + new[part]
    return total


def column_mask(shape, step, flags):
    column = (lax.broadcasted_iota(jnp.int32, shape, 1) % 64) * STEPS + step
    return 0.25 * jnp.where(column < SIDE, flags[2], jnp.where(column >= SIDE + COLS, flags[3], 1.0))


def inner_kernel(
    flags, fields, indices0, indices1, table, spread, strips0, strips1, picture, inner_source, inner_receiver,
    terms, fresh, masks, places, result,
):
    orders = terms.shape[0]
    for plane in range(4):
        for step in range(STEPS):
            terms[0, plane, step, :ROWS, :] = fields[plane, step]
    for step in range(STEPS):
        places[0, step] = indices0[step].astype(jnp.int32)
        places[1, step] = indices1[step].astype(jnp.int32)
        masks[step] = column_mask((8, 128), step, flags)

    def mask(step, r):
        return masks[step]

    for depth in range(2):
        height = ROWS - 2 * HALF * depth
        for first, last in ((0, 1), (1, 3), (3, 7), (7, 11), (11, 12)):
            count = -(-(height - 2 * (first + 1)) // 8)
            count += count == 8

            def step_on(at, carry, first=first, count=count):
                past, pair = lax.div(at, 2), lax.rem(at, 2)
                for plane in range(2):
                    advance(terms, past, 2 * pair + plane, 0, 1, count, mask, first == 0)
                return carry

            start = max(first - 1, 0)
            lax.fori_loop(2 * start, 2 * (start + last - first), step_on, 0)

        strips = (strips0, strips1)[depth]

        def hand_over(order, carry, strips=strips, height=height):
            for plane in range(4):
                for step in range(STEPS):
                    strips[order, plane, step, :STRIP, :] = terms[order, plane, step, :STRIP, :]
                    strips[order, plane, step, STRIP:, :] = terms[order, plane, step, pl.ds(height - STRIP - 2 * order, STRIP), :]
            return carry

        lax.fori_loop(0, orders, hand_over, 0)
        first_row = HALF * (depth + 1)
        count = (ROWS - 2 * first_row) // 8

        def gather(r, carry, depth=depth, first_row=first_row, count=count):
            own_rows = pl.ds(first_row + r, 8, stride=count)
            for step in range(STEPS):
                place = places[depth, step, own_rows, :]
                total = combine(terms, table, place, lambda k: pl.ds(HALF - k + r, 8, stride=count), step, orders)
                for plane in range(4):
                    fresh[plane, step, pl.ds(r, 8, stride=count), :] = total[plane]
                picture[depth, step, own_rows, :] = total[0] * total[2] + total[1] * total[3]
            return carry

        lax.fori_loop(0, count, gather, 0)
        for plane in range(4):
            for step in range(STEPS):
                piece = fresh[plane, step, : 8 * count, :]
                if depth == 0:
                    terms[0, plane, step, : 8 * count, :] = piece
                else:
                    result[plane * 8 * count : (plane + 1) * 8 * count, step * 128 : (step + 1) * 128] = piece

    size = ROWS - 2 * HALO
    values = exact_dot(result[...], spread[: 2 * COLS, :], ((1,), (1,)))
    for plane in range(4):
        out = (inner_source, inner_receiver)[plane // 2]
        for wave in range(2):
            out[plane % 2, wave] = values[plane * size : (plane + 1) * size, wave * COLS : (wave + 1) * COLS]


def rim_kernel(
    flags, fields, indices0, indices1, above, below, strips0, strips1, inner_picture, inner_source, inner_receiver,
    table, spread, source_out, receiver_out, image, upper, lower, fresh, masks, places, picture, result,
):
    orders = upper.shape[0]
    for plane in range(4):
        for step in range(STEPS):
            at = (plane * STEPS + step) * HALO
            upper[0, plane, step, :HALO, :] = above[at : at + HALO, :]
            upper[0, plane, step, HALO:, :] = fields[plane, step, :STRIP, :]
            lower[0, plane, step, :STRIP, :] = fields[plane, step, ROWS - STRIP :, :]
            lower[0, plane, step, STRIP:, :] = below[at : at + HALO, :]
    for step in range(STEPS):
        at = FIELD_ROWS + step * INDEX_HALO
        places[0, 0, step, :INDEX_HALO, :] = above[at : at + INDEX_HALO, :].astype(jnp.int32)
        places[0, 0, step, INDEX_HALO:, :] = indices0[step, :INDEX_HALO, :].astype(jnp.int32)
        places[0, 1, step, :INDEX_HALO, :] = indices0[step, ROWS - INDEX_HALO :, :].astype(jnp.int32)
        places[0, 1, step, INDEX_HALO:, :] = below[at : at + INDEX_HALO, :].astype(jnp.int32)
        places[1, 0, step] = indices1[step, : 2 * INDEX_HALO, :].astype(jnp.int32)
        places[1, 1, step] = indices1[step, ROWS - 2 * INDEX_HALO :, :].astype(jnp.int32)
        masks[step] = column_mask((8, 128), step, flags)
        for depth in range(2):
            picture[depth, step, OFFSET : OFFSET + ROWS, :] = inner_picture[depth, step]

    width = HALO // 8
    sublane = lax.broadcasted_iota(jnp.int32, (8, 128), 0) * width
    for depth in range(2):
        strips = (strips0, strips1)[depth]
        if depth == 1:
            for plane in range(4):
                for step in range(STEPS):
                    upper[0, plane, step, :HALO, :] = fresh[0, plane, step]
                    upper[0, plane, step, HALO:, :] = strips[0, plane, step, :STRIP, :]
                    lower[0, plane, step, :STRIP, :] = strips[0, plane, step, STRIP:, :]
                    lower[0, plane, step, STRIP:, :] = fresh[1, plane, step]

        def step_on(past, carry, first, depth=depth, strips=strips):
            order = 1 if first else past + 2
            shift = order - HALO + HALF * depth
            inside_upper = [jnp.where(sublane + (r + shift) >= 0, 1.0, flags[0]) for r in range(width)]
            inside_lower = [jnp.where(sublane + (r - HALO - shift) < 0, 1.0, flags[1]) for r in range(width)]
            for plane in range(4):
                for step in range(STEPS):
                    upper[order, plane, step, HALO:, :] = strips[order, plane, step, :STRIP, :]
                    lower[order, plane, step, :STRIP, :] = strips[order, plane, step, STRIP:, :]
                advance(upper, past, plane, 0, 1, width, lambda step, r: inside_upper[r] * masks[step], first)
                advance(lower, past, plane, STRIP, -1, width, lambda step, r: inside_lower[r] * masks[step], first)
            return carry

        step_on(0, 0, True)
        lax.fori_loop(0, orders - 2, lambda past, carry: step_on(past, carry, False), 0)

        def gather(r, carry, depth=depth):
            for side, terms in enumerate((upper, lower)):
                ahead, start = ((-1, HALF), (1, STRIP - HALF))[side]
                in_places = ((4, 4), (0, 8))[depth][side]
                in_picture = OFFSET + (-HALF + HALF * depth, ROWS - HALF - HALF * depth)[side]
                for step in range(STEPS):
                    place = places[depth, side, step, pl.ds(in_places + r, 8, stride=width), :]
                    total = combine(
                        terms, table, place, lambda k: pl.ds(start + ahead * k + r, 8, stride=width), step, orders
                    )
                    for plane in range(4):
                        fresh[side, plane, step, pl.ds(r, 8, stride=width), :] = total[plane]
                    picture[depth, step, pl.ds(in_picture + r, 8, stride=width), :] = total[0] * total[2] + total[1] * total[3]
            return carry

        lax.fori_loop(0, width, gather, 0)

    for step in range(STEPS):
        cut = slice(step * 128, (step + 1) * 128)
        for plane in range(4):
            at = 2 * HALO * plane
            result[at : at + HALO, cut] = fresh[0, plane, step]
            result[at + HALO : at + 2 * HALO, cut] = fresh[1, plane, step]
        for depth in range(2):
            at = 8 * HALO + ROWS * depth
            result[at : at + ROWS, cut] = picture[depth, step, OFFSET : OFFSET + ROWS, :]
    values = exact_dot(result[...], spread[: 2 * COLS, :], ((1,), (1,)))
    for plane in range(4):
        out = (source_out, receiver_out)[plane // 2]
        inner = (inner_source, inner_receiver)[plane // 2]
        at = 2 * HALO * plane
        for wave in range(2):
            cut = slice(wave * COLS, (wave + 1) * COLS)
            out[plane % 2, wave, :HALO] = values[at : at + HALO, cut]
            out[plane % 2, wave, INNER] = inner[plane % 2, wave]
            out[plane % 2, wave, ROWS - HALO :] = values[at + HALO : at + 2 * HALO, cut]
    for depth in range(2):
        at = 8 * HALO + ROWS * depth
        total = values[at : at + ROWS, :COLS] + values[at : at + ROWS, COLS:]
        for part in range(8):
            image[part, depth] = total[part * 8 : (part + 1) * 8]


def full(count):
    return [pl.BlockSpec(memory_space=pltpu.VMEM)] * count


def shape(*dims, dtype=jnp.float32):
    return jax.ShapeDtypeStruct(dims, dtype)


def params(megabytes):
    return pltpu.CompilerParams(vmem_limit_bytes=megabytes * 1024 * 1024)


def cost(flops):
    return pl.CostEstimate(flops=flops, bytes_accessed=2**20, transcendentals=0)


def shift(block, axis, forward):
    count = lax.axis_size(axis)
    pairs = [(i, i + 1) for i in range(count - 1)]
    return lax.ppermute(block, axis, pairs if forward else [(b, a) for a, b in pairs])


def extrapolate(source, receiver, table_index, coef_table):
    orders = coef_table.shape[2]
    spread = spread_matrix()
    at_x, at_y = lax.axis_index("sx"), lax.axis_index("sy")
    flags = jnp.stack(
        [at_x > 0, at_x < lax.axis_size("sx") - 1, at_y > 0, at_y < lax.axis_size("sy") - 1]
    ).astype(jnp.float32)
    table = jnp.pad(jnp.swapaxes(coef_table, 1, 2).reshape(2 * orders, -1), ((0, 0), (0, 128 - coef_table.shape[1])))
    scalars = [pl.BlockSpec(memory_space=pltpu.SMEM)]

    left, right = pl.pallas_call(
        edges_kernel,
        out_shape=(shape(3, ROWS, 128), shape(3, ROWS, 128)),
        in_specs=[pl.BlockSpec(memory_space=pltpu.HBM)] * 3,
        out_specs=tuple(full(2)),
        scratch_shapes=[
            pltpu.VMEM((2, 2, 2, ROWS, COLS), jnp.float32),
            pltpu.VMEM((2, ROWS, COLS), jnp.int32),
            pltpu.SemaphoreType.DMA((3,)),
        ],
        compiler_params=params(56),
        name="edges",
    )(source, receiver, table_index)
    low = shift(right, "sy", True)
    high = shift(left, "sy", False)
    own, indices = pl.pallas_call(
        own_kernel,
        out_shape=(shape(4, STEPS, ROWS, 128), shape(2, STEPS, ROWS, 128)),
        in_specs=full(4),
        out_specs=tuple(full(2)),
        scratch_shapes=[pltpu.VMEM((ROWS, 2 * COLS), jnp.float32)],
        compiler_params=params(16),
        cost_estimate=cost(2 * 10**9),
        name="own",
    )(source, receiver, table_index, spread)
    fields, indices0, top, bottom = pl.pallas_call(
        merge_kernel,
        out_shape=(shape(4, STEPS, ROWS, 128), shape(STEPS, ROWS, 128), shape(SEND, 128), shape(SEND, 128)),
        in_specs=full(5),
        out_specs=tuple(full(4)),
        scratch_shapes=[pltpu.VMEM((5 * ROWS, 128), jnp.float32)],
        compiler_params=params(16),
        name="merge",
    )(own, indices, low, high, spread)
    indices1 = indices[1]
    above = shift(bottom, "sx", True)
    below = shift(top, "sx", False)
    strip = shape(orders, 4, STEPS, 2 * STRIP, 128)
    strips0, strips1, picture, inner_source, inner_receiver = pl.pallas_call(
        inner_kernel,
        out_shape=(
            strip,
            strip,
            shape(2, STEPS, ROWS, 128),
            shape(2, 2, ROWS - 2 * HALO, COLS),
            shape(2, 2, ROWS - 2 * HALO, COLS),
        ),
        in_specs=scalars + full(5),
        out_specs=tuple(full(5)),
        scratch_shapes=[
            pltpu.VMEM((orders, 4, STEPS, ROWS + 16, 128), jnp.float32),
            pltpu.VMEM((4, STEPS, ROWS - HALO, 128), jnp.float32),
            pltpu.VMEM((STEPS, 8, 128), jnp.float32),
            pltpu.VMEM((2, STEPS, ROWS, 128), jnp.int32),
            pltpu.VMEM((4 * (ROWS - 2 * HALO), WIDE), jnp.float32),
        ],
        compiler_params=params(32),
        cost_estimate=cost(10**10),
        name="inner",
    )(flags, fields, indices0, indices1, table, spread)
    return pl.pallas_call(
        rim_kernel,
        out_shape=(shape(2, 2, ROWS, COLS), shape(2, 2, ROWS, COLS), shape(8, 2, 8, COLS)),
        in_specs=scalars + full(12),
        out_specs=tuple(full(3)),
        scratch_shapes=[
            pltpu.VMEM((orders, 4, STEPS, HALO + STRIP, 128), jnp.float32),
            pltpu.VMEM((orders, 4, STEPS, HALO + STRIP, 128), jnp.float32),
            pltpu.VMEM((2, 4, STEPS, HALO, 128), jnp.float32),
            pltpu.VMEM((STEPS, 8, 128), jnp.float32),
            pltpu.VMEM((2, 2, STEPS, 2 * INDEX_HALO, 128), jnp.int32),
            pltpu.VMEM((2, STEPS, TALL, 128), jnp.float32),
            pltpu.VMEM((8 * HALO + 2 * ROWS, WIDE), jnp.float32),
        ],
        compiler_params=params(32),
        name="rim",
    )(flags, fields, indices0, indices1, above, below, strips0, strips1, picture, inner_source, inner_receiver, table, spread)


def add_over_freq(pieces):
    groups = [[y * 4 + z * 2 + core for y in range(4) for core in range(2)] for z in range(2)]
    mine = jnp.sum(lax.all_to_all(pieces, "freq", 0, 0, axis_index_groups=groups), axis=0)
    mine = mine + lax.ppermute(mine, "freq", [(i, i ^ 2) for i in range(16)])
    blocks = lax.all_to_all(jnp.broadcast_to(mine[None], pieces.shape), "freq", 0, 0, axis_index_groups=groups)
    return jnp.swapaxes(blocks, 0, 1).reshape(2, ROWS, COLS)


def local(source, receiver, table_index, coef_table):
    source_out, receiver_out, pieces = extrapolate(source, receiver, table_index, coef_table)
    return source_out, receiver_out, add_over_freq(pieces)


def solution(mesh):
    placed = P(None, "freq", "sx", "sy")
    return jax.shard_map(
        local,
        mesh=mesh,
        in_specs=(placed, placed, placed, P()),
        out_specs=(placed, placed, P(None, "sx", "sy")),
        check_vma=False,
    )
```

time: 808 us -> 73.8 us (0.09)
  waiting for transfers between devices: 403 us -> 1.12 us
  starting transfers between devices: 301 us -> 24.6 us
  local copies, waits for them, and re-layouts: 42.1 us -> 1.43 us
  other arithmetic: 37.2 us -> 1.76 us
  Pallas kernels: 0 us -> 22.2 us
  blocking collectives: 0 us -> 21.3 us
  between operations: 14.3 us -> 0.88 us
    psum x1 -> x0, waiting for transfers between devices: 314 us -> none  [local(): images.append(lax.psum(local_image, 'freq'))]
    ppermute x96 -> x5, starting transfers between devices: 300 us -> 24.6 us  [the longest x1 14.5 us: add_over_freq(): mine = mine + lax.ppermute(mine, 'freq', [(i, i ^ 2) for i in range(16)])]
    ppermute x96 -> x5, waiting for transfers between devices: 89.6 us -> 1.12 us  [the longest x1 1.11 us: add_over_freq(): mine = mine + lax.ppermute(mine, 'freq', [(i, i ^ 2) for i in range(16)])]
    pallas_call x0 -> x5, Pallas kernels: none -> 22.2 us  [the longest x1 9.28 us: extrapolate(): pl.pallas_call(rim_kernel, out_shape=(shape(2, 2, ROWS, COLS), shape(2, 2...]
    mul x22 -> x0, local copies, waits for them, and re-layouts: 21.8 us -> none  [combine(): real_part = coef_re * term[:, 0] - signs * coef_im * term[:, 1]]
    all_to_all x0 -> x2, blocking collectives: none -> 21.3 us  [the longest x1 11.8 us: add_over_freq(): lax.all_to_all(pieces, 'freq', 0, 0, axis_index_groups=groups)]
    sub x46 -> x2, other arithmetic: 17.9 us -> 0.01 us  [the longest x1 0.01 us: spread_matrix(): step, lane = (n // 128, n % 128)]
    unnamed x18 -> x6, local copies, waits for them, and re-layouts: 12.6 us -> 0.01 us
  transfers between devices with their start and end apart: 97 -> 5, of which waited for: 69 -> 1; matrix products, arithmetic and copies ran while one was open for 5% -> 3% of each run, Pallas kernels for 0% -> 14%
where the time goes in v2:
time: 73.8 us; the launch traced here: 73.3 us
  starting transfers between devices  24.6 us (33%)
  Pallas kernels  22.2 us (30%)
  blocking collectives  21.3 us (29%)
  other arithmetic  1.76 us (2%)
  local copies, waits for them, and re-layouts  1.43 us (2%)
  waiting for transfers between devices  1.12 us (2%)
  between operations  0.88 us (1%)
    ppermute x1, starting transfers between devices, add_over_freq(): mine = mine + lax.ppermute(mine, 'freq', [(i, i ^ 2) for i in range(16)])  14.5 us
    all_to_all x1, blocking collectives, add_over_freq(): lax.all_to_all(pieces, 'freq', 0, 0, axis_index_groups=groups)  11.8 us
    ppermute x4, starting transfers between devices, shift(): lax.ppermute(block, axis, pairs if forward else [(b, a) for a, b in pairs])  10.1 us
    all_to_all x1, blocking collectives, add_over_freq(): lax.all_to_all(jnp.broadcast_to(mine[None], pieces.shape), 'freq', 0, 0,...  9.49 us
    pallas_call x1, Pallas kernels, extrapolate(): pl.pallas_call(rim_kernel, out_shape=(shape(2, 2, ROWS, COLS), shape(2, 2...  9.28 us
    pallas_call x1, Pallas kernels, extrapolate(): pl.pallas_call(inner_kernel, out_shape=(strip, strip, shape(2, STEPS, ROW...  8.59 us
    pallas_call x1, Pallas kernels, extrapolate(): pl.pallas_call(edges_kernel, out_shape=(shape(3, ROWS, 128), shape(3, ROW...  2.04 us
    pallas_call x1, Pallas kernels, extrapolate(): pl.pallas_call(own_kernel, out_shape=(shape(4, STEPS, ROWS, 128), shape(2...  1.75 us
  transfers between devices with their start and end apart: 5, of which 1 were waited for; matrix products, arithmetic and copies ran while one was open for 3% of the time, Pallas kernels for 14%

profile of v2, /device:TPU:1, one launch (start us, length us, event | category | flops | bytes accessed | tf_op | source)
XLA Modules:
  0.0 73.3 jit_solution(16704408635833667272)
XLA Ops:
  0.6 0.0 copy-start.2
  0.6 0.0 copy-start.1
  0.7 0.0 copy-start
  0.7 2.0 %edges.1 = (f32[3,64,128]{2,1,0:T(8,128)}, f32[3,64,128]{2,1,0:T(8,128)}) custom-call(f32[2,2,64,256]{3,2,1,0:T(8,128)} %source.3, f32[2,2,64,256]{3,2,1,0:T(8,128)} %receiver.3, s32[2,2,64,256]{3,2,1,0:T(8,128)} %index.3), custom_call_target="tpu_custom_call" | custom-call | tf_op jit(solution)/shard_map/edges/pallas_call | solution.py:373
  2.7 3.9 %collective-permute-start = (f32[3,64,128]{2,1,0:T(8,128)}, f32[3,64,128]{2,1,0:T(8,128)S(1)}, u32[]{:S(2)}, u32[]{:S(2)}) collective-permute-start(f32[3,64,128]{2,1,0:T(8,128)} %get-tuple-element.21), channel_id=1, source_target_pairs={{0,1},{1,2},{2,3},{4,5},{5,6},{6,7},{8,9},{9,10},{10,11},{12,13},{... | collective-permute-start | bytes 294920 | tf_op jit(solution)/shard_map/ppermute | solution.py:360
  6.7 1.3 %collective-permute-start.1 = (f32[3,64,128]{2,1,0:T(8,128)}, f32[3,64,128]{2,1,0:T(8,128)S(1)}, u32[]{:S(2)}, u32[]{:S(2)}) collective-permute-start(f32[3,64,128]{2,1,0:T(8,128)} %get-tuple-element.22), channel_id=1, source_target_pairs={{1,0},{2,1},{3,2},{5,4},{6,5},{7,6},{9,8},{10,9},{11,10},{13,12},{... | collective-permute-start | bytes 294920 | tf_op jit(solution)/shard_map/ppermute | solution.py:360
  8.1 0.7 copy.10
  8.8 1.6 %and_convert_fusion.spread = bf16[640,640]{1,0:T(8,128)(2,1)S(1)} fusion(s32[640]{0:T(1024)S(1)} %get-tuple-element.40, s32[640]{0:T(1024)S(1)} %get-tuple-element.50, s32[640]{0:T(1024)S(1)} %get-tuple-element.49, s32[640]{0:T(1024)S(1)} %get-tuple-element.36, s32[640]{0:T(1024)S(1)} %get-tuple-element.44, s32[640]{0:T(1024)S(1)} %get-tuple-element.41, ...), kind=kLoop, calls=%fused_computation.23 | loop fusion | flops 18841600 | bytes 856960 | tf_op jit(solution)/shard_map/convert_element_type | solution.py:32
  10.4 0.0 copy-done.2
  10.4 0.0 copy-done.1
  10.5 0.0 copy-done
  10.5 1.7 %own.1 = (f32[4,5,64,128]{3,2,1,0:T(8,128)S(1)}, f32[2,5,64,128]{3,2,1,0:T(8,128)S(1)}) custom-call(f32[2,2,64,256]{3,2,1,0:T(8,128)S(1)} %copy-done, f32[2,2,64,256]{3,2,1,0:T(8,128)S(1)} %copy-done.1, s32[2,2,64,256]{3,2,1,0:T(8,128)S(1)} %copy-done.2, bf16[640,640]{1,0:T(8,128)(2,1)S(1)} %and_convert_fusion.spread), custom_call_target="tpu_custom_call" | custom-call | flops 2000000000 | bytes 1048576 | tf_op jit(solution)/shard_map/own/pallas_call | solution.py:388
  12.3 0.1 add_convert_fusion.flags
  12.3 0.0 collective-permute-done.low
  12.3 0.0 collective-permute-done.1.high
  12.3 0.5 merge.1
  12.9 3.6 %collective-permute-start.2 = (f32[560,128]{1,0:T(8,128)S(1)}, f32[560,128]{1,0:T(8,128)S(1)}, u32[]{:S(2)}, u32[]{:S(2)}) collective-permute-start(f32[560,128]{1,0:T(8,128)S(1)} %get-tuple-element.25), channel_id=1, source_target_pairs={{0,4},{4,8},{8,12},{12,16},{16,20},{20,24},{24,28},{1,5},{5,9},{9,... | collective-permute-start | bytes 860168 | tf_op jit(solution)/shard_map/ppermute | solution.py:360
  16.4 1.3 %collective-permute-start.3 = (f32[560,128]{1,0:T(8,128)S(1)}, f32[560,128]{1,0:T(8,128)S(1)}, u32[]{:S(2)}, u32[]{:S(2)}) collective-permute-start(f32[560,128]{1,0:T(8,128)S(1)} %get-tuple-element.26), channel_id=1, source_target_pairs={{4,0},{8,4},{12,8},{16,12},{20,16},{24,20},{28,24},{5,1},{9,5},{13... | collective-permute-start | bytes 860168 | tf_op jit(solution)/shard_map/ppermute | solution.py:360
  17.8 8.6 %inner.1 = (f32[13,4,5,32,128]{4,3,2,1,0:T(8,128)S(1)}, f32[13,4,5,32,128]{4,3,2,1,0:T(8,128)S(1)}, f32[2,5,64,128]{3,2,1,0:T(8,128)S(1)}, f32[2,2,16,256]{3,2,1,0:T(8,128)S(1)}, f32[2,2,16,256]{3,2,1,0:T(8,128)S(1)}) custom-call(f32[4]{0:T(128)S(1)} %add_convert_fusion.flags, f32[4,5,64,128]{3,2,1,0:T(8,128)S(1)} %get-tuple-element.23.fields, ...), custom_call_target="tpu_custom_call" | custom-call | flops 10000000000 | bytes 1048576 | tf_op jit(solution)/shard_map/inner/pallas_call | solution.py:411
  26.3 0.0 collective-permute-done.2.above
  26.4 0.0 collective-permute-done.3.below
  26.4 9.3 %rim.1 = (f32[2,2,64,256]{3,2,1,0:T(8,128)}, f32[2,2,64,256]{3,2,1,0:T(8,128)}, f32[8,2,8,256]{3,2,1,0:T(8,128)S(1)}) custom-call(f32[4]{0:T(128)S(1)} %add_convert_fusion.flags, f32[4,5,64,128]{3,2,1,0:T(8,128)S(1)} %get-tuple-element.23.fields, f32[5,64,128]{2,1,0:T(8,128)S(1)} %get-tuple-element.24.indices0, ...), custom_call_target="tpu_custom_call" | custom-call | tf_op jit(solution)/shard_map/rim/pallas_call | solution.py:433
  35.6 11.8 %all_to_all.10 = f32[8,2,8,256]{3,2,1,0:T(8,128)S(1)} all-to-all(f32[8,2,8,256]{3,2,1,0:T(8,128)S(1)} %get-tuple-element.34), channel_id=1, replica_groups={{0,32,128,160,256,288,384,416},{64,96,192,224,320,352,448,480},{1,33,12..., dimensions={0} | all-to-all | bytes 262144 | tf_op jit(solution)/shard_map/all_to_all | solution.py:454
  47.5 14.5 %collective-permute-start.4 = (f32[2,8,256]{2,1,0:T(8,128)S(1)}, f32[2,8,256]{2,1,0:T(8,128)S(1)}, u32[]{:S(2)}, u32[]{:S(2)}) collective-permute-start(f32[2,8,256]{2,1,0:T(8,128)S(1)} %reduce_sum.9), channel_id=1, source_target_pairs={{0,64},{32,96},{64,0},{96,32},{128,192},{160,224},{192,128},{224,1... | collective-permute-start | bytes 49160 | tf_op jit(solution)/shard_map/ppermute | solution.py:455
  62.0 1.1 %collective-permute-done.4 = f32[2,8,256]{2,1,0:T(8,128)S(1)} collective-permute-done((f32[2,8,256]{2,1,0:T(8,128)S(1)}, f32[2,8,256]{2,1,0:T(8,128)S(1)}, u32[]{:S(2)}, u32[]{:S(2)}) %collective-permute-start.4) | collective-permute-done | bytes 16416 | tf_op jit(solution)/shard_map/ppermute | solution.py:455
  63.1 9.5 %all_to_all.11 = f32[8,2,8,256]{3,2,1,0:T(8,128)S(1)} all-to-all(f32[8,2,8,256]{3,2,1,0:T(8,128)S(1)} %broadcast_in_dim.13), channel_id=1, replica_groups={{0,32,128,160,256,288,384,416},{64,96,192,224,320,352,448,480},{1,33,12..., dimensions={0} | all-to-all | bytes 262144 | tf_op jit(solution)/shard_map/all_to_all | solution.py:456
  72.6 0.7 copy.13
  (17 shorter events, 0.1 us)
Async XLA Ops:
  0.6 9.8 %copy-start.2 = (s32[2,2,64,256]{3,2,1,0:T(8,128)S(1)}, s32[2,2,64,256]{3,2,1,0:T(8,128)}, u32[]{:S(2)}) copy-start(s32[2,2,64,256]{3,2,1,0:T(8,128)} %index.3) | copy-start | bytes 786436
  0.6 9.8 %copy-start.1 = (f32[2,2,64,256]{3,2,1,0:T(8,128)S(1)}, f32[2,2,64,256]{3,2,1,0:T(8,128)}, u32[]{:S(2)}) copy-start(f32[2,2,64,256]{3,2,1,0:T(8,128)} %receiver.3) | copy-start | bytes 786436
  0.7 9.8 %copy-start = (f32[2,2,64,256]{3,2,1,0:T(8,128)S(1)}, f32[2,2,64,256]{3,2,1,0:T(8,128)}, u32[]{:S(2)}) copy-start(f32[2,2,64,256]{3,2,1,0:T(8,128)} %source.3) | copy-start | bytes 786436
  2.7 9.6 %collective-permute-start = (f32[3,64,128]{2,1,0:T(8,128)}, f32[3,64,128]{2,1,0:T(8,128)S(1)}, u32[]{:S(2)}, u32[]{:S(2)}) collective-permute-start(f32[3,64,128]{2,1,0:T(8,128)} %get-tuple-element.21), channel_id=1, source_target_pairs={{0,1},{1,2},{2,3},{4,5},{5,6},{6,7},{8,9},{9,10},{10,11},{12,13},{... | collective-permute-start | bytes 294920 | tf_op jit(solution)/shard_map/ppermute | solution.py:360
  6.7 5.7 %collective-permute-start.1 = (f32[3,64,128]{2,1,0:T(8,128)}, f32[3,64,128]{2,1,0:T(8,128)S(1)}, u32[]{:S(2)}, u32[]{:S(2)}) collective-permute-start(f32[3,64,128]{2,1,0:T(8,128)} %get-tuple-element.22), channel_id=1, source_target_pairs={{1,0},{2,1},{3,2},{5,4},{6,5},{7,6},{9,8},{10,9},{11,10},{13,12},{... | collective-permute-start | bytes 294920 | tf_op jit(solution)/shard_map/ppermute | solution.py:360
  12.9 13.5 %collective-permute-start.2 = (f32[560,128]{1,0:T(8,128)S(1)}, f32[560,128]{1,0:T(8,128)S(1)}, u32[]{:S(2)}, u32[]{:S(2)}) collective-permute-start(f32[560,128]{1,0:T(8,128)S(1)} %get-tuple-element.25), channel_id=1, source_target_pairs={{0,4},{4,8},{8,12},{12,16},{16,20},{20,24},{24,28},{1,5},{5,9},{9,... | collective-permute-start | bytes 860168 | tf_op jit(solution)/shard_map/ppermute | solution.py:360
  16.4 9.9 %collective-permute-start.3 = (f32[560,128]{1,0:T(8,128)S(1)}, f32[560,128]{1,0:T(8,128)S(1)}, u32[]{:S(2)}, u32[]{:S(2)}) collective-permute-start(f32[560,128]{1,0:T(8,128)S(1)} %get-tuple-element.26), channel_id=1, source_target_pairs={{4,0},{8,4},{12,8},{16,12},{20,16},{24,20},{28,24},{5,1},{9,5},{13... | collective-permute-start | bytes 860168 | tf_op jit(solution)/shard_map/ppermute | solution.py:360
  47.5 15.7 %collective-permute-start.4 = (f32[2,8,256]{2,1,0:T(8,128)S(1)}, f32[2,8,256]{2,1,0:T(8,128)S(1)}, u32[]{:S(2)}, u32[]{:S(2)}) collective-permute-start(f32[2,8,256]{2,1,0:T(8,128)S(1)} %reduce_sum.9), channel_id=1, source_target_pairs={{0,64},{32,96},{64,0},{96,32},{128,192},{160,224},{192,128},{224,1... | collective-permute-start | bytes 49160 | tf_op jit(solution)/shard_map/ppermute | solution.py:455

commit v3 on v2

--- a/solution.py
+++ b/solution.py
@@ -17,40 +17,46 @@
 STRIP = 16
 OFFSET = 32
 TALL = 128
-INNER = slice(HALO, ROWS - HALO)
-
-
-def spread_matrix():
-    k = lax.broadcasted_iota(jnp.int32, (WIDE, WIDE), 0)
-    n = lax.broadcasted_iota(jnp.int32, (WIDE, WIDE), 1)
-    step, lane = n // 128, n % 128
-    wave, column = lane // 64, (lane % 64) * STEPS + step
-    own = k < 2 * COLS
-    edge = k - 2 * COLS
-    from_wave = jnp.where(own, k // COLS, (edge // SIDE) % 2)
-    from_column = jnp.where(own, SIDE + k % COLS, jnp.where(edge < 2 * SIDE, 0, SIDE + COLS) + edge % SIDE)
-    return ((wave == from_wave) & (column == from_column)).astype(jnp.bfloat16)
+BLOCK = 16
+
+
+def fill_spread(spread):
+    lane = lax.broadcasted_iota(jnp.int32, (128, 128), 1)
+    row = lax.broadcasted_iota(jnp.int32, (128, 128), 0)
+    for part in range(STEPS):
+        if part < 4:
+            wave, column = part // 2, SIDE + (part % 2) * 128 + row
+        else:
+            wave = lax.rem(lax.div(row, SIDE), 2)
+            column = lax.rem(row, SIDE) + jnp.where(row < 2 * SIDE, 0, SIDE + COLS)
+        goes = wave * 512 + column
+        for step in range(STEPS):
+            place = lax.div(lane, 64) * 512 + lax.rem(lane, 64) * STEPS + step
+            here = jnp.where(goes == place, 1.0, 0.0).astype(jnp.bfloat16)
+            spread[part * 128 : (part + 1) * 128, step * 128 : (step + 1) * 128] = here
 
 
 def dot(left, right, contract):
     return lax.dot_general(left, right, (contract, ((), ())), preferred_element_type=jnp.float32)
 
 
-def exact_dot(left, right, contract):
+def move(left, right, contract):
     high = left.astype(jnp.bfloat16)
-    rest = left - high.astype(jnp.float32)
-    middle = rest.astype(jnp.bfloat16)
-    low = (rest - middle.astype(jnp.float32)).astype(jnp.bfloat16)
-    return dot(high, right, contract) + dot(middle, right, contract) + dot(low, right, contract)
+    low = (left - high.astype(jnp.float32)).astype(jnp.bfloat16)
+    return dot(high, right, contract) + dot(low, right, contract)
 
 
 def edges_kernel(source, receiver, index, left, right, waves, places, sems):
     copies = [
-        pltpu.make_async_copy(source, waves.at[0], sems.at[0]),
-        pltpu.make_async_copy(receiver, waves.at[1], sems.at[1]),
-        pltpu.make_async_copy(index.at[0], places, sems.at[2]),
+        [
+            pltpu.make_async_copy(field.at[part, wave], waves.at[kind, part, wave], sems.at[kind, 2 * part + wave])
+            for part in range(2)
+            for wave in range(2)
+        ]
+        for kind, field in enumerate((source, receiver))
     ]
-    for copy in copies:
+    copies.append([pltpu.make_async_copy(index.at[depth], places.at[depth], sems.at[2, depth]) for depth in range(2)])
+    for copy in sum(copies, []):
         copy.start()
     lane = lax.broadcasted_iota(jnp.int32, (ROWS, 128), 1)
 
@@ -64,26 +70,28 @@
 
     ends = ((right, 1, 128 - SIDE), (left, 0, 0))
     for kind in range(3):
-        copies[kind].wait()
+        for copy in copies[kind]:
+            copy.wait()
         for out, tile, start in ends:
             cut = slice(tile * 128, (tile + 1) * 128)
             if kind < 2:
                 out[kind] = join([waves[kind, part, wave, :, cut] for part in range(2) for wave in range(2)], start)
             else:
-                out[2] = join([places[wave, :, cut].astype(jnp.float32) for wave in range(2)], start)
-
-
-def own_kernel(source, receiver, index, spread, fields, indices, joined):
+                out[2] = join([places[0, wave, :, cut].astype(jnp.float32) for wave in range(2)], start)
+
+
+def own_kernel(waves, index, fields, indices, spread, joined):
+    fill_spread(spread)
     matrix = spread[: 2 * COLS, :]
     for plane in range(6):
         for wave in range(2):
             cut = slice(wave * COLS, (wave + 1) * COLS)
             if plane < 4:
-                joined[:, cut] = (source, receiver)[plane // 2][plane % 2, wave]
+                joined[:, cut] = waves[plane // 2, plane % 2, wave]
             else:
                 joined[:, cut] = index[plane - 4, wave].astype(jnp.float32)
         if plane < 4:
-            values = exact_dot(joined[...], matrix, ((1,), (0,)))
+            values = move(joined[...], matrix, ((1,), (0,)))
         else:
             values = dot(joined[...].astype(jnp.bfloat16), matrix, ((1,), (0,)))
         for step in range(STEPS):
@@ -104,7 +112,7 @@
         else:
             from_low = pltpu.roll(from_low, 64, 1)
         joined[plane * ROWS : (plane + 1) * ROWS, :] = jnp.where(lane < 64, from_low, from_high)
-    values = exact_dot(joined[...], matrix, ((1,), (0,)))
+    values = move(joined[...], matrix, ((1,), (0,)))
     for plane in range(5):
         for step in range(STEPS):
             piece = values[plane * ROWS : (plane + 1) * ROWS, step * 128 : (step + 1) * 128]
@@ -167,16 +175,26 @@
     return total
 
 
+def fill(lookup, table):
+    orders, parts, entries = table.shape
+    lookup[...] = jnp.zeros(lookup.shape, jnp.float32)
+    for order in range(orders):
+        for part in range(parts):
+            at = part * orders + order
+            lookup[at : at + 1, :entries] = table[order, part : part + 1, :]
+
+
 def column_mask(shape, step, flags):
     column = (lax.broadcasted_iota(jnp.int32, shape, 1) % 64) * STEPS + step
     return 0.25 * jnp.where(column < SIDE, flags[2], jnp.where(column >= SIDE + COLS, flags[3], 1.0))
 
 
 def inner_kernel(
-    flags, fields, indices0, indices1, table, spread, strips0, strips1, picture, inner_source, inner_receiver,
-    terms, fresh, masks, places, result,
+    flags, fields, indices0, indices1, table, strips0, strips1, picture, centre,
+    terms, fresh, masks, places, lookup,
 ):
     orders = terms.shape[0]
+    fill(lookup, table)
     for plane in range(4):
         for step in range(STEPS):
             terms[0, plane, step, :ROWS, :] = fields[plane, step]
@@ -220,7 +238,7 @@
             own_rows = pl.ds(first_row + r, 8, stride=count)
             for step in range(STEPS):
                 place = places[depth, step, own_rows, :]
-                total = combine(terms, table, place, lambda k: pl.ds(HALF - k + r, 8, stride=count), step, orders)
+                total = combine(terms, lookup, place, lambda k: pl.ds(HALF - k + r, 8, stride=count), step, orders)
                 for plane in range(4):
                     fresh[plane, step, pl.ds(r, 8, stride=count), :] = total[plane]
                 picture[depth, step, own_rows, :] = total[0] * total[2] + total[1] * total[3]
@@ -233,21 +251,15 @@
                 if depth == 0:
                     terms[0, plane, step, : 8 * count, :] = piece
                 else:
-                    result[plane * 8 * count : (plane + 1) * 8 * count, step * 128 : (step + 1) * 128] = piece
-
-    size = ROWS - 2 * HALO
-    values = exact_dot(result[...], spread[: 2 * COLS, :], ((1,), (1,)))
-    for plane in range(4):
-        out = (inner_source, inner_receiver)[plane // 2]
-        for wave in range(2):
-            out[plane % 2, wave] = values[plane * size : (plane + 1) * size, wave * COLS : (wave + 1) * COLS]
+                    centre[plane, step] = piece
 
 
 def rim_kernel(
-    flags, fields, indices0, indices1, above, below, strips0, strips1, inner_picture, inner_source, inner_receiver,
-    table, spread, source_out, receiver_out, image, upper, lower, fresh, masks, places, picture, result,
+    flags, fields, indices0, indices1, above, below, strips0, strips1, inner_picture, table, spread, fresh, image,
+    upper, lower, masks, places, picture, result, lookup,
 ):
     orders = upper.shape[0]
+    fill(lookup, table)
     for plane in range(4):
         for step in range(STEPS):
             at = (plane * STEPS + step) * HALO
@@ -303,7 +315,7 @@
                 for step in range(STEPS):
                     place = places[depth, side, step, pl.ds(in_places + r, 8, stride=width), :]
                     total = combine(
-                        terms, table, place, lambda k: pl.ds(start + ahead * k + r, 8, stride=width), step, orders
+                        terms, lookup, place, lambda k: pl.ds(start + ahead * k + r, 8, stride=width), step, orders
                     )
                     for plane in range(4):
                         fresh[side, plane, step, pl.ds(r, 8, stride=width), :] = total[plane]
@@ -313,29 +325,27 @@
         lax.fori_loop(0, width, gather, 0)
 
     for step in range(STEPS):
-        cut = slice(step * 128, (step + 1) * 128)
-        for plane in range(4):
-            at = 2 * HALO * plane
-            result[at : at + HALO, cut] = fresh[0, plane, step]
-            result[at + HALO : at + 2 * HALO, cut] = fresh[1, plane, step]
         for depth in range(2):
-            at = 8 * HALO + ROWS * depth
-            result[at : at + ROWS, cut] = picture[depth, step, OFFSET : OFFSET + ROWS, :]
-    values = exact_dot(result[...], spread[: 2 * COLS, :], ((1,), (1,)))
+            piece = picture[depth, step, OFFSET : OFFSET + ROWS, :]
+            result[depth * ROWS : (depth + 1) * ROWS, step * 128 : (step + 1) * 128] = piece
+    values = move(result[...], spread[: 2 * COLS, :], ((1,), (1,)))
+    total = values[:, :COLS] + values[:, COLS:]
+    for part in range(8):
+        image[part] = total[part * BLOCK : (part + 1) * BLOCK]
+
+
+def finish_kernel(fresh, centre, spread, source_out, receiver_out, result):
     for plane in range(4):
-        out = (source_out, receiver_out)[plane // 2]
-        inner = (inner_source, inner_receiver)[plane // 2]
-        at = 2 * HALO * plane
+        for step in range(STEPS):
+            rows, cut = plane * ROWS, slice(step * 128, (step + 1) * 128)
+            result[rows : rows + HALO, cut] = fresh[0, plane, step]
+            result[rows + HALO : rows + ROWS - HALO, cut] = centre[plane, step]
+            result[rows + ROWS - HALO : rows + ROWS, cut] = fresh[1, plane, step]
+    values = move(result[...], spread[: 2 * COLS, :], ((1,), (1,)))
+    for plane in range(4):
         for wave in range(2):
-            cut = slice(wave * COLS, (wave + 1) * COLS)
-            out[plane % 2, wave, :HALO] = values[at : at + HALO, cut]
-            out[plane % 2, wave, INNER] = inner[plane % 2, wave]
-            out[plane % 2, wave, ROWS - HALO :] = values[at + HALO : at + 2 * HALO, cut]
-    for depth in range(2):
-        at = 8 * HALO + ROWS * depth
-        total = values[at : at + ROWS, :COLS] + values[at : at + ROWS, COLS:]
-        for part in range(8):
-            image[part, depth] = total[part * 8 : (part + 1) * 8]
+            piece = values[plane * ROWS : (plane + 1) * ROWS, wave * COLS : (wave + 1) * COLS]
+            (source_out, receiver_out)[plane // 2][plane % 2, wave] = piece
 
 
 def full(count):
@@ -362,39 +372,39 @@
 
 def extrapolate(source, receiver, table_index, coef_table):
     orders = coef_table.shape[2]
-    spread = spread_matrix()
     at_x, at_y = lax.axis_index("sx"), lax.axis_index("sy")
     flags = jnp.stack(
         [at_x > 0, at_x < lax.axis_size("sx") - 1, at_y > 0, at_y < lax.axis_size("sy") - 1]
     ).astype(jnp.float32)
-    table = jnp.pad(jnp.swapaxes(coef_table, 1, 2).reshape(2 * orders, -1), ((0, 0), (0, 128 - coef_table.shape[1])))
+    table = jnp.transpose(coef_table, (2, 0, 1))
     scalars = [pl.BlockSpec(memory_space=pltpu.SMEM)]
 
-    left, right = pl.pallas_call(
+    left, right, waves, places = pl.pallas_call(
         edges_kernel,
-        out_shape=(shape(3, ROWS, 128), shape(3, ROWS, 128)),
+        out_shape=(
+            pltpu.VMEM((3, ROWS, 128), jnp.float32),
+            pltpu.VMEM((3, ROWS, 128), jnp.float32),
+            pltpu.VMEM((2, 2, 2, ROWS, COLS), jnp.float32),
+            pltpu.VMEM((2, 2, ROWS, COLS), jnp.int32),
+        ),
         in_specs=[pl.BlockSpec(memory_space=pltpu.HBM)] * 3,
-        out_specs=tuple(full(2)),
-        scratch_shapes=[
-            pltpu.VMEM((2, 2, 2, ROWS, COLS), jnp.float32),
-            pltpu.VMEM((2, ROWS, COLS), jnp.int32),
-            pltpu.SemaphoreType.DMA((3,)),
-        ],
-        compiler_params=params(56),
+        out_specs=tuple(full(4)),
+        scratch_shapes=[pltpu.SemaphoreType.DMA((3, 4))],
+        compiler_params=params(16),
         name="edges",
-    )(source, receiver, table_index)
+    )(*(pltpu.with_memory_space_constraint(array, pltpu.HBM) for array in (source, receiver, table_index)))
     low = shift(right, "sy", True)
     high = shift(left, "sy", False)
-    own, indices = pl.pallas_call(
+    own, indices, spread = pl.pallas_call(
         own_kernel,
-        out_shape=(shape(4, STEPS, ROWS, 128), shape(2, STEPS, ROWS, 128)),
-        in_specs=full(4),
-        out_specs=tuple(full(2)),
+        out_shape=(shape(4, STEPS, ROWS, 128), shape(2, STEPS, ROWS, 128), shape(WIDE, WIDE, dtype=jnp.bfloat16)),
+        in_specs=full(2),
+        out_specs=tuple(full(3)),
         scratch_shapes=[pltpu.VMEM((ROWS, 2 * COLS), jnp.float32)],
         compiler_params=params(16),
         cost_estimate=cost(2 * 10**9),
         name="own",
-    )(source, receiver, table_index, spread)
+    )(waves, places)
     fields, indices0, top, bottom = pl.pallas_call(
         merge_kernel,
         out_shape=(shape(4, STEPS, ROWS, 128), shape(STEPS, ROWS, 128), shape(SEND, 128), shape(SEND, 128)),
@@ -408,45 +418,51 @@
     above = shift(bottom, "sx", True)
     below = shift(top, "sx", False)
     strip = shape(orders, 4, STEPS, 2 * STRIP, 128)
-    strips0, strips1, picture, inner_source, inner_receiver = pl.pallas_call(
+    lookup = pltpu.VMEM((2 * orders, 128), jnp.float32)
+    strips0, strips1, picture, centre = pl.pallas_call(
         inner_kernel,
-        out_shape=(
-            strip,
-            strip,
-            shape(2, STEPS, ROWS, 128),
-            shape(2, 2, ROWS - 2 * HALO, COLS),
-            shape(2, 2, ROWS - 2 * HALO, COLS),
-        ),
-        in_specs=scalars + full(5),
-        out_specs=tuple(full(5)),
+        out_shape=(strip, strip, shape(2, STEPS, ROWS, 128), shape(4, STEPS, ROWS - 2 * HALO, 128)),
+        in_specs=scalars + full(4),
+        out_specs=tuple(full(4)),
         scratch_shapes=[
             pltpu.VMEM((orders, 4, STEPS, ROWS + 16, 128), jnp.float32),
             pltpu.VMEM((4, STEPS, ROWS - HALO, 128), jnp.float32),
             pltpu.VMEM((STEPS, 8, 128), jnp.float32),
             pltpu.VMEM((2, STEPS, ROWS, 128), jnp.int32),
-            pltpu.VMEM((4 * (ROWS - 2 * HALO), WIDE), jnp.float32),
+            lookup,
         ],
         compiler_params=params(32),
         cost_estimate=cost(10**10),
         name="inner",
-    )(flags, fields, indices0, indices1, table, spread)
-    return pl.pallas_call(
+    )(flags, fields, indices0, indices1, table)
+    fresh, image = pl.pallas_call(
         rim_kernel,
-        out_shape=(shape(2, 2, ROWS, COLS), shape(2, 2, ROWS, COLS), shape(8, 2, 8, COLS)),
-        in_specs=scalars + full(12),
-        out_specs=tuple(full(3)),
+        out_shape=(shape(2, 4, STEPS, HALO, 128), shape(8, BLOCK, COLS)),
+        in_specs=scalars + full(10),
+        out_specs=tuple(full(2)),
         scratch_shapes=[
             pltpu.VMEM((orders, 4, STEPS, HALO + STRIP, 128), jnp.float32),
             pltpu.VMEM((orders, 4, STEPS, HALO + STRIP, 128), jnp.float32),
-            pltpu.VMEM((2, 4, STEPS, HALO, 128), jnp.float32),
             pltpu.VMEM((STEPS, 8, 128), jnp.float32),
             pltpu.VMEM((2, 2, STEPS, 2 * INDEX_HALO, 128), jnp.int32),
             pltpu.VMEM((2, STEPS, TALL, 128), jnp.float32),
-            pltpu.VMEM((8 * HALO + 2 * ROWS, WIDE), jnp.float32),
+            pltpu.VMEM((2 * ROWS, WIDE), jnp.float32),
+            lookup,
         ],
         compiler_params=params(32),
         name="rim",
-    )(flags, fields, indices0, indices1, above, below, strips0, strips1, picture, inner_source, inner_receiver, table, spread)
+    )(flags, fields, indices0, indices1, above, below, strips0, strips1, picture, table, spread)
+    source_out, receiver_out = pl.pallas_call(
+        finish_kernel,
+        out_shape=(shape(2, 2, ROWS, COLS), shape(2, 2, ROWS, COLS)),
+        in_specs=full(3),
+        out_specs=tuple(full(2)),
+        scratch_shapes=[pltpu.VMEM((4 * ROWS, WIDE), jnp.float32)],
+        compiler_params=params(16),
+        cost_estimate=cost(2 * 10**9),
+        name="finish",
+    )(fresh, centre, spread)
+    return source_out, receiver_out, image
 
 
 def add_over_freq(pieces):
@@ -454,7 +470,7 @@
     mine = jnp.sum(lax.all_to_all(pieces, "freq", 0, 0, axis_index_groups=groups), axis=0)
     mine = mine + lax.ppermute(mine, "freq", [(i, i ^ 2) for i in range(16)])
     blocks = lax.all_to_all(jnp.broadcast_to(mine[None], pieces.shape), "freq", 0, 0, axis_index_groups=groups)
-    return jnp.swapaxes(blocks, 0, 1).reshape(2, ROWS, COLS)
+    return blocks.reshape(2, ROWS, COLS)
 
 
 def local(source, receiver, table_index, coef_table):

time: 73.8 us -> 72.4 us (0.981)
  blocking collectives: 21.3 us -> 11.9 us
  waiting for transfers between devices: 1.12 us -> 7.5 us
  starting transfers between devices: 24.6 us -> 29.7 us
  other arithmetic: 1.76 us -> 0.1 us
  Pallas kernels: 22.2 us -> 20.7 us
    all_to_all x1 -> x0, blocking collectives: 9.49 us -> none  [add_over_freq(): lax.all_to_all(jnp.broadcast_to(mine[None], pieces.shape), 'freq', 0, 0,...]
    all_to_all x0 -> x1, starting transfers between devices: none -> 5.11 us  [add_over_freq(): lax.all_to_all(jnp.broadcast_to(mine[None], pieces.shape), 'freq', 0, 0,...]
    all_to_all x0 -> x1, waiting for transfers between devices: none -> 3.93 us  [add_over_freq(): lax.all_to_all(jnp.broadcast_to(mine[None], pieces.shape), 'freq', 0, 0,...]
    ppermute x4, waiting for transfers between devices: 0.01 us -> 2.46 us  [shift(): lax.ppermute(block, axis, pairs if forward else [(b, a) for a, b in pairs])]
    convert_element_type x1 -> x0, other arithmetic: 1.58 us -> none  [spread_matrix(): return ((wave == from_wave) & (column == from_column)).astype(jnp.bfloat16)]
    pallas_call x2 -> x3, Pallas kernels: 11.3 us -> 10.8 us  [the longest x1 8.08 us: extrapolate(): pl.pallas_call(rim_kernel, out_shape=(shape(2, 4, STEPS, HALO, 128), shap...]
  transfers between devices with their start and end apart: 5 -> 6, of which waited for: 1 -> 3; matrix products, arithmetic and copies ran while one was open for 3% -> 0% of each run, Pallas kernels for 14% -> 15%
where the time goes in v3:
time: 72.4 us; the launch traced here: 72 us
  starting transfers between devices  29.7 us (41%)
  Pallas kernels  20.7 us (29%)
  blocking collectives  11.9 us (16%)
  waiting for transfers between devices  7.5 us (10%)
  local copies, waits for them, and re-layouts  1.34 us (2%)
  between operations  0.77 us (1%)
    ppermute x1, starting transfers between devices, add_over_freq(): mine = mine + lax.ppermute(mine, 'freq', [(i, i ^ 2) for i in range(16)])  14.5 us
    all_to_all x1, blocking collectives, add_over_freq(): lax.all_to_all(pieces, 'freq', 0, 0, axis_index_groups=groups)  11.9 us
    ppermute x4, starting transfers between devices, shift(): lax.ppermute(block, axis, pairs if forward else [(b, a) for a, b in pairs])  10.1 us
    pallas_call x1, Pallas kernels, extrapolate(): pl.pallas_call(rim_kernel, out_shape=(shape(2, 4, STEPS, HALO, 128), shap...  8.08 us
    pallas_call x1, Pallas kernels, extrapolate(): pl.pallas_call(inner_kernel, out_shape=(strip, strip, shape(2, STEPS, ROW...  7.9 us
    all_to_all x1, starting transfers between devices, add_over_freq(): lax.all_to_all(jnp.broadcast_to(mine[None], pieces.shape), 'freq', 0, 0,...  5.11 us
    all_to_all x1, waiting for transfers between devices, add_over_freq(): lax.all_to_all(jnp.broadcast_to(mine[None], pieces.shape), 'freq', 0, 0,...  3.93 us
    ppermute x4, waiting for transfers between devices, shift(): lax.ppermute(block, axis, pairs if forward else [(b, a) for a, b in pairs])  2.46 us
  transfers between devices with their start and end apart: 6, of which 3 were waited for; matrix products, arithmetic and copies ran while one was open for 0% of the time, Pallas kernels for 15%

profile of v3, /device:TPU:1, one launch (start us, length us, event | category | flops | bytes accessed | tf_op | source)
XLA Modules:
  0.0 72.0 jit_solution(17755873724097892666)
XLA Ops:
  0.6 1.4 %edges.1 = (f32[3,64,128]{2,1,0:T(8,128)S(1)}, f32[3,64,128]{2,1,0:T(8,128)S(1)}, f32[2,2,2,64,256]{4,3,2,1,0:T(8,128)S(1)}, s32[2,2,64,256]{3,2,1,0:T(8,128)S(1)}) custom-call(f32[2,2,64,256]{3,2,1,0:T(8,128)} %source.1, f32[2,2,64,256]{3,2,1,0:T(8,128)} %receiver.1, s32[2,2,64,256]{3,2,1,0:T(8,128)} %index.1), custom_call_target="tpu_custom_call" | custom-call | tf_op jit(solution)/shard_map/edges/pallas_call | solution.py:382
  2.0 4.0 %collective-permute-start = (f32[3,64,128]{2,1,0:T(8,128)S(1)}, f32[3,64,128]{2,1,0:T(8,128)S(1)}, u32[]{:S(2)}, u32[]{:S(2)}) collective-permute-start(f32[3,64,128]{2,1,0:T(8,128)S(1)} %get-tuple-element.26), channel_id=1, source_target_pairs={{0,1},{1,2},{2,3},{4,5},{5,6},{6,7},{8,9},{9,10},{10,11},{12,13},{... | collective-permute-start | bytes 294920 | tf_op jit(solution)/shard_map/ppermute | solution.py:370
  6.0 1.3 %collective-permute-start.1 = (f32[3,64,128]{2,1,0:T(8,128)S(1)}, f32[3,64,128]{2,1,0:T(8,128)S(1)}, u32[]{:S(2)}, u32[]{:S(2)}) collective-permute-start(f32[3,64,128]{2,1,0:T(8,128)S(1)} %get-tuple-element.27), channel_id=1, source_target_pairs={{1,0},{2,1},{3,2},{5,4},{6,5},{7,6},{9,8},{10,9},{11,10},{13,12},{... | collective-permute-start | bytes 294920 | tf_op jit(solution)/shard_map/ppermute | solution.py:370
  7.3 0.0 copy-start
  7.3 1.5 %own.1 = (f32[4,5,64,128]{3,2,1,0:T(8,128)S(1)}, f32[2,5,64,128]{3,2,1,0:T(8,128)S(1)}, bf16[640,640]{1,0:T(8,128)(2,1)S(1)}) custom-call(f32[2,2,2,64,256]{4,3,2,1,0:T(8,128)S(1)} %get-tuple-element.22.waves, s32[2,2,64,256]{3,2,1,0:T(8,128)S(1)} %get-tuple-element.23.index), custom_call_target="tpu_custom_call" | custom-call | flops 2000000000 | bytes 1048576 | tf_op jit(solution)/shard_map/own/pallas_call | solution.py:398
  8.8 0.1 add_convert_fusion.flags
  8.9 0.0 collective-permute-done.low
  8.9 2.4 %collective-permute-done.1.high = f32[3,64,128]{2,1,0:T(8,128)S(1)} collective-permute-done((f32[3,64,128]{2,1,0:T(8,128)S(1)}, f32[3,64,128]{2,1,0:T(8,128)S(1)}, u32[]{:S(2)}, u32[]{:S(2)}) %collective-permute-start.1) | collective-permute-done | bytes 98336 | tf_op jit(solution)/shard_map/ppermute | solution.py:370
  11.4 0.4 merge.1
  11.8 3.6 %collective-permute-start.2 = (f32[560,128]{1,0:T(8,128)S(1)}, f32[560,128]{1,0:T(8,128)S(1)}, u32[]{:S(2)}, u32[]{:S(2)}) collective-permute-start(f32[560,128]{1,0:T(8,128)S(1)} %get-tuple-element.31), channel_id=1, source_target_pairs={{0,4},{4,8},{8,12},{12,16},{16,20},{20,24},{24,28},{1,5},{5,9},{9,... | collective-permute-start | bytes 860168 | tf_op jit(solution)/shard_map/ppermute | solution.py:370
  15.4 1.3 %collective-permute-start.3 = (f32[560,128]{1,0:T(8,128)S(1)}, f32[560,128]{1,0:T(8,128)S(1)}, u32[]{:S(2)}, u32[]{:S(2)}) collective-permute-start(f32[560,128]{1,0:T(8,128)S(1)} %get-tuple-element.32), channel_id=1, source_target_pairs={{4,0},{8,4},{12,8},{16,12},{20,16},{24,20},{28,24},{5,1},{9,5},{13... | collective-permute-start | bytes 860168 | tf_op jit(solution)/shard_map/ppermute | solution.py:370
  16.7 0.0 copy-done
  16.7 7.9 %inner.1 = (f32[13,4,5,32,128]{4,3,2,1,0:T(8,128)S(1)}, f32[13,4,5,32,128]{4,3,2,1,0:T(8,128)S(1)}, f32[2,5,64,128]{3,2,1,0:T(8,128)S(1)}, f32[4,5,16,128]{3,2,1,0:T(8,128)S(1)}) custom-call(f32[4]{0:T(128)S(1)} %add_convert_fusion.flags, f32[4,5,64,128]{3,2,1,0:T(8,128)S(1)} %get-tuple-element.29.fields, f32[5,64,128]{2,1,0:T(8,128)S(1)} %get-tuple-element.30.indices0, ...), custom_call_target="tpu_custom_call" | custom-call | flops 10000000000 | bytes 1048576 | tf_op jit(solution)/shard_map/inner/pallas_call | solution.py:422
  24.6 0.0 collective-permute-done.2.above
  24.6 0.0 collective-permute-done.3.below
  24.6 8.1 %rim.1 = (f32[2,4,5,24,128]{4,3,2,1,0:T(8,128)S(1)}, f32[8,16,256]{2,1,0:T(8,128)S(1)}) custom-call(f32[4]{0:T(128)S(1)} %add_convert_fusion.flags, f32[4,5,64,128]{3,2,1,0:T(8,128)S(1)} %get-tuple-element.29.fields, f32[5,64,128]{2,1,0:T(8,128)S(1)} %get-tuple-element.30.indices0, f32[5,64,128]{2,1,0:T(8,128)S(1)} %slice_bitcast_fusion.indices1, ...), custom_call_target="tpu_custom_call" | custom-call | tf_op jit(solution)/shard_map/rim/pallas_call | solution.py:438
  32.7 11.9 %all_to_all.10 = f32[8,16,256]{2,1,0:T(8,128)S(1)} all-to-all(f32[8,16,256]{2,1,0:T(8,128)S(1)} %get-tuple-element.40), channel_id=1, replica_groups={{0,32,128,160,256,288,384,416},{64,96,192,224,320,352,448,480},{1,33,12..., dimensions={0} | all-to-all | bytes 262144 | tf_op jit(solution)/shard_map/all_to_all | solution.py:470
  44.6 14.5 %collective-permute-start.4 = (f32[16,256]{1,0:T(8,128)S(1)}, f32[16,256]{1,0:T(8,128)S(1)}, u32[]{:S(2)}, u32[]{:S(2)}) collective-permute-start(f32[16,256]{1,0:T(8,128)S(1)} %reduce_sum.9), channel_id=1, source_target_pairs={{0,64},{32,96},{64,0},{96,32},{128,192},{160,224},{192,128},{224,1... | collective-permute-start | bytes 49160 | tf_op jit(solution)/shard_map/ppermute | solution.py:471
  59.2 1.1 %collective-permute-done.4 = f32[16,256]{1,0:T(8,128)S(1)} collective-permute-done((f32[16,256]{1,0:T(8,128)S(1)}, f32[16,256]{1,0:T(8,128)S(1)}, u32[]{:S(2)}, u32[]{:S(2)}) %collective-permute-start.4) | collective-permute-done | bytes 16416 | tf_op jit(solution)/shard_map/ppermute | solution.py:471
  60.3 0.7 broadcast_in_dim.2
  61.0 5.1 %all-to-all-start.1 = ((f32[8,16,256]{2,1,0:T(8,128)}), f32[8,16,256]{2,1,0:T(8,128)S(1)}, u32[]{:S(2)}, u32[]{:S(2)}) async-start(f32[8,16,256]{2,1,0:T(8,128)} %broadcast_in_dim.2), calls=%async_computation.1 | async-start | bytes 262144 | tf_op jit(solution)/shard_map/all_to_all | solution.py:472
  66.1 1.4 %finish.1 = (f32[2,2,64,256]{3,2,1,0:T(8,128)}, f32[2,2,64,256]{3,2,1,0:T(8,128)}) custom-call(f32[2,4,5,24,128]{4,3,2,1,0:T(8,128)S(1)} %get-tuple-element.36.fresh, f32[4,5,16,128]{3,2,1,0:T(8,128)S(1)} %get-tuple-element.37.centre, bf16[640,640]{1,0:T(8,128)(2,1)S(1)} %get-tuple-element.28.spread), custom_call_target="tpu_custom_call" | custom-call | flops 2000000000 | bytes 1048576 | tf_op jit(solution)/shard_map/finish/pallas_call | solution.py:455
  67.4 3.9 %all-to-all-done.1 = f32[8,16,256]{2,1,0:T(8,128)S(1)} async-done(((f32[8,16,256]{2,1,0:T(8,128)}), f32[8,16,256]{2,1,0:T(8,128)S(1)}, u32[]{:S(2)}, u32[]{:S(2)}) %all-to-all-start.1) | async-done | bytes 131104 | tf_op jit(solution)/shard_map/all_to_all | solution.py:472
  71.4 0.7 copy.8
  (3 shorter events, 0.0 us)
Async XLA Ops:
  2.0 6.9 %collective-permute-start = (f32[3,64,128]{2,1,0:T(8,128)S(1)}, f32[3,64,128]{2,1,0:T(8,128)S(1)}, u32[]{:S(2)}, u32[]{:S(2)}) collective-permute-start(f32[3,64,128]{2,1,0:T(8,128)S(1)} %get-tuple-element.26), channel_id=1, source_target_pairs={{0,1},{1,2},{2,3},{4,5},{5,6},{6,7},{8,9},{9,10},{10,11},{12,13},{... | collective-permute-start | bytes 294920 | tf_op jit(solution)/shard_map/ppermute | solution.py:370
  6.0 5.4 %collective-permute-start.1 = (f32[3,64,128]{2,1,0:T(8,128)S(1)}, f32[3,64,128]{2,1,0:T(8,128)S(1)}, u32[]{:S(2)}, u32[]{:S(2)}) collective-permute-start(f32[3,64,128]{2,1,0:T(8,128)S(1)} %get-tuple-element.27), channel_id=1, source_target_pairs={{1,0},{2,1},{3,2},{5,4},{6,5},{7,6},{9,8},{10,9},{11,10},{13,12},{... | collective-permute-start | bytes 294920 | tf_op jit(solution)/shard_map/ppermute | solution.py:370
  7.3 9.4 %copy-start = (f32[2,32,13]{1,0,2:T(2,128)S(1)}, f32[2,32,13]{1,0,2:T(2,128)}, u32[]{:S(2)}) copy-start(f32[2,32,13]{1,0,2:T(2,128)} %param.7) | copy-start | bytes 9988
  11.8 12.8 %collective-permute-start.2 = (f32[560,128]{1,0:T(8,128)S(1)}, f32[560,128]{1,0:T(8,128)S(1)}, u32[]{:S(2)}, u32[]{:S(2)}) collective-permute-start(f32[560,128]{1,0:T(8,128)S(1)} %get-tuple-element.31), channel_id=1, source_target_pairs={{0,4},{4,8},{8,12},{12,16},{16,20},{20,24},{24,28},{1,5},{5,9},{9,... | collective-permute-start | bytes 860168 | tf_op jit(solution)/shard_map/ppermute | solution.py:370
  15.4 9.2 %collective-permute-start.3 = (f32[560,128]{1,0:T(8,128)S(1)}, f32[560,128]{1,0:T(8,128)S(1)}, u32[]{:S(2)}, u32[]{:S(2)}) collective-permute-start(f32[560,128]{1,0:T(8,128)S(1)} %get-tuple-element.32), channel_id=1, source_target_pairs={{4,0},{8,4},{12,8},{16,12},{20,16},{24,20},{28,24},{5,1},{9,5},{13... | collective-permute-start | bytes 860168 | tf_op jit(solution)/shard_map/ppermute | solution.py:370
  44.6 15.7 %collective-permute-start.4 = (f32[16,256]{1,0:T(8,128)S(1)}, f32[16,256]{1,0:T(8,128)S(1)}, u32[]{:S(2)}, u32[]{:S(2)}) collective-permute-start(f32[16,256]{1,0:T(8,128)S(1)} %reduce_sum.9), channel_id=1, source_target_pairs={{0,64},{32,96},{64,0},{96,32},{128,192},{160,224},{192,128},{224,1... | collective-permute-start | bytes 49160 | tf_op jit(solution)/shard_map/ppermute | solution.py:471
  61.0 10.4 %all-to-all-start.1 = ((f32[8,16,256]{2,1,0:T(8,128)}), f32[8,16,256]{2,1,0:T(8,128)S(1)}, u32[]{:S(2)}, u32[]{:S(2)}) async-start(f32[8,16,256]{2,1,0:T(8,128)} %broadcast_in_dim.2), calls=%async_computation.1 | async-start | bytes 262144 | tf_op jit(solution)/shard_map/all_to_all | solution.py:472

commit v4 on v3

--- a/solution.py
+++ b/solution.py
@@ -208,29 +208,31 @@
 
     for depth in range(2):
         height = ROWS - 2 * HALF * depth
+        strips = (strips0, strips1)[depth]
+
+        def hand_over(order, plane, strips=strips, height=height):
+            for step in range(STEPS):
+                strips[order, plane, step, :STRIP, :] = terms[order, plane, step, :STRIP, :]
+                strips[order, plane, step, STRIP:, :] = terms[order, plane, step, pl.ds(height - STRIP - 2 * order, STRIP), :]
+
         for first, last in ((0, 1), (1, 3), (3, 7), (7, 11), (11, 12)):
             count = -(-(height - 2 * (first + 1)) // 8)
             count += count == 8
 
-            def step_on(at, carry, first=first, count=count):
-                past, pair = lax.div(at, 2), lax.rem(at, 2)
-                for plane in range(2):
-                    advance(terms, past, 2 * pair + plane, 0, 1, count, mask, first == 0)
+            def step_on(past, carry, first=first, count=count, hand_over=hand_over):
+                for plane in range(4):
+                    hand_over(0 if first == 0 else past + 1, plane)
+                for plane in range(4):
+                    advance(terms, past, plane, 0, 1, count, mask, first == 0)
                 return carry
 
             start = max(first - 1, 0)
-            lax.fori_loop(2 * start, 2 * (start + last - first), step_on, 0)
-
-        strips = (strips0, strips1)[depth]
-
-        def hand_over(order, carry, strips=strips, height=height):
-            for plane in range(4):
-                for step in range(STEPS):
-                    strips[order, plane, step, :STRIP, :] = terms[order, plane, step, :STRIP, :]
-                    strips[order, plane, step, STRIP:, :] = terms[order, plane, step, pl.ds(height - STRIP - 2 * order, STRIP), :]
-            return carry
-
-        lax.fori_loop(0, orders, hand_over, 0)
+            if last - first == 1:
+                step_on(start, 0)
+            else:
+                lax.fori_loop(start, start + last - first, step_on, 0)
+        for plane in range(4):
+            hand_over(orders - 1, plane)
         first_row = HALF * (depth + 1)
         count = (ROWS - 2 * first_row) // 8
 
@@ -300,7 +302,9 @@
                 for step in range(STEPS):
                     upper[order, plane, step, HALO:, :] = strips[order, plane, step, :STRIP, :]
                     lower[order, plane, step, :STRIP, :] = strips[order, plane, step, STRIP:, :]
+            for plane in range(4):
                 advance(upper, past, plane, 0, 1, width, lambda step, r: inside_upper[r] * masks[step], first)
+            for plane in range(4):
                 advance(lower, past, plane, STRIP, -1, width, lambda step, r: inside_lower[r] * masks[step], first)
             return carry
 
@@ -465,17 +469,19 @@
     return source_out, receiver_out, image
 
 
-def add_over_freq(pieces):
+def add_over_freq(pieces, beside):
     groups = [[y * 4 + z * 2 + core for y in range(4) for core in range(2)] for z in range(2)]
     mine = jnp.sum(lax.all_to_all(pieces, "freq", 0, 0, axis_index_groups=groups), axis=0)
-    mine = mine + lax.ppermute(mine, "freq", [(i, i ^ 2) for i in range(16)])
+    other = lax.ppermute(mine, "freq", [(i, i ^ 2) for i in range(16)])
+    other, *beside = lax.optimization_barrier((other, *beside))
+    mine = mine + other
     blocks = lax.all_to_all(jnp.broadcast_to(mine[None], pieces.shape), "freq", 0, 0, axis_index_groups=groups)
-    return blocks.reshape(2, ROWS, COLS)
+    return *beside, blocks.reshape(2, ROWS, COLS)
 
 
 def local(source, receiver, table_index, coef_table):
     source_out, receiver_out, pieces = extrapolate(source, receiver, table_index, coef_table)
-    return source_out, receiver_out, add_over_freq(pieces)
+    return add_over_freq(pieces, (source_out, receiver_out))
 
 
 def solution(mesh):

time: 72.4 us -> 70 us (0.967)
  blocking collectives: 11.9 us -> 22.4 us
  starting transfers between devices: 29.7 us -> 24.5 us
  waiting for transfers between devices: 7.5 us -> 2.54 us
  Pallas kernels: 20.7 us -> 18.7 us
    all_to_all x0 -> x1, blocking collectives: none -> 9.13 us  [add_over_freq(): lax.all_to_all(jnp.broadcast_to(mine[None], pieces.shape), 'freq', 0, 0,...]
    all_to_all x1 -> x0, starting transfers between devices: 5.11 us -> none  [add_over_freq(): lax.all_to_all(jnp.broadcast_to(mine[None], pieces.shape), 'freq', 0, 0,...]
    all_to_all x1 -> x0, waiting for transfers between devices: 3.93 us -> none  [add_over_freq(): lax.all_to_all(jnp.broadcast_to(mine[None], pieces.shape), 'freq', 0, 0,...]
    pallas_call x1, Pallas kernels: 7.9 us -> 6.14 us  [extrapolate(): pl.pallas_call(inner_kernel, out_shape=(strip, strip, shape(2, STEPS, ROW...]
    all_to_all x1, blocking collectives: 11.9 us -> 13.3 us  [add_over_freq(): lax.all_to_all(pieces, 'freq', 0, 0, axis_index_groups=groups)]
    ppermute x1, waiting for transfers between devices: 1.11 us -> 0.01 us  [add_over_freq(): other = lax.ppermute(mine, 'freq', [(i, i ^ 2) for i in range(16)])]
  transfers between devices with their start and end apart: 6 -> 5, of which waited for: 3 -> 2; matrix products, arithmetic and copies ran while one was open for 0% -> 0% of each run, Pallas kernels for 15% -> 13%
where the time goes in v4:
time: 70 us; the launch traced here: 69.7 us
  starting transfers between devices  24.5 us (35%)
  blocking collectives  22.4 us (32%)
  Pallas kernels  18.7 us (27%)
  waiting for transfers between devices  2.54 us (4%)
  between operations  0.77 us (1%)
    ppermute x1, starting transfers between devices, add_over_freq(): other = lax.ppermute(mine, 'freq', [(i, i ^ 2) for i in range(16)])  14.4 us
    all_to_all x1, blocking collectives, add_over_freq(): lax.all_to_all(pieces, 'freq', 0, 0, axis_index_groups=groups)  13.3 us
    ppermute x4, starting transfers between devices, shift(): lax.ppermute(block, axis, pairs if forward else [(b, a) for a, b in pairs])  10.1 us
    all_to_all x1, blocking collectives, add_over_freq(): lax.all_to_all(jnp.broadcast_to(mine[None], pieces.shape), 'freq', 0, 0,...  9.13 us
    pallas_call x1, Pallas kernels, extrapolate(): pl.pallas_call(rim_kernel, out_shape=(shape(2, 4, STEPS, HALO, 128), shap...  7.92 us
    pallas_call x1, Pallas kernels, extrapolate(): pl.pallas_call(inner_kernel, out_shape=(strip, strip, shape(2, STEPS, ROW...  6.14 us
    ppermute x4, waiting for transfers between devices, shift(): lax.ppermute(block, axis, pairs if forward else [(b, a) for a, b in pairs])  2.54 us
    pallas_call x1, Pallas kernels, extrapolate(): pl.pallas_call(own_kernel, out_shape=(shape(4, STEPS, ROWS, 128), shape(2...  1.48 us
  transfers between devices with their start and end apart: 5, of which 2 were waited for; matrix products, arithmetic and copies ran while one was open for 0% of the time, Pallas kernels for 13%

profile of v4, /device:TPU:1, one launch (start us, length us, event | category | flops | bytes accessed | tf_op | source)
XLA Modules:
  0.0 69.7 jit_solution(14249237441292360919)
XLA Ops:
  0.6 1.4 %edges.1 = (f32[3,64,128]{2,1,0:T(8,128)S(1)}, f32[3,64,128]{2,1,0:T(8,128)S(1)}, f32[2,2,2,64,256]{4,3,2,1,0:T(8,128)S(1)}, s32[2,2,64,256]{3,2,1,0:T(8,128)S(1)}) custom-call(f32[2,2,64,256]{3,2,1,0:T(8,128)} %source.1, f32[2,2,64,256]{3,2,1,0:T(8,128)} %receiver.1, s32[2,2,64,256]{3,2,1,0:T(8,128)} %index.1), custom_call_target="tpu_custom_call" | custom-call | tf_op jit(solution)/shard_map/edges/pallas_call | solution.py:386
  2.0 4.0 %collective-permute-start = (f32[3,64,128]{2,1,0:T(8,128)S(1)}, f32[3,64,128]{2,1,0:T(8,128)S(1)}, u32[]{:S(2)}, u32[]{:S(2)}) collective-permute-start(f32[3,64,128]{2,1,0:T(8,128)S(1)} %get-tuple-element.29), channel_id=1, source_target_pairs={{0,1},{1,2},{2,3},{4,5},{5,6},{6,7},{8,9},{9,10},{10,11},{12,13},{... | collective-permute-start | bytes 294920 | tf_op jit(solution)/shard_map/ppermute | solution.py:374
  6.0 1.3 %collective-permute-start.1 = (f32[3,64,128]{2,1,0:T(8,128)S(1)}, f32[3,64,128]{2,1,0:T(8,128)S(1)}, u32[]{:S(2)}, u32[]{:S(2)}) collective-permute-start(f32[3,64,128]{2,1,0:T(8,128)S(1)} %get-tuple-element.30), channel_id=1, source_target_pairs={{1,0},{2,1},{3,2},{5,4},{6,5},{7,6},{9,8},{10,9},{11,10},{13,12},{... | collective-permute-start | bytes 294920 | tf_op jit(solution)/shard_map/ppermute | solution.py:374
  7.3 0.0 copy-start
  7.3 1.5 %own.1 = (f32[4,5,64,128]{3,2,1,0:T(8,128)S(1)}, f32[2,5,64,128]{3,2,1,0:T(8,128)S(1)}, bf16[640,640]{1,0:T(8,128)(2,1)S(1)}) custom-call(f32[2,2,2,64,256]{4,3,2,1,0:T(8,128)S(1)} %get-tuple-element.25.waves, s32[2,2,64,256]{3,2,1,0:T(8,128)S(1)} %get-tuple-element.26.index), custom_call_target="tpu_custom_call" | custom-call | flops 2000000000 | bytes 1048576 | tf_op jit(solution)/shard_map/own/pallas_call | solution.py:402
  8.8 0.1 add_convert_fusion.flags
  8.9 0.0 collective-permute-done.low
  8.9 2.4 %collective-permute-done.1.high = f32[3,64,128]{2,1,0:T(8,128)S(1)} collective-permute-done((f32[3,64,128]{2,1,0:T(8,128)S(1)}, f32[3,64,128]{2,1,0:T(8,128)S(1)}, u32[]{:S(2)}, u32[]{:S(2)}) %collective-permute-start.1) | collective-permute-done | bytes 98336 | tf_op jit(solution)/shard_map/ppermute | solution.py:374
  11.4 0.4 merge.1
  11.8 3.6 %collective-permute-start.2 = (f32[560,128]{1,0:T(8,128)S(1)}, f32[560,128]{1,0:T(8,128)S(1)}, u32[]{:S(2)}, u32[]{:S(2)}) collective-permute-start(f32[560,128]{1,0:T(8,128)S(1)} %get-tuple-element.34), channel_id=1, source_target_pairs={{0,4},{4,8},{8,12},{12,16},{16,20},{20,24},{24,28},{1,5},{5,9},{9,... | collective-permute-start | bytes 860168 | tf_op jit(solution)/shard_map/ppermute | solution.py:374
  15.4 1.3 %collective-permute-start.3 = (f32[560,128]{1,0:T(8,128)S(1)}, f32[560,128]{1,0:T(8,128)S(1)}, u32[]{:S(2)}, u32[]{:S(2)}) collective-permute-start(f32[560,128]{1,0:T(8,128)S(1)} %get-tuple-element.35), channel_id=1, source_target_pairs={{4,0},{8,4},{12,8},{16,12},{20,16},{24,20},{28,24},{5,1},{9,5},{13... | collective-permute-start | bytes 860168 | tf_op jit(solution)/shard_map/ppermute | solution.py:374
  16.7 0.0 copy-done
  16.7 6.1 %inner.1 = (f32[13,4,5,32,128]{4,3,2,1,0:T(8,128)S(1)}, f32[13,4,5,32,128]{4,3,2,1,0:T(8,128)S(1)}, f32[2,5,64,128]{3,2,1,0:T(8,128)S(1)}, f32[4,5,16,128]{3,2,1,0:T(8,128)S(1)}) custom-call(f32[4]{0:T(128)S(1)} %add_convert_fusion.flags, f32[4,5,64,128]{3,2,1,0:T(8,128)S(1)} %get-tuple-element.32.fields, f32[5,64,128]{2,1,0:T(8,128)S(1)} %get-tuple-element.33.indices0, ...), custom_call_target="tpu_custom_call" | custom-call | flops 10000000000 | bytes 1048576 | tf_op jit(solution)/shard_map/inner/pallas_call | solution.py:426
  22.8 0.0 collective-permute-done.2.above
  22.8 0.1 collective-permute-done.3.below
  22.9 7.9 %rim.1 = (f32[2,4,5,24,128]{4,3,2,1,0:T(8,128)S(1)}, f32[8,16,256]{2,1,0:T(8,128)S(1)}) custom-call(f32[4]{0:T(128)S(1)} %add_convert_fusion.flags, f32[4,5,64,128]{3,2,1,0:T(8,128)S(1)} %get-tuple-element.32.fields, f32[5,64,128]{2,1,0:T(8,128)S(1)} %get-tuple-element.33.indices0, f32[5,64,128]{2,1,0:T(8,128)S(1)} %slice_bitcast_fusion.indices1, ...), custom_call_target="tpu_custom_call" | custom-call | tf_op jit(solution)/shard_map/rim/pallas_call | solution.py:442
  30.9 13.3 %all_to_all.10 = f32[8,16,256]{2,1,0:T(8,128)S(1)} all-to-all(f32[8,16,256]{2,1,0:T(8,128)S(1)} %get-tuple-element.39), channel_id=1, replica_groups={{0,32,128,160,256,288,384,416},{64,96,192,224,320,352,448,480},{1,33,12..., dimensions={0} | all-to-all | bytes 262144 | tf_op jit(solution)/shard_map/all_to_all | solution.py:474
  44.2 14.4 %collective-permute-start.4 = (f32[16,256]{1,0:T(8,128)S(1)}, f32[16,256]{1,0:T(8,128)S(1)}, u32[]{:S(2)}, u32[]{:S(2)}) collective-permute-start(f32[16,256]{1,0:T(8,128)S(1)} %reduce_sum.9), channel_id=1, source_target_pairs={{0,64},{32,96},{64,0},{96,32},{128,192},{160,224},{192,128},{224,1... | collective-permute-start | bytes 49160 | tf_op jit(solution)/shard_map/ppermute | solution.py:475
  58.5 1.4 %finish.1 = (f32[2,2,64,256]{3,2,1,0:T(8,128)}, f32[2,2,64,256]{3,2,1,0:T(8,128)}) custom-call(f32[2,4,5,24,128]{4,3,2,1,0:T(8,128)S(1)} %get-tuple-element.40.fresh, f32[4,5,16,128]{3,2,1,0:T(8,128)S(1)} %get-tuple-element.41.centre, bf16[640,640]{1,0:T(8,128)(2,1)S(1)} %get-tuple-element.31.spread), custom_call_target="tpu_custom_call" | custom-call | flops 2000000000 | bytes 1048576 | tf_op jit(solution)/shard_map/finish/pallas_call | solution.py:459
  59.9 0.0 collective-permute-done.4
  59.9 9.1 %all_to_all.11 = f32[8,16,256]{2,1,0:T(8,128)S(1)} all-to-all(f32[8,16,256]{2,1,0:T(8,128)S(1)} %broadcast_in_dim.2), channel_id=1, replica_groups={{0,32,128,160,256,288,384,416},{64,96,192,224,320,352,448,480},{1,33,12..., dimensions={0} | all-to-all | bytes 262144 | tf_op jit(solution)/shard_map/all_to_all | solution.py:478
  69.1 0.7 copy.8
  (4 shorter events, 0.0 us)
Async XLA Ops:
  2.0 6.9 %collective-permute-start = (f32[3,64,128]{2,1,0:T(8,128)S(1)}, f32[3,64,128]{2,1,0:T(8,128)S(1)}, u32[]{:S(2)}, u32[]{:S(2)}) collective-permute-start(f32[3,64,128]{2,1,0:T(8,128)S(1)} %get-tuple-element.29), channel_id=1, source_target_pairs={{0,1},{1,2},{2,3},{4,5},{5,6},{6,7},{8,9},{9,10},{10,11},{12,13},{... | collective-permute-start | bytes 294920 | tf_op jit(solution)/shard_map/ppermute | solution.py:374
  6.0 5.4 %collective-permute-start.1 = (f32[3,64,128]{2,1,0:T(8,128)S(1)}, f32[3,64,128]{2,1,0:T(8,128)S(1)}, u32[]{:S(2)}, u32[]{:S(2)}) collective-permute-start(f32[3,64,128]{2,1,0:T(8,128)S(1)} %get-tuple-element.30), channel_id=1, source_target_pairs={{1,0},{2,1},{3,2},{5,4},{6,5},{7,6},{9,8},{10,9},{11,10},{13,12},{... | collective-permute-start | bytes 294920 | tf_op jit(solution)/shard_map/ppermute | solution.py:374
  7.3 9.4 %copy-start = (f32[2,32,13]{1,0,2:T(2,128)S(1)}, f32[2,32,13]{1,0,2:T(2,128)}, u32[]{:S(2)}) copy-start(f32[2,32,13]{1,0,2:T(2,128)} %param.7) | copy-start | bytes 9988
  11.8 11.0 %collective-permute-start.2 = (f32[560,128]{1,0:T(8,128)S(1)}, f32[560,128]{1,0:T(8,128)S(1)}, u32[]{:S(2)}, u32[]{:S(2)}) collective-permute-start(f32[560,128]{1,0:T(8,128)S(1)} %get-tuple-element.34), channel_id=1, source_target_pairs={{0,4},{4,8},{8,12},{12,16},{16,20},{20,24},{24,28},{1,5},{5,9},{9,... | collective-permute-start | bytes 860168 | tf_op jit(solution)/shard_map/ppermute | solution.py:374
  15.4 7.6 %collective-permute-start.3 = (f32[560,128]{1,0:T(8,128)S(1)}, f32[560,128]{1,0:T(8,128)S(1)}, u32[]{:S(2)}, u32[]{:S(2)}) collective-permute-start(f32[560,128]{1,0:T(8,128)S(1)} %get-tuple-element.35), channel_id=1, source_target_pairs={{4,0},{8,4},{12,8},{16,12},{20,16},{24,20},{28,24},{5,1},{9,5},{13... | collective-permute-start | bytes 860168 | tf_op jit(solution)/shard_map/ppermute | solution.py:374
  44.2 15.8 %collective-permute-start.4 = (f32[16,256]{1,0:T(8,128)S(1)}, f32[16,256]{1,0:T(8,128)S(1)}, u32[]{:S(2)}, u32[]{:S(2)}) collective-permute-start(f32[16,256]{1,0:T(8,128)S(1)} %reduce_sum.9), channel_id=1, source_target_pairs={{0,64},{32,96},{64,0},{96,32},{128,192},{160,224},{192,128},{224,1... | collective-permute-start | bytes 49160 | tf_op jit(solution)/shard_map/ppermute | solution.py:475

commit v5 on v4

--- a/solution.py
+++ b/solution.py
@@ -186,7 +186,7 @@
 
 def column_mask(shape, step, flags):
     column = (lax.broadcasted_iota(jnp.int32, shape, 1) % 64) * STEPS + step
-    return 0.25 * jnp.where(column < SIDE, flags[2], jnp.where(column >= SIDE + COLS, flags[3], 1.0))
+    return 0.25 * jnp.where(column < SIDE, flags[2:3, :], jnp.where(column >= SIDE + COLS, flags[3:4, :], 1.0))
 
 
 def inner_kernel(
@@ -257,8 +257,8 @@
 
 
 def rim_kernel(
-    flags, fields, indices0, indices1, above, below, strips0, strips1, inner_picture, table, spread, fresh, image,
-    upper, lower, masks, places, picture, result, lookup,
+    flags, fields, indices0, indices1, above, below, strips0, strips1, inner_picture, centre, table, spread,
+    fresh, image, source_out, receiver_out, upper, lower, masks, places, picture, result, lookup, whole, natural, sems,
 ):
     orders = upper.shape[0]
     fill(lookup, table)
@@ -296,8 +296,8 @@
         def step_on(past, carry, first, depth=depth, strips=strips):
             order = 1 if first else past + 2
             shift = order - HALO + HALF * depth
-            inside_upper = [jnp.where(sublane + (r + shift) >= 0, 1.0, flags[0]) for r in range(width)]
-            inside_lower = [jnp.where(sublane + (r - HALO - shift) < 0, 1.0, flags[1]) for r in range(width)]
+            inside_upper = [jnp.where(sublane + (r + shift) >= 0, 1.0, flags[0:1, :]) for r in range(width)]
+            inside_lower = [jnp.where(sublane + (r - HALO - shift) < 0, 1.0, flags[1:2, :]) for r in range(width)]
             for plane in range(4):
                 for step in range(STEPS):
                     upper[order, plane, step, HALO:, :] = strips[order, plane, step, :STRIP, :]
@@ -338,18 +338,36 @@
         image[part] = total[part * BLOCK : (part + 1) * BLOCK]
 
 
-def finish_kernel(fresh, centre, spread, source_out, receiver_out, result):
+    @pl.when(flags[4, 0] > 0.5)
+    def _():
+        to_natural(fresh, centre, spread, source_out, receiver_out, whole, natural, sems)
+
+
+def to_natural(fresh, centre, spread, source_out, receiver_out, whole, natural, sems):
     for plane in range(4):
         for step in range(STEPS):
             rows, cut = plane * ROWS, slice(step * 128, (step + 1) * 128)
-            result[rows : rows + HALO, cut] = fresh[0, plane, step]
-            result[rows + HALO : rows + ROWS - HALO, cut] = centre[plane, step]
-            result[rows + ROWS - HALO : rows + ROWS, cut] = fresh[1, plane, step]
-    values = move(result[...], spread[: 2 * COLS, :], ((1,), (1,)))
+            whole[rows : rows + HALO, cut] = fresh[0, plane, step]
+            whole[rows + HALO : rows + ROWS - HALO, cut] = centre[plane, step]
+            whole[rows + ROWS - HALO : rows + ROWS, cut] = fresh[1, plane, step]
+    values = move(whole[...], spread[: 2 * COLS, :], ((1,), (1,)))
     for plane in range(4):
         for wave in range(2):
             piece = values[plane * ROWS : (plane + 1) * ROWS, wave * COLS : (wave + 1) * COLS]
-            (source_out, receiver_out)[plane // 2][plane % 2, wave] = piece
+            natural[plane // 2, plane % 2, wave] = piece
+    copies = [pltpu.make_async_copy(natural.at[kind], out, sems.at[kind]) for kind, out in enumerate((source_out, receiver_out))]
+    for copy in copies:
+        copy.start()
+    for copy in copies:
+        copy.wait()
+
+
+def finish_kernel(flags, fresh, centre, spread, source_in, receiver_in, source_out, receiver_out, whole, natural, sems):
+    del source_in, receiver_in
+
+    @pl.when(flags[4, 0] < 0.5)
+    def _():
+        to_natural(fresh, centre, spread, source_out, receiver_out, whole, natural, sems)
 
 
 def full(count):
@@ -377,11 +395,13 @@
 def extrapolate(source, receiver, table_index, coef_table):
     orders = coef_table.shape[2]
     at_x, at_y = lax.axis_index("sx"), lax.axis_index("sy")
-    flags = jnp.stack(
-        [at_x > 0, at_x < lax.axis_size("sx") - 1, at_y > 0, at_y < lax.axis_size("sy") - 1]
-    ).astype(jnp.float32)
+    early = (lax.axis_index("freq") // 2) % 2 == 0
+    row = lax.broadcasted_iota(jnp.int32, (8, 128), 0)
+    flags = jnp.zeros((8, 128), jnp.float32)
+    tests = [at_x > 0, at_x < lax.axis_size("sx") - 1, at_y > 0, at_y < lax.axis_size("sy") - 1, early]
+    for place, test in enumerate(tests):
+        flags = jnp.where((row == place) & test, 1.0, flags)
     table = jnp.transpose(coef_table, (2, 0, 1))
-    scalars = [pl.BlockSpec(memory_space=pltpu.SMEM)]
 
     left, right, waves, places = pl.pallas_call(
         edges_kernel,
@@ -426,7 +446,7 @@
     strips0, strips1, picture, centre = pl.pallas_call(
         inner_kernel,
         out_shape=(strip, strip, shape(2, STEPS, ROWS, 128), shape(4, STEPS, ROWS - 2 * HALO, 128)),
-        in_specs=scalars + full(4),
+        in_specs=full(5),
         out_specs=tuple(full(4)),
         scratch_shapes=[
             pltpu.VMEM((orders, 4, STEPS, ROWS + 16, 128), jnp.float32),
@@ -439,11 +459,22 @@
         cost_estimate=cost(10**10),
         name="inner",
     )(flags, fields, indices0, indices1, table)
-    fresh, image = pl.pallas_call(
+    back = [
+        pltpu.VMEM((4 * ROWS, WIDE), jnp.float32),
+        pltpu.VMEM((2, 2, 2, ROWS, COLS), jnp.float32),
+        pltpu.SemaphoreType.DMA((2,)),
+    ]
+    hbm = [pl.BlockSpec(memory_space=pltpu.HBM)] * 2
+    fresh, image, source_out, receiver_out = pl.pallas_call(
         rim_kernel,
-        out_shape=(shape(2, 4, STEPS, HALO, 128), shape(8, BLOCK, COLS)),
-        in_specs=scalars + full(10),
-        out_specs=tuple(full(2)),
+        out_shape=(
+            shape(2, 4, STEPS, HALO, 128),
+            shape(8, BLOCK, COLS),
+            shape(2, 2, ROWS, COLS),
+            shape(2, 2, ROWS, COLS),
+        ),
+        in_specs=full(12),
+        out_specs=tuple(full(2) + hbm),
         scratch_shapes=[
             pltpu.VMEM((orders, 4, STEPS, HALO + STRIP, 128), jnp.float32),
             pltpu.VMEM((orders, 4, STEPS, HALO + STRIP, 128), jnp.float32),
@@ -452,20 +483,22 @@
             pltpu.VMEM((2, STEPS, TALL, 128), jnp.float32),
             pltpu.VMEM((2 * ROWS, WIDE), jnp.float32),
             lookup,
+            *back,
         ],
         compiler_params=params(32),
         name="rim",
-    )(flags, fields, indices0, indices1, above, below, strips0, strips1, picture, table, spread)
+    )(flags, fields, indices0, indices1, above, below, strips0, strips1, picture, centre, table, spread)
     source_out, receiver_out = pl.pallas_call(
         finish_kernel,
         out_shape=(shape(2, 2, ROWS, COLS), shape(2, 2, ROWS, COLS)),
-        in_specs=full(3),
-        out_specs=tuple(full(2)),
-        scratch_shapes=[pltpu.VMEM((4 * ROWS, WIDE), jnp.float32)],
+        in_specs=full(4) + hbm,
+        out_specs=tuple(hbm),
+        scratch_shapes=back,
+        input_output_aliases={4: 0, 5: 1},
         compiler_params=params(16),
         cost_estimate=cost(2 * 10**9),
         name="finish",
-    )(fresh, centre, spread)
+    )(flags, fresh, centre, spread, source_out, receiver_out)
     return source_out, receiver_out, image
 
 

time: 70 us -> 70.5 us (level); the launches traced: 69.7 us -> 69.3 us
  waiting for transfers between devices: 2.54 us -> 4.05 us
  starting transfers between devices: 24.5 us -> 23.1 us
  Pallas kernels: 18.7 us -> 17.8 us
    ppermute x1, starting transfers between devices: 14.4 us -> 13 us  [add_over_freq(): other = lax.ppermute(mine, 'freq', [(i, i ^ 2) for i in range(16)])]
    pallas_call x1, Pallas kernels: 1.37 us -> 0.06 us  [extrapolate(): pl.pallas_call(finish_kernel, out_shape=(shape(2, 2, ROWS, COLS), shape(2...]
    ppermute x1, waiting for transfers between devices: 0.01 us -> 1.04 us  [add_over_freq(): other = lax.ppermute(mine, 'freq', [(i, i ^ 2) for i in range(16)])]
    pallas_call x1, Pallas kernels: 7.92 us -> 8.85 us  [extrapolate(): pl.pallas_call(rim_kernel, out_shape=(shape(2, 4, STEPS, HALO, 128), shap...]
  transfers between devices with their start and end apart: 5 -> 5, of which waited for: 2 -> 3; matrix products, arithmetic and copies ran while one was open for 0% -> 0% of each run, Pallas kernels for 13% -> 10%
where the time goes in v5:
time: 70.5 us; the launch traced here: 69.3 us
  starting transfers between devices  23.1 us (33%)
  blocking collectives  22.7 us (32%)
  Pallas kernels  17.8 us (25%)
  waiting for transfers between devices  4.05 us (6%)
  between operations  0.82 us (1%)
    all_to_all x1, blocking collectives, add_over_freq(): lax.all_to_all(pieces, 'freq', 0, 0, axis_index_groups=groups)  13.3 us
    ppermute x1, starting transfers between devices, add_over_freq(): other = lax.ppermute(mine, 'freq', [(i, i ^ 2) for i in range(16)])  13 us
    ppermute x4, starting transfers between devices, shift(): lax.ppermute(block, axis, pairs if forward else [(b, a) for a, b in pairs])  10.1 us
    all_to_all x1, blocking collectives, add_over_freq(): lax.all_to_all(jnp.broadcast_to(mine[None], pieces.shape), 'freq', 0, 0,...  9.44 us
    pallas_call x1, Pallas kernels, extrapolate(): pl.pallas_call(rim_kernel, out_shape=(shape(2, 4, STEPS, HALO, 128), shap...  8.85 us
    pallas_call x1, Pallas kernels, extrapolate(): pl.pallas_call(inner_kernel, out_shape=(strip, strip, shape(2, STEPS, ROW...  5.6 us
    ppermute x4, waiting for transfers between devices, shift(): lax.ppermute(block, axis, pairs if forward else [(b, a) for a, b in pairs])  3.01 us
    pallas_call x1, Pallas kernels, extrapolate(): pl.pallas_call(own_kernel, out_shape=(shape(4, STEPS, ROWS, 128), shape(2...  1.47 us
  transfers between devices with their start and end apart: 5, of which 3 were waited for; matrix products, arithmetic and copies ran while one was open for 0% of the time, Pallas kernels for 10%

profile of v5, /device:TPU:1, one launch (start us, length us, event | category | flops | bytes accessed | tf_op | source)
XLA Modules:
  0.0 69.3 jit_solution(319433409537833162)
XLA Ops:
  0.6 1.4 %edges.1 = (f32[3,64,128]{2,1,0:T(8,128)S(1)}, f32[3,64,128]{2,1,0:T(8,128)S(1)}, f32[2,2,2,64,256]{4,3,2,1,0:T(8,128)S(1)}, s32[2,2,64,256]{3,2,1,0:T(8,128)S(1)}) custom-call(f32[2,2,64,256]{3,2,1,0:T(8,128)} %source.1, f32[2,2,64,256]{3,2,1,0:T(8,128)} %receiver.1, s32[2,2,64,256]{3,2,1,0:T(8,128)} %index.1), custom_call_target="tpu_custom_call" | custom-call | tf_op jit(solution)/shard_map/edges/pallas_call | solution.py:406
  2.0 4.0 %collective-permute-start = (f32[3,64,128]{2,1,0:T(8,128)S(1)}, f32[3,64,128]{2,1,0:T(8,128)S(1)}, u32[]{:S(2)}, u32[]{:S(2)}) collective-permute-start(f32[3,64,128]{2,1,0:T(8,128)S(1)} %get-tuple-element.31), channel_id=1, source_target_pairs={{0,1},{1,2},{2,3},{4,5},{5,6},{6,7},{8,9},{9,10},{10,11},{12,13},{... | collective-permute-start | bytes 294920 | tf_op jit(solution)/shard_map/ppermute | solution.py:392
  6.0 1.3 %collective-permute-start.1 = (f32[3,64,128]{2,1,0:T(8,128)S(1)}, f32[3,64,128]{2,1,0:T(8,128)S(1)}, u32[]{:S(2)}, u32[]{:S(2)}) collective-permute-start(f32[3,64,128]{2,1,0:T(8,128)S(1)} %get-tuple-element.32), channel_id=1, source_target_pairs={{1,0},{2,1},{3,2},{5,4},{6,5},{7,6},{9,8},{10,9},{11,10},{13,12},{... | collective-permute-start | bytes 294920 | tf_op jit(solution)/shard_map/ppermute | solution.py:392
  7.4 0.0 copy-start
  7.4 1.5 %own.1 = (f32[4,5,64,128]{3,2,1,0:T(8,128)S(1)}, f32[2,5,64,128]{3,2,1,0:T(8,128)S(1)}, bf16[640,640]{1,0:T(8,128)(2,1)S(1)}) custom-call(f32[2,2,2,64,256]{4,3,2,1,0:T(8,128)S(1)} %get-tuple-element.27.waves, s32[2,2,64,256]{3,2,1,0:T(8,128)S(1)} %get-tuple-element.28.index), custom_call_target="tpu_custom_call" | custom-call | flops 2000000000 | bytes 1048576 | tf_op jit(solution)/shard_map/own/pallas_call | solution.py:422
  8.9 0.1 select_select_fusion.flags
  9.0 0.0 collective-permute-done.low
  9.0 2.4 %collective-permute-done.1.high = f32[3,64,128]{2,1,0:T(8,128)S(1)} collective-permute-done((f32[3,64,128]{2,1,0:T(8,128)S(1)}, f32[3,64,128]{2,1,0:T(8,128)S(1)}, u32[]{:S(2)}, u32[]{:S(2)}) %collective-permute-start.1) | collective-permute-done | bytes 98336 | tf_op jit(solution)/shard_map/ppermute | solution.py:392
  11.4 0.4 merge.1
  11.8 3.6 %collective-permute-start.2 = (f32[560,128]{1,0:T(8,128)S(1)}, f32[560,128]{1,0:T(8,128)S(1)}, u32[]{:S(2)}, u32[]{:S(2)}) collective-permute-start(f32[560,128]{1,0:T(8,128)S(1)} %get-tuple-element.36), channel_id=1, source_target_pairs={{0,4},{4,8},{8,12},{12,16},{16,20},{20,24},{24,28},{1,5},{5,9},{9,... | collective-permute-start | bytes 860168 | tf_op jit(solution)/shard_map/ppermute | solution.py:392
  15.4 1.3 %collective-permute-start.3 = (f32[560,128]{1,0:T(8,128)S(1)}, f32[560,128]{1,0:T(8,128)S(1)}, u32[]{:S(2)}, u32[]{:S(2)}) collective-permute-start(f32[560,128]{1,0:T(8,128)S(1)} %get-tuple-element.37), channel_id=1, source_target_pairs={{4,0},{8,4},{12,8},{16,12},{20,16},{24,20},{28,24},{5,1},{9,5},{13... | collective-permute-start | bytes 860168 | tf_op jit(solution)/shard_map/ppermute | solution.py:392
  16.7 0.0 copy-done
  16.7 5.6 %inner.1 = (f32[13,4,5,32,128]{4,3,2,1,0:T(8,128)S(1)}, f32[13,4,5,32,128]{4,3,2,1,0:T(8,128)S(1)}, f32[2,5,64,128]{3,2,1,0:T(8,128)S(1)}, f32[4,5,16,128]{3,2,1,0:T(8,128)S(1)}) custom-call(f32[8,128]{1,0:T(8,128)S(1)} %select_select_fusion.flags, f32[4,5,64,128]{3,2,1,0:T(8,128)S(1)} %get-tuple-element.34.fields, ...), custom_call_target="tpu_custom_call" | custom-call | flops 10000000000 | bytes 1048576 | tf_op jit(solution)/shard_map/inner/pallas_call | solution.py:446
  22.3 0.0 collective-permute-done.2.above
  22.3 0.6 collective-permute-done.3.below
  22.9 8.8 %rim.1 = (f32[2,4,5,24,128]{4,3,2,1,0:T(8,128)S(1)}, f32[8,16,256]{2,1,0:T(8,128)S(1)}, f32[2,2,64,256]{3,2,1,0:T(8,128)}, f32[2,2,64,256]{3,2,1,0:T(8,128)}) custom-call(f32[8,128]{1,0:T(8,128)S(1)} %select_select_fusion.flags, f32[4,5,64,128]{3,2,1,0:T(8,128)S(1)} %get-tuple-element.34.fields, f32[5,64,128]{2,1,0:T(8,128)S(1)} %get-tuple-element.35.indices0, ...), custom_call_target="tpu_custom_call" | custom-call | tf_op jit(solution)/shard_map/rim/pallas_call | solution.py:468
  31.8 13.3 %all_to_all.10 = f32[8,16,256]{2,1,0:T(8,128)S(1)} all-to-all(f32[8,16,256]{2,1,0:T(8,128)S(1)} %get-tuple-element.42), channel_id=1, replica_groups={{0,32,128,160,256,288,384,416},{64,96,192,224,320,352,448,480},{1,33,12..., dimensions={0} | all-to-all | bytes 262144 | tf_op jit(solution)/shard_map/all_to_all | solution.py:507
  45.1 13.0 %collective-permute-start.4 = (f32[16,256]{1,0:T(8,128)S(1)}, f32[16,256]{1,0:T(8,128)S(1)}, u32[]{:S(2)}, u32[]{:S(2)}) collective-permute-start(f32[16,256]{1,0:T(8,128)S(1)} %reduce_sum.9), channel_id=1, source_target_pairs={{0,64},{32,96},{64,0},{96,32},{128,192},{160,224},{192,128},{224,1... | collective-permute-start | bytes 49160 | tf_op jit(solution)/shard_map/ppermute | solution.py:508
  58.1 0.1 finish.1
  58.1 1.0 %collective-permute-done.4 = f32[16,256]{1,0:T(8,128)S(1)} collective-permute-done((f32[16,256]{1,0:T(8,128)S(1)}, f32[16,256]{1,0:T(8,128)S(1)}, u32[]{:S(2)}, u32[]{:S(2)}) %collective-permute-start.4) | collective-permute-done | bytes 16416 | tf_op jit(solution)/shard_map/ppermute | solution.py:508
  59.2 9.4 %all_to_all.11 = f32[8,16,256]{2,1,0:T(8,128)S(1)} all-to-all(f32[8,16,256]{2,1,0:T(8,128)S(1)} %broadcast_in_dim.22), channel_id=1, replica_groups={{0,32,128,160,256,288,384,416},{64,96,192,224,320,352,448,480},{1,33,12..., dimensions={0} | all-to-all | bytes 262144 | tf_op jit(solution)/shard_map/all_to_all | solution.py:511
  68.6 0.7 copy.12
  (7 shorter events, 0.1 us)
Async XLA Ops:
  2.0 6.9 %collective-permute-start = (f32[3,64,128]{2,1,0:T(8,128)S(1)}, f32[3,64,128]{2,1,0:T(8,128)S(1)}, u32[]{:S(2)}, u32[]{:S(2)}) collective-permute-start(f32[3,64,128]{2,1,0:T(8,128)S(1)} %get-tuple-element.31), channel_id=1, source_target_pairs={{0,1},{1,2},{2,3},{4,5},{5,6},{6,7},{8,9},{9,10},{10,11},{12,13},{... | collective-permute-start | bytes 294920 | tf_op jit(solution)/shard_map/ppermute | solution.py:392
  6.0 5.4 %collective-permute-start.1 = (f32[3,64,128]{2,1,0:T(8,128)S(1)}, f32[3,64,128]{2,1,0:T(8,128)S(1)}, u32[]{:S(2)}, u32[]{:S(2)}) collective-permute-start(f32[3,64,128]{2,1,0:T(8,128)S(1)} %get-tuple-element.32), channel_id=1, source_target_pairs={{1,0},{2,1},{3,2},{5,4},{6,5},{7,6},{9,8},{10,9},{11,10},{13,12},{... | collective-permute-start | bytes 294920 | tf_op jit(solution)/shard_map/ppermute | solution.py:392
  7.4 9.3 %copy-start = (f32[2,32,13]{1,0,2:T(2,128)S(1)}, f32[2,32,13]{1,0,2:T(2,128)}, u32[]{:S(2)}) copy-start(f32[2,32,13]{1,0,2:T(2,128)} %param.7) | copy-start | bytes 9988
  11.8 10.5 %collective-permute-start.2 = (f32[560,128]{1,0:T(8,128)S(1)}, f32[560,128]{1,0:T(8,128)S(1)}, u32[]{:S(2)}, u32[]{:S(2)}) collective-permute-start(f32[560,128]{1,0:T(8,128)S(1)} %get-tuple-element.36), channel_id=1, source_target_pairs={{0,4},{4,8},{8,12},{12,16},{16,20},{20,24},{24,28},{1,5},{5,9},{9,... | collective-permute-start | bytes 860168 | tf_op jit(solution)/shard_map/ppermute | solution.py:392
  15.4 7.6 %collective-permute-start.3 = (f32[560,128]{1,0:T(8,128)S(1)}, f32[560,128]{1,0:T(8,128)S(1)}, u32[]{:S(2)}, u32[]{:S(2)}) collective-permute-start(f32[560,128]{1,0:T(8,128)S(1)} %get-tuple-element.37), channel_id=1, source_target_pairs={{4,0},{8,4},{12,8},{16,12},{20,16},{24,20},{28,24},{5,1},{9,5},{13... | collective-permute-start | bytes 860168 | tf_op jit(solution)/shard_map/ppermute | solution.py:392
  45.1 14.1 %collective-permute-start.4 = (f32[16,256]{1,0:T(8,128)S(1)}, f32[16,256]{1,0:T(8,128)S(1)}, u32[]{:S(2)}, u32[]{:S(2)}) collective-permute-start(f32[16,256]{1,0:T(8,128)S(1)} %reduce_sum.9), channel_id=1, source_target_pairs={{0,64},{32,96},{64,0},{96,32},{128,192},{160,224},{192,128},{224,1... | collective-permute-start | bytes 49160 | tf_op jit(solution)/shard_map/ppermute | solution.py:508

commit v6 on v4

--- a/solution.py
+++ b/solution.py
@@ -186,7 +186,7 @@
 
 def column_mask(shape, step, flags):
     column = (lax.broadcasted_iota(jnp.int32, shape, 1) % 64) * STEPS + step
-    return 0.25 * jnp.where(column < SIDE, flags[2], jnp.where(column >= SIDE + COLS, flags[3], 1.0))
+    return 0.25 * jnp.where(column < SIDE, flags[2:3, :], jnp.where(column >= SIDE + COLS, flags[3:4, :], 1.0))
 
 
 def inner_kernel(
@@ -296,8 +296,8 @@
         def step_on(past, carry, first, depth=depth, strips=strips):
             order = 1 if first else past + 2
             shift = order - HALO + HALF * depth
-            inside_upper = [jnp.where(sublane + (r + shift) >= 0, 1.0, flags[0]) for r in range(width)]
-            inside_lower = [jnp.where(sublane + (r - HALO - shift) < 0, 1.0, flags[1]) for r in range(width)]
+            inside_upper = [jnp.where(sublane + (r + shift) >= 0, 1.0, flags[0:1, :]) for r in range(width)]
+            inside_lower = [jnp.where(sublane + (r - HALO - shift) < 0, 1.0, flags[1:2, :]) for r in range(width)]
             for plane in range(4):
                 for step in range(STEPS):
                     upper[order, plane, step, HALO:, :] = strips[order, plane, step, :STRIP, :]
@@ -377,11 +377,12 @@
 def extrapolate(source, receiver, table_index, coef_table):
     orders = coef_table.shape[2]
     at_x, at_y = lax.axis_index("sx"), lax.axis_index("sy")
-    flags = jnp.stack(
-        [at_x > 0, at_x < lax.axis_size("sx") - 1, at_y > 0, at_y < lax.axis_size("sy") - 1]
-    ).astype(jnp.float32)
+    row = lax.broadcasted_iota(jnp.int32, (8, 128), 0)
+    flags = jnp.zeros((8, 128), jnp.float32)
+    tests = [at_x > 0, at_x < lax.axis_size("sx") - 1, at_y > 0, at_y < lax.axis_size("sy") - 1]
+    for place, test in enumerate(tests):
+        flags = jnp.where((row == place) & test, 1.0, flags)
     table = jnp.transpose(coef_table, (2, 0, 1))
-    scalars = [pl.BlockSpec(memory_space=pltpu.SMEM)]
 
     left, right, waves, places = pl.pallas_call(
         edges_kernel,
@@ -426,7 +427,7 @@
     strips0, strips1, picture, centre = pl.pallas_call(
         inner_kernel,
         out_shape=(strip, strip, shape(2, STEPS, ROWS, 128), shape(4, STEPS, ROWS - 2 * HALO, 128)),
-        in_specs=scalars + full(4),
+        in_specs=full(5),
         out_specs=tuple(full(4)),
         scratch_shapes=[
             pltpu.VMEM((orders, 4, STEPS, ROWS + 16, 128), jnp.float32),
@@ -442,7 +443,7 @@
     fresh, image = pl.pallas_call(
         rim_kernel,
         out_shape=(shape(2, 4, STEPS, HALO, 128), shape(8, BLOCK, COLS)),
-        in_specs=scalars + full(10),
+        in_specs=full(11),
         out_specs=tuple(full(2)),
         scratch_shapes=[
             pltpu.VMEM((orders, 4, STEPS, HALO + STRIP, 128), jnp.float32),

time: 70 us -> 69.5 us (level)
  Pallas kernels: 18.7 us -> 17.7 us
  transfers between devices with their start and end apart: 5 -> 5, of which waited for: 2 -> 2; matrix products, arithmetic and copies ran while one was open for 0% -> 0% of each run, Pallas kernels for 13% -> 12%
where the time goes in v6:
time: 69.5 us; the launch traced here: 69.2 us
  starting transfers between devices  24.5 us (35%)
  blocking collectives  22.4 us (32%)
  Pallas kernels  17.7 us (25%)
  waiting for transfers between devices  3.04 us (4%)
  between operations  0.79 us (1%)
    ppermute x1, starting transfers between devices, add_over_freq(): other = lax.ppermute(mine, 'freq', [(i, i ^ 2) for i in range(16)])  14.4 us
    all_to_all x1, blocking collectives, add_over_freq(): lax.all_to_all(pieces, 'freq', 0, 0, axis_index_groups=groups)  13.3 us
    ppermute x4, starting transfers between devices, shift(): lax.ppermute(block, axis, pairs if forward else [(b, a) for a, b in pairs])  10.1 us
    all_to_all x1, blocking collectives, add_over_freq(): lax.all_to_all(jnp.broadcast_to(mine[None], pieces.shape), 'freq', 0, 0,...  9.13 us
    pallas_call x1, Pallas kernels, extrapolate(): pl.pallas_call(rim_kernel, out_shape=(shape(2, 4, STEPS, HALO, 128), shap...  7.42 us
    pallas_call x1, Pallas kernels, extrapolate(): pl.pallas_call(inner_kernel, out_shape=(strip, strip, shape(2, STEPS, ROW...  5.6 us
    ppermute x4, waiting for transfers between devices, shift(): lax.ppermute(block, axis, pairs if forward else [(b, a) for a, b in pairs])  3.04 us
    pallas_call x1, Pallas kernels, extrapolate(): pl.pallas_call(own_kernel, out_shape=(shape(4, STEPS, ROWS, 128), shape(2...  1.47 us
  transfers between devices with their start and end apart: 5, of which 2 were waited for; matrix products, arithmetic and copies ran while one was open for 0% of the time, Pallas kernels for 12%

profile of v6, /device:TPU:1, one launch (start us, length us, event | category | flops | bytes accessed | tf_op | source)
XLA Modules:
  0.0 69.2 jit_solution(14778782194198210566)
XLA Ops:
  0.6 1.4 %edges.1 = (f32[3,64,128]{2,1,0:T(8,128)S(1)}, f32[3,64,128]{2,1,0:T(8,128)S(1)}, f32[2,2,2,64,256]{4,3,2,1,0:T(8,128)S(1)}, s32[2,2,64,256]{3,2,1,0:T(8,128)S(1)}) custom-call(f32[2,2,64,256]{3,2,1,0:T(8,128)} %source.1, f32[2,2,64,256]{3,2,1,0:T(8,128)} %receiver.1, s32[2,2,64,256]{3,2,1,0:T(8,128)} %index.1), custom_call_target="tpu_custom_call" | custom-call | tf_op jit(solution)/shard_map/edges/pallas_call | solution.py:387
  2.0 4.0 %collective-permute-start = (f32[3,64,128]{2,1,0:T(8,128)S(1)}, f32[3,64,128]{2,1,0:T(8,128)S(1)}, u32[]{:S(2)}, u32[]{:S(2)}) collective-permute-start(f32[3,64,128]{2,1,0:T(8,128)S(1)} %get-tuple-element.29), channel_id=1, source_target_pairs={{0,1},{1,2},{2,3},{4,5},{5,6},{6,7},{8,9},{9,10},{10,11},{12,13},{... | collective-permute-start | bytes 294920 | tf_op jit(solution)/shard_map/ppermute | solution.py:374
  6.0 1.3 %collective-permute-start.1 = (f32[3,64,128]{2,1,0:T(8,128)S(1)}, f32[3,64,128]{2,1,0:T(8,128)S(1)}, u32[]{:S(2)}, u32[]{:S(2)}) collective-permute-start(f32[3,64,128]{2,1,0:T(8,128)S(1)} %get-tuple-element.30), channel_id=1, source_target_pairs={{1,0},{2,1},{3,2},{5,4},{6,5},{7,6},{9,8},{10,9},{11,10},{13,12},{... | collective-permute-start | bytes 294920 | tf_op jit(solution)/shard_map/ppermute | solution.py:374
  7.3 0.0 copy-start
  7.4 1.5 %own.1 = (f32[4,5,64,128]{3,2,1,0:T(8,128)S(1)}, f32[2,5,64,128]{3,2,1,0:T(8,128)S(1)}, bf16[640,640]{1,0:T(8,128)(2,1)S(1)}) custom-call(f32[2,2,2,64,256]{4,3,2,1,0:T(8,128)S(1)} %get-tuple-element.25.waves, s32[2,2,64,256]{3,2,1,0:T(8,128)S(1)} %get-tuple-element.26.index), custom_call_target="tpu_custom_call" | custom-call | flops 2000000000 | bytes 1048576 | tf_op jit(solution)/shard_map/own/pallas_call | solution.py:403
  8.9 0.1 select_select_fusion.flags
  9.0 0.0 collective-permute-done.low
  9.0 2.4 %collective-permute-done.1.high = f32[3,64,128]{2,1,0:T(8,128)S(1)} collective-permute-done((f32[3,64,128]{2,1,0:T(8,128)S(1)}, f32[3,64,128]{2,1,0:T(8,128)S(1)}, u32[]{:S(2)}, u32[]{:S(2)}) %collective-permute-start.1) | collective-permute-done | bytes 98336 | tf_op jit(solution)/shard_map/ppermute | solution.py:374
  11.4 0.4 merge.1
  11.8 3.6 %collective-permute-start.2 = (f32[560,128]{1,0:T(8,128)S(1)}, f32[560,128]{1,0:T(8,128)S(1)}, u32[]{:S(2)}, u32[]{:S(2)}) collective-permute-start(f32[560,128]{1,0:T(8,128)S(1)} %get-tuple-element.34), channel_id=1, source_target_pairs={{0,4},{4,8},{8,12},{12,16},{16,20},{20,24},{24,28},{1,5},{5,9},{9,... | collective-permute-start | bytes 860168 | tf_op jit(solution)/shard_map/ppermute | solution.py:374
  15.4 1.3 %collective-permute-start.3 = (f32[560,128]{1,0:T(8,128)S(1)}, f32[560,128]{1,0:T(8,128)S(1)}, u32[]{:S(2)}, u32[]{:S(2)}) collective-permute-start(f32[560,128]{1,0:T(8,128)S(1)} %get-tuple-element.35), channel_id=1, source_target_pairs={{4,0},{8,4},{12,8},{16,12},{20,16},{24,20},{28,24},{5,1},{9,5},{13... | collective-permute-start | bytes 860168 | tf_op jit(solution)/shard_map/ppermute | solution.py:374
  16.7 0.0 copy-done
  16.7 5.6 %inner.1 = (f32[13,4,5,32,128]{4,3,2,1,0:T(8,128)S(1)}, f32[13,4,5,32,128]{4,3,2,1,0:T(8,128)S(1)}, f32[2,5,64,128]{3,2,1,0:T(8,128)S(1)}, f32[4,5,16,128]{3,2,1,0:T(8,128)S(1)}) custom-call(f32[8,128]{1,0:T(8,128)S(1)} %select_select_fusion.flags, f32[4,5,64,128]{3,2,1,0:T(8,128)S(1)} %get-tuple-element.32.fields, ...), custom_call_target="tpu_custom_call" | custom-call | flops 10000000000 | bytes 1048576 | tf_op jit(solution)/shard_map/inner/pallas_call | solution.py:427
  22.3 0.0 collective-permute-done.2.above
  22.3 0.6 collective-permute-done.3.below
  22.9 7.4 %rim.1 = (f32[2,4,5,24,128]{4,3,2,1,0:T(8,128)S(1)}, f32[8,16,256]{2,1,0:T(8,128)S(1)}) custom-call(f32[8,128]{1,0:T(8,128)S(1)} %select_select_fusion.flags, f32[4,5,64,128]{3,2,1,0:T(8,128)S(1)} %get-tuple-element.32.fields, f32[5,64,128]{2,1,0:T(8,128)S(1)} %get-tuple-element.33.indices0, f32[5,64,128]{2,1,0:T(8,128)S(1)} %slice_bitcast_fusion.indices1, ...), custom_call_target="tpu_custom_call" | custom-call | tf_op jit(solution)/shard_map/rim/pallas_call | solution.py:443
  30.3 13.3 %all_to_all.10 = f32[8,16,256]{2,1,0:T(8,128)S(1)} all-to-all(f32[8,16,256]{2,1,0:T(8,128)S(1)} %get-tuple-element.39), channel_id=1, replica_groups={{0,32,128,160,256,288,384,416},{64,96,192,224,320,352,448,480},{1,33,12..., dimensions={0} | all-to-all | bytes 262144 | tf_op jit(solution)/shard_map/all_to_all | solution.py:475
  43.7 14.4 %collective-permute-start.4 = (f32[16,256]{1,0:T(8,128)S(1)}, f32[16,256]{1,0:T(8,128)S(1)}, u32[]{:S(2)}, u32[]{:S(2)}) collective-permute-start(f32[16,256]{1,0:T(8,128)S(1)} %reduce_sum.9), channel_id=1, source_target_pairs={{0,64},{32,96},{64,0},{96,32},{128,192},{160,224},{192,128},{224,1... | collective-permute-start | bytes 49160 | tf_op jit(solution)/shard_map/ppermute | solution.py:476
  58.0 1.4 %finish.1 = (f32[2,2,64,256]{3,2,1,0:T(8,128)}, f32[2,2,64,256]{3,2,1,0:T(8,128)}) custom-call(f32[2,4,5,24,128]{4,3,2,1,0:T(8,128)S(1)} %get-tuple-element.40.fresh, f32[4,5,16,128]{3,2,1,0:T(8,128)S(1)} %get-tuple-element.41.centre, bf16[640,640]{1,0:T(8,128)(2,1)S(1)} %get-tuple-element.31.spread), custom_call_target="tpu_custom_call" | custom-call | flops 2000000000 | bytes 1048576 | tf_op jit(solution)/shard_map/finish/pallas_call | solution.py:460
  59.4 0.0 collective-permute-done.4
  59.4 9.1 %all_to_all.11 = f32[8,16,256]{2,1,0:T(8,128)S(1)} all-to-all(f32[8,16,256]{2,1,0:T(8,128)S(1)} %broadcast_in_dim.21), channel_id=1, replica_groups={{0,32,128,160,256,288,384,416},{64,96,192,224,320,352,448,480},{1,33,12..., dimensions={0} | all-to-all | bytes 262144 | tf_op jit(solution)/shard_map/all_to_all | solution.py:479
  68.6 0.7 copy.8
  (7 shorter events, 0.1 us)
Async XLA Ops:
  2.0 6.9 %collective-permute-start = (f32[3,64,128]{2,1,0:T(8,128)S(1)}, f32[3,64,128]{2,1,0:T(8,128)S(1)}, u32[]{:S(2)}, u32[]{:S(2)}) collective-permute-start(f32[3,64,128]{2,1,0:T(8,128)S(1)} %get-tuple-element.29), channel_id=1, source_target_pairs={{0,1},{1,2},{2,3},{4,5},{5,6},{6,7},{8,9},{9,10},{10,11},{12,13},{... | collective-permute-start | bytes 294920 | tf_op jit(solution)/shard_map/ppermute | solution.py:374
  6.0 5.4 %collective-permute-start.1 = (f32[3,64,128]{2,1,0:T(8,128)S(1)}, f32[3,64,128]{2,1,0:T(8,128)S(1)}, u32[]{:S(2)}, u32[]{:S(2)}) collective-permute-start(f32[3,64,128]{2,1,0:T(8,128)S(1)} %get-tuple-element.30), channel_id=1, source_target_pairs={{1,0},{2,1},{3,2},{5,4},{6,5},{7,6},{9,8},{10,9},{11,10},{13,12},{... | collective-permute-start | bytes 294920 | tf_op jit(solution)/shard_map/ppermute | solution.py:374
  7.3 9.3 %copy-start = (f32[2,32,13]{1,0,2:T(2,128)S(1)}, f32[2,32,13]{1,0,2:T(2,128)}, u32[]{:S(2)}) copy-start(f32[2,32,13]{1,0,2:T(2,128)} %param.7) | copy-start | bytes 9988
  11.8 10.5 %collective-permute-start.2 = (f32[560,128]{1,0:T(8,128)S(1)}, f32[560,128]{1,0:T(8,128)S(1)}, u32[]{:S(2)}, u32[]{:S(2)}) collective-permute-start(f32[560,128]{1,0:T(8,128)S(1)} %get-tuple-element.34), channel_id=1, source_target_pairs={{0,4},{4,8},{8,12},{12,16},{16,20},{20,24},{24,28},{1,5},{5,9},{9,... | collective-permute-start | bytes 860168 | tf_op jit(solution)/shard_map/ppermute | solution.py:374
  15.4 7.6 %collective-permute-start.3 = (f32[560,128]{1,0:T(8,128)S(1)}, f32[560,128]{1,0:T(8,128)S(1)}, u32[]{:S(2)}, u32[]{:S(2)}) collective-permute-start(f32[560,128]{1,0:T(8,128)S(1)} %get-tuple-element.35), channel_id=1, source_target_pairs={{4,0},{8,4},{12,8},{16,12},{20,16},{24,20},{28,24},{5,1},{9,5},{13... | collective-permute-start | bytes 860168 | tf_op jit(solution)/shard_map/ppermute | solution.py:374
  43.7 15.7 %collective-permute-start.4 = (f32[16,256]{1,0:T(8,128)S(1)}, f32[16,256]{1,0:T(8,128)S(1)}, u32[]{:S(2)}, u32[]{:S(2)}) collective-permute-start(f32[16,256]{1,0:T(8,128)S(1)} %reduce_sum.9), channel_id=1, source_target_pairs={{0,64},{32,96},{64,0},{96,32},{128,192},{160,224},{192,128},{224,1... | collective-permute-start | bytes 49160 | tf_op jit(solution)/shard_map/ppermute | solution.py:476

commit v7 on v6

--- a/solution.py
+++ b/solution.py
@@ -157,6 +157,18 @@
             terms[now + 1, plane, step, rows(origin + r), :] = new
 
 
+def in_pairs(first, last, body):
+    pairs = (last - first) // 2
+
+    def two(at, carry):
+        body(first + 2 * at, carry)
+        return body(first + 2 * at + 1, carry)
+
+    lax.fori_loop(0, pairs, two, 0)
+    for at in range(first + 2 * pairs, last):
+        body(at, 0)
+
+
 def combine(terms, table, place, rows, step, orders):
     total = [None] * 4
     for order in range(orders):
@@ -230,7 +242,7 @@
             if last - first == 1:
                 step_on(start, 0)
             else:
-                lax.fori_loop(start, start + last - first, step_on, 0)
+                in_pairs(start, start + last - first, step_on)
         for plane in range(4):
             hand_over(orders - 1, plane)
         first_row = HALF * (depth + 1)
@@ -309,7 +321,7 @@
             return carry
 
         step_on(0, 0, True)
-        lax.fori_loop(0, orders - 2, lambda past, carry: step_on(past, carry, False), 0)
+        in_pairs(0, orders - 2, lambda past, carry: step_on(past, carry, False))
 
         def gather(r, carry, depth=depth):
             for side, terms in enumerate((upper, lower)):

time: 69.5 us -> 69.5 us (level)
  no operation moved by 1% of the time
where the time goes in v7:
time: 69.5 us; the launch traced here: 69.2 us
  starting transfers between devices  24.5 us (35%)
  blocking collectives  22.4 us (32%)
  Pallas kernels  17.5 us (25%)
  waiting for transfers between devices  3.18 us (5%)
  between operations  0.79 us (1%)
    ppermute x1, starting transfers between devices, add_over_freq(): other = lax.ppermute(mine, 'freq', [(i, i ^ 2) for i in range(16)])  14.4 us
    all_to_all x1, blocking collectives, add_over_freq(): lax.all_to_all(pieces, 'freq', 0, 0, axis_index_groups=groups)  13.3 us
    ppermute x4, starting transfers between devices, shift(): lax.ppermute(block, axis, pairs if forward else [(b, a) for a, b in pairs])  10.1 us
    all_to_all x1, blocking collectives, add_over_freq(): lax.all_to_all(jnp.broadcast_to(mine[None], pieces.shape), 'freq', 0, 0,...  9.13 us
    pallas_call x1, Pallas kernels, extrapolate(): pl.pallas_call(rim_kernel, out_shape=(shape(2, 4, STEPS, HALO, 128), shap...  7.36 us
    pallas_call x1, Pallas kernels, extrapolate(): pl.pallas_call(inner_kernel, out_shape=(strip, strip, shape(2, STEPS, ROW...  5.46 us
    ppermute x4, waiting for transfers between devices, shift(): lax.ppermute(block, axis, pairs if forward else [(b, a) for a, b in pairs])  3.17 us
    pallas_call x1, Pallas kernels, extrapolate(): pl.pallas_call(own_kernel, out_shape=(shape(4, STEPS, ROWS, 128), shape(2...  1.47 us
  transfers between devices with their start and end apart: 5, of which 2 were waited for; matrix products, arithmetic and copies ran while one was open for 0% of the time, Pallas kernels for 12%

profile of v7, /device:TPU:1, one launch (start us, length us, event | category | flops | bytes accessed | tf_op | source)
XLA Modules:
  0.0 69.2 jit_solution(18050831413757738435)
XLA Ops:
  0.6 1.4 %edges.1 = (f32[3,64,128]{2,1,0:T(8,128)S(1)}, f32[3,64,128]{2,1,0:T(8,128)S(1)}, f32[2,2,2,64,256]{4,3,2,1,0:T(8,128)S(1)}, s32[2,2,64,256]{3,2,1,0:T(8,128)S(1)}) custom-call(f32[2,2,64,256]{3,2,1,0:T(8,128)} %source.1, f32[2,2,64,256]{3,2,1,0:T(8,128)} %receiver.1, s32[2,2,64,256]{3,2,1,0:T(8,128)} %index.1), custom_call_target="tpu_custom_call" | custom-call | tf_op jit(solution)/shard_map/edges/pallas_call | solution.py:399
  2.0 4.0 %collective-permute-start = (f32[3,64,128]{2,1,0:T(8,128)S(1)}, f32[3,64,128]{2,1,0:T(8,128)S(1)}, u32[]{:S(2)}, u32[]{:S(2)}) collective-permute-start(f32[3,64,128]{2,1,0:T(8,128)S(1)} %get-tuple-element.29), channel_id=1, source_target_pairs={{0,1},{1,2},{2,3},{4,5},{5,6},{6,7},{8,9},{9,10},{10,11},{12,13},{... | collective-permute-start | bytes 294920 | tf_op jit(solution)/shard_map/ppermute | solution.py:386
  6.0 1.3 %collective-permute-start.1 = (f32[3,64,128]{2,1,0:T(8,128)S(1)}, f32[3,64,128]{2,1,0:T(8,128)S(1)}, u32[]{:S(2)}, u32[]{:S(2)}) collective-permute-start(f32[3,64,128]{2,1,0:T(8,128)S(1)} %get-tuple-element.30), channel_id=1, source_target_pairs={{1,0},{2,1},{3,2},{5,4},{6,5},{7,6},{9,8},{10,9},{11,10},{13,12},{... | collective-permute-start | bytes 294920 | tf_op jit(solution)/shard_map/ppermute | solution.py:386
  7.3 0.0 copy-start
  7.4 1.5 %own.1 = (f32[4,5,64,128]{3,2,1,0:T(8,128)S(1)}, f32[2,5,64,128]{3,2,1,0:T(8,128)S(1)}, bf16[640,640]{1,0:T(8,128)(2,1)S(1)}) custom-call(f32[2,2,2,64,256]{4,3,2,1,0:T(8,128)S(1)} %get-tuple-element.25.waves, s32[2,2,64,256]{3,2,1,0:T(8,128)S(1)} %get-tuple-element.26.index), custom_call_target="tpu_custom_call" | custom-call | flops 2000000000 | bytes 1048576 | tf_op jit(solution)/shard_map/own/pallas_call | solution.py:415
  8.9 0.1 select_select_fusion.flags
  9.0 0.0 collective-permute-done.low
  9.0 2.4 %collective-permute-done.1.high = f32[3,64,128]{2,1,0:T(8,128)S(1)} collective-permute-done((f32[3,64,128]{2,1,0:T(8,128)S(1)}, f32[3,64,128]{2,1,0:T(8,128)S(1)}, u32[]{:S(2)}, u32[]{:S(2)}) %collective-permute-start.1) | collective-permute-done | bytes 98336 | tf_op jit(solution)/shard_map/ppermute | solution.py:386
  11.4 0.4 merge.1
  11.8 3.6 %collective-permute-start.2 = (f32[560,128]{1,0:T(8,128)S(1)}, f32[560,128]{1,0:T(8,128)S(1)}, u32[]{:S(2)}, u32[]{:S(2)}) collective-permute-start(f32[560,128]{1,0:T(8,128)S(1)} %get-tuple-element.34), channel_id=1, source_target_pairs={{0,4},{4,8},{8,12},{12,16},{16,20},{20,24},{24,28},{1,5},{5,9},{9,... | collective-permute-start | bytes 860168 | tf_op jit(solution)/shard_map/ppermute | solution.py:386
  15.4 1.3 %collective-permute-start.3 = (f32[560,128]{1,0:T(8,128)S(1)}, f32[560,128]{1,0:T(8,128)S(1)}, u32[]{:S(2)}, u32[]{:S(2)}) collective-permute-start(f32[560,128]{1,0:T(8,128)S(1)} %get-tuple-element.35), channel_id=1, source_target_pairs={{4,0},{8,4},{12,8},{16,12},{20,16},{24,20},{28,24},{5,1},{9,5},{13... | collective-permute-start | bytes 860168 | tf_op jit(solution)/shard_map/ppermute | solution.py:386
  16.7 0.0 copy-done
  16.7 5.5 %inner.1 = (f32[13,4,5,32,128]{4,3,2,1,0:T(8,128)S(1)}, f32[13,4,5,32,128]{4,3,2,1,0:T(8,128)S(1)}, f32[2,5,64,128]{3,2,1,0:T(8,128)S(1)}, f32[4,5,16,128]{3,2,1,0:T(8,128)S(1)}) custom-call(f32[8,128]{1,0:T(8,128)S(1)} %select_select_fusion.flags, f32[4,5,64,128]{3,2,1,0:T(8,128)S(1)} %get-tuple-element.32.fields, ...), custom_call_target="tpu_custom_call" | custom-call | flops 10000000000 | bytes 1048576 | tf_op jit(solution)/shard_map/inner/pallas_call | solution.py:439
  22.1 0.0 collective-permute-done.2.above
  22.2 0.8 %collective-permute-done.3.below = f32[560,128]{1,0:T(8,128)S(1)} collective-permute-done((f32[560,128]{1,0:T(8,128)S(1)}, f32[560,128]{1,0:T(8,128)S(1)}, u32[]{:S(2)}, u32[]{:S(2)}) %collective-permute-start.3) | collective-permute-done | bytes 286752 | tf_op jit(solution)/shard_map/ppermute | solution.py:386
  22.9 7.4 %rim.1 = (f32[2,4,5,24,128]{4,3,2,1,0:T(8,128)S(1)}, f32[8,16,256]{2,1,0:T(8,128)S(1)}) custom-call(f32[8,128]{1,0:T(8,128)S(1)} %select_select_fusion.flags, f32[4,5,64,128]{3,2,1,0:T(8,128)S(1)} %get-tuple-element.32.fields, f32[5,64,128]{2,1,0:T(8,128)S(1)} %get-tuple-element.33.indices0, f32[5,64,128]{2,1,0:T(8,128)S(1)} %slice_bitcast_fusion.indices1, ...), custom_call_target="tpu_custom_call" | custom-call | tf_op jit(solution)/shard_map/rim/pallas_call | solution.py:455
  30.3 13.3 %all_to_all.10 = f32[8,16,256]{2,1,0:T(8,128)S(1)} all-to-all(f32[8,16,256]{2,1,0:T(8,128)S(1)} %get-tuple-element.39), channel_id=1, replica_groups={{0,32,128,160,256,288,384,416},{64,96,192,224,320,352,448,480},{1,33,12..., dimensions={0} | all-to-all | bytes 262144 | tf_op jit(solution)/shard_map/all_to_all | solution.py:487
  43.6 14.4 %collective-permute-start.4 = (f32[16,256]{1,0:T(8,128)S(1)}, f32[16,256]{1,0:T(8,128)S(1)}, u32[]{:S(2)}, u32[]{:S(2)}) collective-permute-start(f32[16,256]{1,0:T(8,128)S(1)} %reduce_sum.9), channel_id=1, source_target_pairs={{0,64},{32,96},{64,0},{96,32},{128,192},{160,224},{192,128},{224,1... | collective-permute-start | bytes 49160 | tf_op jit(solution)/shard_map/ppermute | solution.py:488
  58.0 1.4 %finish.1 = (f32[2,2,64,256]{3,2,1,0:T(8,128)}, f32[2,2,64,256]{3,2,1,0:T(8,128)}) custom-call(f32[2,4,5,24,128]{4,3,2,1,0:T(8,128)S(1)} %get-tuple-element.40.fresh, f32[4,5,16,128]{3,2,1,0:T(8,128)S(1)} %get-tuple-element.41.centre, bf16[640,640]{1,0:T(8,128)(2,1)S(1)} %get-tuple-element.31.spread), custom_call_target="tpu_custom_call" | custom-call | flops 2000000000 | bytes 1048576 | tf_op jit(solution)/shard_map/finish/pallas_call | solution.py:472
  59.3 0.0 collective-permute-done.4
  59.4 9.1 %all_to_all.11 = f32[8,16,256]{2,1,0:T(8,128)S(1)} all-to-all(f32[8,16,256]{2,1,0:T(8,128)S(1)} %broadcast_in_dim.21), channel_id=1, replica_groups={{0,32,128,160,256,288,384,416},{64,96,192,224,320,352,448,480},{1,33,12..., dimensions={0} | all-to-all | bytes 262144 | tf_op jit(solution)/shard_map/all_to_all | solution.py:491
  68.5 0.7 copy.8
  (7 shorter events, 0.1 us)
Async XLA Ops:
  2.0 6.9 %collective-permute-start = (f32[3,64,128]{2,1,0:T(8,128)S(1)}, f32[3,64,128]{2,1,0:T(8,128)S(1)}, u32[]{:S(2)}, u32[]{:S(2)}) collective-permute-start(f32[3,64,128]{2,1,0:T(8,128)S(1)} %get-tuple-element.29), channel_id=1, source_target_pairs={{0,1},{1,2},{2,3},{4,5},{5,6},{6,7},{8,9},{9,10},{10,11},{12,13},{... | collective-permute-start | bytes 294920 | tf_op jit(solution)/shard_map/ppermute | solution.py:386
  6.0 5.4 %collective-permute-start.1 = (f32[3,64,128]{2,1,0:T(8,128)S(1)}, f32[3,64,128]{2,1,0:T(8,128)S(1)}, u32[]{:S(2)}, u32[]{:S(2)}) collective-permute-start(f32[3,64,128]{2,1,0:T(8,128)S(1)} %get-tuple-element.30), channel_id=1, source_target_pairs={{1,0},{2,1},{3,2},{5,4},{6,5},{7,6},{9,8},{10,9},{11,10},{13,12},{... | collective-permute-start | bytes 294920 | tf_op jit(solution)/shard_map/ppermute | solution.py:386
  7.3 9.3 %copy-start = (f32[2,32,13]{1,0,2:T(2,128)S(1)}, f32[2,32,13]{1,0,2:T(2,128)}, u32[]{:S(2)}) copy-start(f32[2,32,13]{1,0,2:T(2,128)} %param.7) | copy-start | bytes 9988
  11.8 10.3 %collective-permute-start.2 = (f32[560,128]{1,0:T(8,128)S(1)}, f32[560,128]{1,0:T(8,128)S(1)}, u32[]{:S(2)}, u32[]{:S(2)}) collective-permute-start(f32[560,128]{1,0:T(8,128)S(1)} %get-tuple-element.34), channel_id=1, source_target_pairs={{0,4},{4,8},{8,12},{12,16},{16,20},{20,24},{24,28},{1,5},{5,9},{9,... | collective-permute-start | bytes 860168 | tf_op jit(solution)/shard_map/ppermute | solution.py:386
  15.4 7.6 %collective-permute-start.3 = (f32[560,128]{1,0:T(8,128)S(1)}, f32[560,128]{1,0:T(8,128)S(1)}, u32[]{:S(2)}, u32[]{:S(2)}) collective-permute-start(f32[560,128]{1,0:T(8,128)S(1)} %get-tuple-element.35), channel_id=1, source_target_pairs={{4,0},{8,4},{12,8},{16,12},{20,16},{24,20},{28,24},{5,1},{9,5},{13... | collective-permute-start | bytes 860168 | tf_op jit(solution)/shard_map/ppermute | solution.py:386
  43.6 15.7 %collective-permute-start.4 = (f32[16,256]{1,0:T(8,128)S(1)}, f32[16,256]{1,0:T(8,128)S(1)}, u32[]{:S(2)}, u32[]{:S(2)}) collective-permute-start(f32[16,256]{1,0:T(8,128)S(1)} %reduce_sum.9), channel_id=1, source_target_pairs={{0,64},{32,96},{64,0},{96,32},{128,192},{160,224},{192,128},{224,1... | collective-permute-start | bytes 49160 | tf_op jit(solution)/shard_map/ppermute | solution.py:488
